TPU v7x, 32 devices: a whole 2x2x4 slice. The times are simulated.
32 devices in a mesh: rows: 8 (over z, y), aux: 4 (over x, core).
Axes of the slice: x: 2, y: 2, z: 4, core: 2. Of those that a mesh axis runs over, the one named last changes fastest.
Arguments:
- density: bfloat16 [128, 8, 4096], P('aux', None, 'rows'), may hold values from -64 to 64, as said below
- vir_coeffs: bfloat16 [4096, 4096], P('rows'), may hold values from -0.09375 to 0.09375
- occ_coeffs: bfloat16 [8, 4096], P(None, 'rows'), may hold values from -2 to 2
- shell_len: int32 [8, 64], replicated, may hold values from 1 to 16, 512 in all within a row
- mu_shell: int32 [2048], P('rows'), may hold values from 0 to 511
- nu_shell: int32 [2048], P('rows'), may hold values from 0 to 63
- owner: int32 [2048, 1], P('rows'), may hold values from 0 to 7; in each aligned block of 256 rows (0 to 255, 256 to 511, ...) at most 64 rows name the same one
Outputs:
- pair_blocks: bfloat16 [4096, 128, 256], P('rows', 'aux')
- pair_scale: float32 [4096], P('rows')
Inputs may be any that keep to these rules, and one draw needn't show every extreme that they name: Each index of rows names at most 64 of its 256 pairs for one owner, and exactly 64 for some owner. `shell_len`: shell lengths of each slab sum to 512; the longest is 16. `density`: Real-valued, of varying scale over auxiliary functions and orbital pairs.
All inputs are finite; a program needn't handle non-finite values.
Results may differ from a plain program's by a relative error of at most 0.0049.
Values may be sent and summed in bfloat16 or wider, within the bound.
No kernel may reach another device: no remote copies, remote signals or barrier semaphores. Data moves between devices by JAX's collectives and lax.ppermute only.
A program may use at most 192 MiB of HBM per device.

v0:
```python
import jax
import jax.numpy as jnp
from jax import lax
from jax.sharding import PartitionSpec as P

NAUX = 128
PAD = 16


def lookup(table, index):
    hits = index[:, None] == jnp.arange(table.shape[0], dtype=jnp.int32)[None, :]
    return jnp.sum(jnp.where(hits, table[None, :], 0), axis=1)


def per_device(density, vir_coeffs, occ_coeffs, shell_len, mu_shell, nu_shell, owner):
    row_count = lax.axis_size("rows")
    position = lax.axis_index("rows")
    slab = vir_coeffs.shape[0]
    local_aux = density.shape[0]
    occupied = density.shape[1]
    pair_count = mu_shell.shape[0]
    capacity = 2 * pair_count // row_count
    slot_total = row_count * capacity
    half = jnp.einsum(
        "pia,na->pin",
        lax.all_gather(density, "rows", axis=2, tiled=True),
        vir_coeffs,
        preferred_element_type=jnp.float32,
    ).astype(jnp.bfloat16)
    occ_full = lax.all_gather(occ_coeffs, "rows", axis=1, tiled=True)
    starts = jnp.cumsum(shell_len, axis=1) - shell_len
    flat_start = (starts + jnp.arange(row_count, dtype=jnp.int32)[:, None] * slab).reshape(-1)
    flat_len = shell_len.reshape(-1)
    mu_start = lookup(flat_start, mu_shell)
    mu_length = lookup(flat_len, mu_shell)
    own_start = lax.dynamic_index_in_dim(starts, position, 0, keepdims=False)
    own_length = lax.dynamic_index_in_dim(shell_len, position, 0, keepdims=False)
    nu_start = lookup(own_start, nu_shell)
    nu_length = lookup(own_length, nu_shell)
    target = owner[:, 0]
    onehot = (target[:, None] == jnp.arange(row_count, dtype=jnp.int32)[None, :]).astype(jnp.int32)
    earlier = jnp.cumsum(onehot, axis=0) - onehot
    rank = jnp.sum(earlier * onehot, axis=1)
    send_row = target * capacity + rank
    placed = send_row[None, :] == jnp.arange(slot_total, dtype=jnp.int32)[:, None]
    live = jnp.any(placed, axis=1)
    slot_mu_start = jnp.sum(jnp.where(placed, mu_start[None, :], 0), axis=1)
    slot_mu_length = jnp.sum(jnp.where(placed, mu_length[None, :], 0), axis=1)
    slot_nu_start = jnp.sum(jnp.where(placed, nu_start[None, :], 0), axis=1)
    slot_nu_length = jnp.sum(jnp.where(placed, nu_length[None, :], 0), axis=1)
    offsets = jnp.arange(PAD, dtype=jnp.int32)
    nu_column = (slot_nu_start[:, None] + offsets[None, :]).reshape(-1)
    nu_valid = ((offsets[None, :] < slot_nu_length[:, None]) & live[:, None]).reshape(-1)
    selector = (
        (nu_column[:, None] == jnp.arange(slab, dtype=jnp.int32)[None, :]) & nu_valid[:, None]
    ).astype(jnp.bfloat16)
    half_slots = jnp.einsum(
        "pin,xn->pix", half, selector, preferred_element_type=jnp.float32
    ).astype(jnp.bfloat16)
    mu_column = (slot_mu_start[:, None] + offsets[None, :]).reshape(-1)
    mu_valid = ((offsets[None, :] < slot_mu_length[:, None]) & live[:, None]).reshape(-1)
    occ_pad = jnp.pad(occ_full, ((0, 0), (0, PAD)))
    coeff_slots = jnp.where(
        mu_valid[None, :], jnp.take(occ_pad, mu_column, axis=1), jnp.zeros((), jnp.bfloat16)
    )
    blocks = jnp.einsum(
        "ism,pisn->spmn",
        coeff_slots.reshape(occupied, slot_total, PAD),
        half_slots.reshape(local_aux, occupied, slot_total, PAD),
        preferred_element_type=jnp.float32,
    )
    outgoing = blocks.astype(jnp.bfloat16).reshape(slot_total, local_aux, PAD * PAD)
    received = lax.all_to_all(outgoing, "rows", split_axis=0, concat_axis=0, tiled=True)
    partial_squares = jnp.sum(jnp.square(received.astype(jnp.float32)), axis=(1, 2))
    total = lax.psum(partial_squares, "aux")
    pair_scale = jnp.sqrt(total / (NAUX * PAD * PAD) + 1e-06)
    return (received, pair_scale)


def solution(mesh):
    return jax.shard_map(
        per_device,
        mesh=mesh,
        in_specs=(
            P("aux", None, "rows"),
            P("rows", None),
            P(None, "rows"),
            P(),
            P("rows"),
            P("rows"),
            P("rows", None),
        ),
        out_specs=(P("rows", "aux", None), P("rows")),
        check_vma=False,
    )
```

profile of v0, /device:TPU:0, one launch (start us, length us, event | category | flops | bytes accessed | tf_op | source)
XLA Modules:
  0.0 400.3 jit_solution(11285405338002230441)
XLA Ops:
  7.2 0.0 all-gather.2.cloned.1.call-start
  7.2 0.7 all-gather.2.cloned.1.call-update
  7.9 0.8 broadcast_in_dim.133
  8.7 0.9 reduce_window_sum.28
  9.6 0.8 broadcast_add_fusion
  10.3 0.1 broadcast_in_dim.138
  10.4 0.7 fusion.28
  11.1 0.6 reduce-window.6
  11.7 0.2 slice_reduce_fusion
  11.9 0.7 dynamic-slice_bitcast_fusion
  12.6 0.8 select_reduce_fusion.6
  13.4 0.8 fusion.27
  14.2 1.0 select_reduce_fusion.3
  15.1 0.7 multiply_add_fusion
  15.8 0.4 select_reduce_fusion.2
  16.2 0.2 copy.31
  16.4 0.2 fusion.23
  16.6 0.3 fusion.25
  16.9 0.1 and.44
  17.0 0.9 copy.32
  17.9 0.1 copy.33
  18.0 0.2 add.118
  18.2 0.1 iota_add_fusion
  18.3 0.1 add.108
  18.5 35.7 %all_gather.7 = bf16[8,4096]{0,1:T(8,128)(2,1)S(1)} all-gather(bf16[8,512]{0,1:T(8,128)(2,1)S(1)} %copy.32), channel_id=1, replica_groups=mesh['rows'=8,'aux'=4] {'rows'}, dimensions={1}, use_global_device_ids=true | all-gather | bytes 73728 | tf_op jit(solution)/shard_map/all_gather | solution.py:30
  54.1 0.2 pad.4
  54.4 24.0 %gather_fusion = bf16[8192,8]{1,0:T(8,128)(2,1)S(1)} fusion(bf16[8,4112]{0,1:T(8,128)(2,1)S(1)} %pad.4, s32[8192]{0:T(1024)S(1)} %broadcast_clamp_fusion), kind=kCustom, calls=%fused_computation | custom fusion | bytes 294912 | tf_op jit(solution)/shard_map/jit(_take)/gather | solution.py:64
  78.5 1.0 copy.34
  79.5 0.0 all-gather.2.cloned.1.call-done
  79.5 4.1 %fusion.11.clone.5 = bf16[32,8,512]{2,1,0:T(8,128)(2,1)S(1)} fusion(bf16[32,8,4096]{2,1,0:T(8,128)(2,1)} %all-gather.2.cloned.1.call-done, bf16[512,4096]{1,0:T(8,128)(2,1)} %param.8), kind=kOutput, calls=%fused_computation.12.clone.clone.clone.2 | convolution fusion | flops 1073872896 | bytes 6553600 | tf_op jit(solution)/shard_map/pia,na->pin/dot_general | solution.py:24
  83.6 6.9 %fusion.4 = bf16[32,8,8192]{2,1,0:T(8,128)(2,1)} fusion(s32[8192]{0:T(1024)S(1)} %add.108, pred[8192]{0:T(1024)(128)(4,1)S(1)} %and.44, bf16[32,8,512]{2,1,0:T(8,128)(2,1)S(1)} %fusion.11.clone.5), kind=kOutput, calls=%fused_computation.7 | convolution fusion | flops 2157969408 | bytes 4497408 | tf_op jit(solution)/shard_map/pin,xn->pix/dot_general | solution.py:57
  90.6 17.7 %copy.39 = bf16[32,8,8192]{0,1,2:T(8,128)(2,1)} copy(bf16[32,8,8192]{2,1,0:T(8,128)(2,1)} %fusion.4) | data formatting | bytes 8388608 | tf_op jit(solution)/shard_map/reshape | solution.py:69
  108.2 19.8 %convert_bitcast_fusion = bf16[512,32,16,16]{1,2,3,0:T(8,128)(2,1)} fusion(bf16[32,8,512,16]{0,1,3,2:T(8,128)(2,1)} %bitcast.54, bf16[8,512,16]{2,0,1:T(8,128)(2,1)S(1)} %copy.34, pred[512,16]{1,0:T(8,128)(4,1)S(1)} %copy.31, pred[512,16]{1,0:T(8,128)(4,1)S(1)} %get-tuple-element.14), kind=kOutput, calls=%fused_computation.1 | convolution fusion | flops 71434240 | bytes 12730368 | tf_op jit(solution)/shard_map/ism,pisn->spmn/dot_general | solution.py:66
  128.0 48.5 %copy.36 = bf16[512,32,16,16]{0,3,2,1:T(8,128)(2,1)} copy(bf16[512,32,16,16]{1,2,3,0:T(8,128)(2,1)} %convert_bitcast_fusion) | data formatting | bytes 16777216 | tf_op jit(solution)/shard_map/convert_element_type | solution.py:72
  176.5 14.7 %copy.37 = bf16[512,32,256]{2,1,0:T(8,128)(2,1)} copy(bf16[512,32,256]{0,2,1:T(8,128)(2,1)} %bitcast.55) | data formatting | bytes 16777216 | tf_op jit(solution)/shard_map/reshape | solution.py:72
  191.2 182.8 %all_to_all.5 = bf16[512,32,256]{2,1,0:T(8,128)(2,1)S(1)} all-to-all(bf16[512,32,256]{2,1,0:T(8,128)(2,1)} %copy.37), channel_id=1, replica_groups=mesh['rows'=8,'aux'=4] {'rows'}, dimensions={0} | all-to-all | bytes 16777216 | tf_op jit(solution)/shard_map/all_to_all | solution.py:73
  374.0 0.0 copy-start
  374.0 3.2 copy-done
  377.2 2.2 multiply_reduce_fusion
  379.4 5.7 %psum.7 = f32[512]{0:T(512)S(1)} all-reduce(f32[512]{0:T(512)S(1)} %multiply_reduce_fusion), channel_id=1, replica_groups=mesh['rows'=8,'aux'=4] {'aux'}, use_global_device_ids=true, to_apply=%region_14.15 | all-reduce | flops 512 | bytes 4096 | tf_op jit(solution)/shard_map/psum | solution.py:75
  385.1 0.6 add_sqrt_fusion
  385.7 7.8 %copy.41 = bf16[512,32,256]{2,1,0:T(8,128)(2,1)} copy(bf16[512,32,256]{2,1,0:T(8,128)(2,1)} %copy-done) | data formatting | bytes 16777216
  (7 shorter events, 0.1 us)
Async XLA Ops:
  7.2 72.3 %all-gather.2.cloned.1.call-start = ((), (), s32[]{:S(2)}) async-start(), calls=%async_computation.1 | async-start | bytes 2359296 | tf_op jit(solution)/shard_map/all_gather | solution.py:26
  374.0 3.2 copy-start
Sparse Core Ops, SparseCore 0:
  10.0 60.8 all-gather.1
where the time goes:
time: 402 us; the launch traced here: 400 us
  blocking collectives  224 us (56%)
  local copies, waits for them, and re-layouts  120 us (30%)
  matrix products  30.8 us (8%)
  between operations  14.2 us (4%)
  other arithmetic  9.99 us (2%)
    all_to_all x1, blocking collectives, per_device(): lax.all_to_all(outgoing, 'rows', split_axis=0, concat_axis=0, tiled=True)  183 us
    convert_element_type x1, local copies, waits for them, and re-layouts, per_device(): blocks.astype(jnp.bfloat16).reshape(slot_total, local_aux, PAD * PAD)  48.5 us
    all_gather x1, blocking collectives, per_device(): occ_full = lax.all_gather(occ_coeffs, 'rows', axis=1, tiled=True)  35.7 us
    gather x2, local copies, waits for them, and re-layouts, per_device(): jnp.take(occ_pad, mu_column, axis=1)  25.1 us
    dot_general x1, matrix products, per_device(): jnp.einsum('ism,pisn->spmn', coeff_slots.reshape(occupied, slot_total, PA...  19.8 us
    reshape x1, local copies, waits for them, and re-layouts, per_device(): half_slots.reshape(local_aux, occupied, slot_total, PAD)  17.7 us
    reshape x1, local copies, waits for them, and re-layouts, per_device(): blocks.astype(jnp.bfloat16).reshape(slot_total, local_aux, PAD * PAD)  14.7 us
    unnamed x4, local copies, waits for them, and re-layouts  11.8 us
  transfers between devices with their start and end apart: 1, of which 0 were waited for; matrix products, arithmetic and copies ran while one was open for 9% of the time, Pallas kernels for 0%

commit v1 on v0

v1 whole, which is shorter than its diff:
```python
import functools

import jax
import jax.numpy as jnp
from jax import lax
from jax.experimental import pallas as pl
from jax.experimental.pallas import tpu as pltpu
from jax.sharding import PartitionSpec as P

NAUX = 128
PAD = 16
LANES = 128
DIGIT = 128
CODE = 32
GROUP = 16
MIB = 1 << 20
VMEM = pl.BlockSpec(memory_space=pltpu.VMEM)
HBM = pl.BlockSpec(memory_space=pltpu.HBM)


def swap(x, k, count, axis="rows"):
    return lax.ppermute(x, axis, [(i, i ^ k) for i in range(count)])


def after(x, *earlier):
    return lax.optimization_barrier((x, *earlier))[0]


def gather(x, count, first, second):
    parts = {0: x}
    for k in (4, 2):
        if k < count:
            parts[k] = swap(x, k, count)
    parts[1] = swap(x, 1, count)
    late = after(x, parts[1])
    for k in range(6, count, 2):
        parts[k] = swap(late, k, count)
    parts[3] = swap(parts[2], 1, count)
    parts[5] = swap(after(parts[4], first(parts)), 1, count)
    wait = second(parts)
    for k in range(6, count, 2):
        parts[k + 1] = swap(after(parts[k], wait) if wait is not None else parts[k], 1, count)
    return [parts[k] for k in range(count)]


def dot(a, b):
    return jnp.dot(a, b, preferred_element_type=jnp.float32)


def dot_t(a, b):
    return lax.dot_general(a, b, (((1,), (1,)), ((), ())), preferred_element_type=jnp.float32)


def whole(body, out_shape, args, scratch=(), scalars=0, specs=None, cost=None):
    outs = out_shape if isinstance(out_shape, tuple) else (out_shape,)
    return pl.pallas_call(
        body,
        out_shape=out_shape,
        grid_spec=pltpu.PrefetchScalarGridSpec(
            num_scalar_prefetch=scalars,
            grid=(),
            in_specs=specs or [VMEM] * (len(args) - scalars),
            out_specs=tuple(VMEM for _ in outs) if isinstance(out_shape, tuple) else VMEM,
            scratch_shapes=list(scratch),
        ),
        compiler_params=pltpu.CompilerParams(vmem_limit_bytes=44 * MIB),
        cost_estimate=pl.CostEstimate(flops=0, transcendentals=0, bytes_accessed=cost) if cost else None,
    )(*args)


def pack_kernel(density_ref, occ_ref, mu_ref, nu_ref, owner_ref, out_ref, small_ref, sems):
    aux, occupied, width = density_ref.shape
    pairs = mu_ref.shape[1]
    copies = [
        pltpu.make_async_copy(density_ref, out_ref.at[pl.ds(0, aux)], sems.at[0]),
        pltpu.make_async_copy(occ_ref, out_ref.at[aux], sems.at[1]),
    ]
    for n, ref in enumerate((mu_ref, nu_ref, owner_ref)):
        copies.append(pltpu.make_async_copy(ref, small_ref.at[n], sems.at[2 + n]))
    for copy in copies:
        copy.start()
    for copy in copies[2:]:
        copy.wait()
    mu = small_ref[0]
    digits = [mu // DIGIT, mu % DIGIT, small_ref[1], small_ref[2]]
    per = width // pairs
    rows = [jnp.concatenate(digits[n : n + per], axis=1) for n in range(0, 4, per)]
    rows.append(jnp.zeros((occupied - len(rows), width), jnp.int32))
    out_ref[aux + 1] = jnp.concatenate(rows, axis=0).astype(jnp.float32).astype(jnp.bfloat16)
    for copy in copies[:2]:
        copy.wait()


def part_kernel(ks, resumed, ahead, aux, where_ref, vir_ref, *refs):
    refs = list(refs)
    blocks = [refs.pop(0) for _ in ks]
    before_ref = refs.pop(0) if resumed else None
    total_ref, token_ref = refs.pop(0), refs.pop(0)
    ahead_ref = refs.pop(0) if ahead is not None else None
    token_ref[...] = jnp.zeros(token_ref.shape, jnp.float32)
    columns_ref, sems = refs
    _, occupied, width = blocks[0].shape

    def fetch(k, target, n):
        start = pl.multiple_of((where_ref[0] ^ k) * width, width)
        return pltpu.make_async_copy(vir_ref.at[:, pl.ds(start, width)], target, sems.at[n])

    copies = [fetch(k, columns_ref.at[n], n) for n, k in enumerate(ks)]
    if ahead is not None:
        copies.append(fetch(ahead, ahead_ref, len(ks)))
    for copy in copies:
        copy.start()
    total = None if before_ref is None else before_ref[...]
    for n in range(len(ks)):
        copies[n].wait()
        term = dot_t(blocks[n][:aux].reshape(aux * occupied, width), columns_ref[n])
        total = term if total is None else total + term
    total_ref[...] = total
    if ahead is not None:
        copies[-1].wait()


def add_part(position, vir, parts, ks, before, ahead, aux):
    slab = vir.shape[0]
    _, occupied, width = parts[0].shape
    out = [jax.ShapeDtypeStruct(shape, jnp.float32) for shape in ((aux * occupied, slab), (8, LANES))]
    if ahead is not None:
        out.append(jax.ShapeDtypeStruct((slab, width), vir.dtype))
    args = [position, vir] + [parts[k] for k in ks] + ([] if before is None else [before])
    return whole(
        functools.partial(part_kernel, ks, before is not None, ahead, aux),
        tuple(out),
        args,
        scratch=[
            pltpu.VMEM((len(ks), slab, width), vir.dtype),
            pltpu.SemaphoreType.DMA((len(ks) + 1,)),
        ],
        scalars=1,
        specs=[HBM] + [VMEM] * (len(args) - 2),
        cost=len(ks) * 2 * MIB,
    )


def half_kernel(aux, before_ref, part_ref, column_ref, spread_ref, out_ref, total_ref):
    _, occupied, width = part_ref.shape
    tiles = total_ref.shape[0]
    total = before_ref[...] + dot_t(part_ref[:aux].reshape(aux * occupied, width), column_ref[...])
    for t in range(tiles):
        total_ref[t] = total[:, t * LANES : (t + 1) * LANES]
    columns = []
    for i in range(occupied):
        h = [total_ref[t, pl.ds(i, aux, stride=occupied), :].astype(jnp.bfloat16) for t in range(tiles)]
        columns.append(jnp.concatenate(h, axis=0))
    mixed = dot(jnp.concatenate(columns, axis=1), spread_ref[...]).astype(jnp.bfloat16)
    wide = occupied * LANES
    for t in range(tiles):
        out_ref[:, t * wide : (t + 1) * wide] = mixed[t * aux : (t + 1) * aux]


def make_half(position, packed, vir, spread, aux):
    count = lax.axis_size("rows")
    slab = vir.shape[0]
    occupied = packed.shape[1]
    order = [0, 1, 2, 4] + list(range(6, count, 2)) + list(range(3, count, 2))
    early, middle, last = order[:4], order[4:-1], order[-1]
    totals = []

    def start(parts):
        total, token = add_part(position, vir, parts, early, None, None, aux)
        totals.append(total)
        return token

    parts = gather(packed, count, start, lambda parts: None)
    total, _, column = add_part(position, vir, parts, middle, totals[0], last, aux)
    half = whole(
        functools.partial(half_kernel, aux),
        jax.ShapeDtypeStruct((aux, slab * occupied), jnp.bfloat16),
        [total, parts[last], column, spread],
        scratch=[pltpu.VMEM((slab // LANES, aux * occupied, LANES), jnp.float32)],
        cost=4 * MIB,
    )
    return half, parts


def table_kernel(count, pairs, capacity, shells, slab, where_ref, *refs):
    parts, (shell_ref, repeat_ref, meta_ref, table_ref, digit_ref) = refs[:count], refs[count:]
    occupied, width = parts[0].shape[1:]
    tiles = width // LANES
    for k in range(count):
        first = (where_ref[0] ^ k) * (tiles * PAD)
        occ = jnp.concatenate([parts[k][0, :, t * LANES : (t + 1) * LANES] for t in range(tiles)], axis=0)
        wide = dot(occ, repeat_ref[...])
        for t in range(tiles):
            for q in range(PAD):
                table_ref[first + t * PAD + q] = wide[
                    t * occupied : (t + 1) * occupied, q * LANES : (q + 1) * LANES
                ]
        digit_ref[k] = parts[k][1].astype(jnp.float32)
    last = count * tiles * PAD
    table_ref[last] = jnp.zeros((occupied, LANES), jnp.float32)
    table_ref[last + 1] = jnp.zeros((occupied, LANES), jnp.float32)
    meta_ref[2 * count :, :] = jnp.full((meta_ref.shape[0] - 2 * count, LANES), where_ref[0], jnp.int32)

    per = width // pairs
    total = shell_ref.shape[1]
    f32, bf16 = jnp.float32, jnp.bfloat16
    before = (
        lax.broadcasted_iota(jnp.int32, (pairs, pairs), 0) < lax.broadcasted_iota(jnp.int32, (pairs, pairs), 1)
    ).astype(f32).astype(bf16)
    number = lax.broadcasted_iota(jnp.int32, (total, pairs), 0).astype(f32)
    slot = lax.broadcasted_iota(jnp.int32, (LANES, pairs), 0).astype(f32)
    place = where_ref[0].astype(f32)

    def body(k, carry):
        source = (where_ref[0] ^ k).astype(f32)
        rows = digit_ref[k]
        d = [rows[n // per : n // per + 1, n % per * pairs : (n % per + 1) * pairs] for n in range(4)]
        mu = d[0] * DIGIT + d[1]
        nu = d[2] + source * shells
        mine = jnp.where(d[3] == place, 1.0, 0.0)
        rank = dot(jnp.broadcast_to(mine, (8, pairs)).astype(bf16), before)[:1]
        rank = jnp.where(mine > 0, rank, -1.0)
        found = []
        for wanted in (mu, nu):
            hits = jnp.where(number == wanted, 1.0, 0.0).astype(bf16)
            found.append(dot(shell_ref[...], hits).astype(bf16))
        placed = [
            jnp.where((slot == rank + shift) & (rank >= 0), 1.0, 0.0).astype(bf16) for shift in (0, capacity)
        ]
        mixed = dot_t(found[0], placed[0]) + dot_t(found[1], placed[1])
        code = ((mixed[0:1] * DIGIT + mixed[1:2]) * CODE + mixed[2:3]).astype(jnp.int32)
        meta_ref[pl.ds(k, 1), :] = code
        live = jnp.sum(mine, axis=1, keepdims=True).astype(jnp.int32)
        meta_ref[pl.ds(count + k, 1), :] = jnp.broadcast_to(live, (1, LANES))
        return carry

    lax.fori_loop(0, count, body, 0)


def make_tables(position, parts, shell_table, repeat, pairs, capacity, shells, slab, aux):
    count = len(parts)
    _, occupied, width = parts[0].shape
    return pl.pallas_call(
        functools.partial(table_kernel, count, pairs, capacity, shells, slab),
        out_shape=(
            jax.ShapeDtypeStruct((2 * count + 8, LANES), jnp.int32),
            jax.ShapeDtypeStruct((count * width // 8 + 2, occupied, LANES), jnp.float32),
        ),
        grid_spec=pltpu.PrefetchScalarGridSpec(
            num_scalar_prefetch=1,
            grid=(1,),
            in_specs=[pl.BlockSpec((2, occupied, width), lambda g, w: (aux // 2, 0, 0))] * count + [VMEM] * 2,
            out_specs=(VMEM, VMEM),
            scratch_shapes=[pltpu.VMEM((count, occupied, width), jnp.float32)],
        ),
        compiler_params=pltpu.CompilerParams(vmem_limit_bytes=44 * MIB),
        cost_estimate=pl.CostEstimate(flops=0, transcendentals=0, bytes_accessed=16 * MIB),
    )(position, *parts, shell_table, repeat)


def window(ref, tile, shift, lane):
    top = ref.shape[1] // LANES - 1
    tiles = [ref[:, pl.ds(pl.multiple_of(t * LANES, LANES), LANES)] for t in (tile, jnp.minimum(tile + 1, top))]
    turned = [pltpu.roll(t.astype(jnp.float32), (LANES - shift) % LANES, 1) for t in tiles]
    return jnp.where(lane < LANES - shift, turned[0], turned[1]).astype(jnp.bfloat16)


def block_kernel(ks, resumed, group, count, capacity, slab, meta_ref, table_ref, *refs):
    refs = list(refs)
    halves = [refs.pop(0) for _ in ks]
    old_sum_ref = refs.pop(1) if resumed else None
    if resumed:
        refs.pop(0)
    out_ref, sum_ref, buffer_ref, zero_ref, square_ref, sems = refs
    aux = halves[0].shape[0]
    occupied = table_ref.shape[1]
    per = LANES // occupied
    lane = lax.broadcasted_iota(jnp.int32, (occupied, LANES), 1)
    column = lane % PAD
    wide_lane = lax.broadcasted_iota(jnp.int32, (aux, LANES), 1)
    ones = jnp.ones((8, LANES), jnp.float32)
    zero_ref[...] = jnp.zeros(zero_ref.shape, zero_ref.dtype)
    sum_ref[...] = old_sum_ref[...] if resumed else jnp.zeros(sum_ref.shape, jnp.float32)
    groups = capacity // group

    for n, k in enumerate(ks):
        base = meta_ref[2 * count, 0] ^ k
        live = meta_ref[count + k, 0]

        def send(source, at, n=n, base=base):
            target = out_ref.at[pl.ds(base * capacity + at, group)]
            return pltpu.make_async_copy(source, target, sems.at[n * groups + at // group])

        @pl.loop(0, groups)
        def _(turn, n=n, k=k, base=base, live=live, send=send):
            at = turn * group

            @pl.when(at < live)
            def _():
                for s in range(group):
                    mu, nu = meta_ref[k, at + s], meta_ref[k, capacity + at + s]
                    mu_start, mu_length = mu // CODE, mu % CODE
                    nu_length = nu % CODE
                    nu_start = jnp.maximum(nu // CODE - base * slab, 0)
                    left = window(halves[n], nu_start // per, nu_start % per * occupied, wide_lane)
                    tile, shift = mu_start // (LANES // PAD), mu_start % (LANES // PAD) * PAD
                    x = [pltpu.roll(table_ref[tile + q], (LANES - shift) % LANES, 1) for q in range(3)]
                    keep = lane < LANES - shift
                    coeff = []
                    for q in range(2):
                        valid = (column < nu_length) & (lane + q * LANES < mu_length * PAD)
                        coeff.append(jnp.where(valid, jnp.where(keep, x[q], x[q + 1]), 0.0))
                    right = [
                        jnp.concatenate([jnp.where(column == m, c, 0.0) for m in range(PAD)], axis=0) for c in coeff
                    ]
                    right = jnp.concatenate(right, axis=1).astype(jnp.bfloat16)
                    block = dot(left, right).astype(jnp.bfloat16)
                    buffer_ref[n, at + s] = block
                    wide = block.astype(jnp.float32)
                    total = jnp.sum(wide * wide, axis=0, keepdims=True)
                    square_ref[pl.ds(at + s, 1), :] = total[:, :LANES] + total[:, LANES:]
                send(buffer_ref.at[n, pl.ds(at, group)], at).start()

            @pl.when(at >= live)
            def _():
                square_ref[pl.ds(at, group), :] = jnp.zeros((group, LANES), jnp.float32)
                send(zero_ref, at).start()

        sums = lax.dot_general(
            ones,
            square_ref[...],
            (((1,), (1,)), ((), ())),
            precision=lax.Precision.HIGHEST,
            preferred_element_type=jnp.float32,
        )
        sum_ref[pl.ds(base, 1), :] = sums[:1]

    for n, k in enumerate(ks):
        base = meta_ref[2 * count, 0] ^ k
        for turn in range(groups):
            target = out_ref.at[pl.ds(base * capacity + turn * group, group)]
            pltpu.make_async_copy(zero_ref, target, sems.at[n * groups + turn]).wait()


def make_blocks(ks, count, capacity, slab, meta, halves, table, done):
    aux = halves[ks[0]].shape[0]
    slots = count * capacity
    group = min(GROUP, capacity)
    carried = [] if done is None else list(done)
    return pl.pallas_call(
        functools.partial(block_kernel, ks, bool(carried), group, count, capacity, slab),
        out_shape=(
            jax.ShapeDtypeStruct((slots, aux, PAD * PAD), jnp.bfloat16),
            jax.ShapeDtypeStruct((count, capacity), jnp.float32),
        ),
        grid_spec=pltpu.PrefetchScalarGridSpec(
            num_scalar_prefetch=1,
            grid=(),
            in_specs=[VMEM] * (1 + len(ks)) + ([HBM, VMEM] if carried else []),
            out_specs=(HBM, VMEM),
            scratch_shapes=[
                pltpu.VMEM((len(ks), capacity, aux, PAD * PAD), jnp.bfloat16),
                pltpu.VMEM((group, aux, PAD * PAD), jnp.bfloat16),
                pltpu.VMEM((capacity, LANES), jnp.float32),
                pltpu.SemaphoreType.DMA((len(ks) * capacity // group,)),
            ],
        ),
        input_output_aliases={2 + len(ks): 0} if carried else {},
        compiler_params=pltpu.CompilerParams(vmem_limit_bytes=24 * MIB),
        cost_estimate=pl.CostEstimate(flops=0, transcendentals=0, bytes_accessed=len(ks) * 6 * MIB),
    )(meta, table, *[halves[k] for k in ks], *carried)


def per_device(density, vir_coeffs, occ_coeffs, shell_len, mu_shell, nu_shell, owner):
    count = lax.axis_size("rows")
    columns = lax.axis_size("aux")
    position = lax.axis_index("rows").astype(jnp.int32).reshape(1)
    aux, occupied, width = density.shape
    slab = vir_coeffs.shape[0]
    shells = shell_len.shape[1]
    pairs = mu_shell.shape[0]
    capacity = 2 * pairs // count

    packed = whole(
        pack_kernel,
        jax.ShapeDtypeStruct((aux + 2, occupied, width), jnp.bfloat16),
        [density, occ_coeffs, mu_shell.reshape(1, pairs), nu_shell.reshape(1, pairs), owner.reshape(1, pairs)],
        scratch=[pltpu.VMEM((3, 1, pairs), jnp.int32), pltpu.SemaphoreType.DMA((5,))],
        specs=[HBM] * 5,
    )

    span = occupied * LANES
    source = jnp.arange(span, dtype=jnp.int32)[:, None]
    target = jnp.arange(span, dtype=jnp.int32)[None, :]
    spread = (target == source % LANES * occupied + source // LANES).astype(jnp.bfloat16)
    repeat = (
        jnp.arange(LANES, dtype=jnp.int32)[:, None] == jnp.arange(LANES * PAD, dtype=jnp.int32)[None, :] // PAD
    ).astype(jnp.bfloat16)
    earlier = jnp.arange(shells)[:, None] < jnp.arange(shells)[None, :]
    starts = jnp.sum(jnp.where(earlier[None], shell_len[:, :, None], 0), axis=1)
    starts = (starts + jnp.arange(count, dtype=jnp.int32)[:, None] * slab).reshape(-1)
    digits = jnp.stack([starts // DIGIT, starts % DIGIT, shell_len.reshape(-1)])
    shell_table = jnp.pad(digits, ((0, 5), (0, 0))).astype(jnp.bfloat16)

    half, parts = make_half(position, packed, vir_coeffs, spread, aux)
    state = {}

    def tables(halves):
        state["meta"], state["table"] = make_tables(
            position, parts, shell_table, repeat, pairs, capacity, shells, slab, aux
        )
        return state["meta"]

    def blocks_of(ks, halves):
        state["done"] = make_blocks(
            ks, count, capacity, slab, state["meta"], halves, state["table"], state.get("done")
        )
        return state["done"][1]

    halves = gather(half, count, tables, lambda halves: blocks_of([0, 1, 2], halves))
    blocks_of([4, *range(6, count, 2), 3], halves)
    for k in range(5, count, 2):
        blocks_of([k], halves)
    blocks, sums = state["done"]
    sums = [sums] + [swap(sums, k, columns, "aux") for k in range(1, columns)]
    while len(sums) > 1:
        sums = [sums[n] + sums[n + 1] for n in range(0, len(sums), 2)]
    pair_scale = jnp.sqrt(sums[0].reshape(-1) / (NAUX * PAD * PAD) + 1e-06)
    return blocks, pair_scale


def solution(mesh):
    return jax.shard_map(
        per_device,
        mesh=mesh,
        in_specs=(
            P("aux", None, "rows"),
            P("rows", None),
            P(None, "rows"),
            P(),
            P("rows"),
            P("rows"),
            P("rows", None),
        ),
        out_specs=(P("rows", "aux", None), P("rows")),
        check_vma=False,
    )
```

time: 402 us -> 107 us (0.27)
  blocking collectives: 224 us -> 0 us
  local copies, waits for them, and re-layouts: 120 us -> 6.68 us
  Pallas kernels: 0 us -> 38.1 us
  waiting for transfers between devices: 0.7 us -> 34.6 us
  matrix products: 30.8 us -> 0 us
  starting transfers between devices: 0.04 us -> 26.1 us
  between operations: 14.2 us -> 0.81 us
  other arithmetic: 9.99 us -> 1.49 us
    all_to_all x1 -> x0, blocking collectives: 183 us -> none  [per_device(): lax.all_to_all(outgoing, 'rows', split_axis=0, concat_axis=0, tiled=True)]
    convert_element_type x1 -> x0, local copies, waits for them, and re-layouts: 48.5 us -> none  [per_device(): blocks.astype(jnp.bfloat16).reshape(slot_total, local_aux, PAD * PAD)]
    pallas_call x0 -> x9, Pallas kernels: none -> 38.1 us  [the longest x4 30.3 us: make_blocks(): pl.pallas_call(functools.partial(block_kernel, ks, bool(carried), group,...]
    all_gather x1 -> x0, blocking collectives: 35.7 us -> none  [per_device(): occ_full = lax.all_gather(occ_coeffs, 'rows', axis=1, tiled=True)]
    ppermute x0 -> x17, waiting for transfers between devices: none -> 34.6 us  [swap(): return lax.ppermute(x, axis, [(i, i ^ k) for i in range(count)])]
    reshape x2 -> x0, local copies, waits for them, and re-layouts: 32.3 us -> none  [the longest x1 17.7 us: per_device(): half_slots.reshape(local_aux, occupied, slot_total, PAD)]
    dot_general x3 -> x0, matrix products: 30.8 us -> none  [the longest x1 19.8 us: per_device(): jnp.einsum('ism,pisn->spmn', coeff_slots.reshape(occupied, slot_total, PA...]
    ppermute x0 -> x17, starting transfers between devices: none -> 26.1 us  [swap(): return lax.ppermute(x, axis, [(i, i ^ k) for i in range(count)])]
  transfers between devices with their start and end apart: 1 -> 17, of which waited for: 0 -> 8; matrix products, arithmetic and copies ran while one was open for 9% -> 2% of each run, Pallas kernels for 0% -> 30%
where the time goes in v1:
time: 107 us; the launch traced here: 108 us
  Pallas kernels  38.1 us (36%)
  waiting for transfers between devices  34.6 us (32%)
  starting transfers between devices  26.1 us (24%)
  local copies, waits for them, and re-layouts  6.68 us (6%)
  other arithmetic  1.49 us (1%)
    ppermute x17, waiting for transfers between devices, swap(): return lax.ppermute(x, axis, [(i, i ^ k) for i in range(count)])  34.6 us
    pallas_call x4, Pallas kernels, make_blocks(): pl.pallas_call(functools.partial(block_kernel, ks, bool(carried), group,...  30.3 us
    ppermute x17, starting transfers between devices, swap(): return lax.ppermute(x, axis, [(i, i ^ k) for i in range(count)])  26.1 us
    unnamed x16, local copies, waits for them, and re-layouts  5.87 us
    pallas_call x4, Pallas kernels, whole(): pl.pallas_call(body, out_shape=out_shape, grid_spec=pltpu.PrefetchScalarG...  4.16 us
    pallas_call x1, Pallas kernels, make_tables(): pl.pallas_call(functools.partial(table_kernel, count, pairs, capacity, sh...  3.65 us
  transfers between devices with their start and end apart: 17, of which 8 were waited for; matrix products, arithmetic and copies ran while one was open for 2% of the time, Pallas kernels for 30%

profile of v1, /device:TPU:0, one launch (start us, length us, event | category | flops | bytes accessed | tf_op | source)
XLA Modules:
  0.0 107.8 jit_solution(13264352234514267595)
XLA Ops:
  0.6 0.0 copy-start.2
  0.6 0.9 copy-done.2
  1.6 0.0 copy-start.3
  1.6 0.7 copy-done.3
  2.3 0.0 copy-start.4
  2.3 0.7 copy-done.4
  3.0 0.0 copy-start.5
  3.0 0.7 copy-done.5
  3.6 0.0 copy-start.6
  3.6 0.7 copy-done.6
  4.3 0.1 shard_map.86.refs_0_
  4.4 3.0 %collective-permute-start = (bf16[34,8,512]{2,1,0:T(8,128)(2,1)S(1)}, bf16[34,8,512]{2,1,0:T(8,128)(2,1)S(1)}, u32[]{:S(2)}, u32[]{:S(2)}) collective-permute-start(bf16[34,8,512]{2,1,0:T(8,128)(2,1)S(1)} %shard_map.86.refs_0_), channel_id=1, source_target_pairs={{0,4},{4,0},{8,12},{12,8},{16,20},{20,16},{24,28},{28,24},{1,5},{5... | collective-permute-start | bytes 835592 | tf_op jit(solution)/shard_map/ppermute | solution.py:22
  7.5 1.6 %collective-permute-start.1 = (bf16[34,8,512]{2,1,0:T(8,128)(2,1)S(1)}, bf16[34,8,512]{2,1,0:T(8,128)(2,1)S(1)}, u32[]{:S(2)}, u32[]{:S(2)}) collective-permute-start(bf16[34,8,512]{2,1,0:T(8,128)(2,1)S(1)} %shard_map.86.refs_0_), channel_id=1, source_target_pairs={{0,8},{4,12},{8,0},{12,4},{16,24},{20,28},{24,16},{28,20},{1,9},{5... | collective-permute-start | bytes 835592 | tf_op jit(solution)/shard_map/ppermute | solution.py:22
  9.0 2.6 %collective-permute-start.3 = (bf16[34,8,512]{2,1,0:T(8,128)(2,1)S(1)}, bf16[34,8,512]{2,1,0:T(8,128)(2,1)S(1)}, u32[]{:S(2)}, u32[]{:S(2)}) collective-permute-start(bf16[34,8,512]{2,1,0:T(8,128)(2,1)S(1)} %shard_map.86.refs_0_), channel_id=1, source_target_pairs={{0,16},{4,20},{8,24},{12,28},{16,0},{20,4},{24,8},{28,12},{1,17},{... | collective-permute-start | bytes 835592 | tf_op jit(solution)/shard_map/ppermute | solution.py:22
  11.6 0.1 fusion.1.refs_9_
  11.7 2.4 %collective-permute-done.refs_1_ = bf16[34,8,512]{2,1,0:T(8,128)(2,1)S(1)} collective-permute-done((bf16[34,8,512]{2,1,0:T(8,128)(2,1)S(1)}, bf16[34,8,512]{2,1,0:T(8,128)(2,1)S(1)}, u32[]{:S(2)}, u32[]{:S(2)}) %collective-permute-start) | collective-permute-done | bytes 278560 | tf_op jit(solution)/shard_map/ppermute | solution.py:22
  14.1 3.8 %collective-permute-start.5 = (bf16[34,8,512]{2,1,0:T(8,128)(2,1)S(1)}, bf16[34,8,512]{2,1,0:T(8,128)(2,1)S(1)}, u32[]{:S(2)}, u32[]{:S(2)}) collective-permute-start(bf16[34,8,512]{2,1,0:T(8,128)(2,1)S(1)} %shard_map.86.refs_0_), channel_id=1, source_target_pairs={{0,24},{4,28},{8,16},{12,20},{16,8},{20,12},{24,0},{28,4},{1,25},{... | collective-permute-start | bytes 835592 | tf_op jit(solution)/shard_map/ppermute | solution.py:22
  17.9 0.8 select_reduce_fusion
  18.8 12.2 %collective-permute-done.3.refs_4_.refs_3_ = bf16[34,8,512]{2,1,0:T(8,128)(2,1)S(1)} collective-permute-done((bf16[34,8,512]{2,1,0:T(8,128)(2,1)S(1)}, bf16[34,8,512]{2,1,0:T(8,128)(2,1)S(1)}, u32[]{:S(2)}, u32[]{:S(2)}) %collective-permute-start.3) | collective-permute-done | bytes 278560 | tf_op jit(solution)/shard_map/ppermute | solution.py:22
  31.0 0.0 collective-permute-start.4
  31.0 0.0 collective-permute-done.1.refs_2_
  31.0 2.0 %collective-permute-start.2 = (bf16[34,8,512]{2,1,0:T(8,128)(2,1)S(1)}, bf16[34,8,512]{2,1,0:T(8,128)(2,1)S(1)}, u32[]{:S(2)}, u32[]{:S(2)}) collective-permute-start(bf16[34,8,512]{2,1,0:T(8,128)(2,1)S(1)} %collective-permute-done.1.refs_2_), channel_id=1, source_target_pairs={{0,4},{4,0},{8,12},{12,8},{16,20},{20,16},{24,28},{28,24},{1,5},{5... | collective-permute-start | bytes 835592 | tf_op jit(solution)/shard_map/ppermute | solution.py:22
  33.0 0.0 collective-permute-done.5.refs_6_.refs_0_
  33.0 0.1 collective-permute-start.6
  33.1 0.4 fusion.spread_ref
  33.5 0.0 copy-start
  33.5 2.2 %copy-done = bf16[512,4096]{1,0:T(8,128)(2,1)S(1)} copy-done((bf16[512,4096]{1,0:T(8,128)(2,1)S(1)}, bf16[512,4096]{1,0:T(8,128)(2,1)}, u32[]{:S(2)}) %copy-start) | copy-done | bytes 4194328
  35.7 1.5 %shard_map.88 = (f32[256,512]{1,0:T(8,128)S(1)}, f32[8,128]{1,0:T(8,128)}) custom-call(s32[1]{0:T(128)} %bitcast.where_ref, bf16[512,4096]{1,0:T(8,128)(2,1)S(1)} %copy-done, bf16[34,8,512]{2,1,0:T(8,128)(2,1)S(1)} %shard_map.86.refs_0_, bf16[34,8,512]{2,1,0:T(8,128)(2,1)S(1)} %collective-permute-done.refs_1_, ...), custom_call_target="tpu_custom_call" | custom-call | bytes 8388608 | tf_op jit(solution)/shard_map/pallas_call | solution.py:56
  37.2 5.3 %collective-permute-done.2.refs_3_.refs_1_ = bf16[34,8,512]{2,1,0:T(8,128)(2,1)S(1)} collective-permute-done((bf16[34,8,512]{2,1,0:T(8,128)(2,1)S(1)}, bf16[34,8,512]{2,1,0:T(8,128)(2,1)S(1)}, u32[]{:S(2)}, u32[]{:S(2)}) %collective-permute-start.2) | collective-permute-done | bytes 278560 | tf_op jit(solution)/shard_map/ppermute | solution.py:22
  42.5 0.0 collective-permute-done.4.refs_5_.refs_2_
  42.5 0.0 copy-done.1
  42.5 1.8 %shard_map.89 = (f32[256,512]{1,0:T(8,128)S(1)}, f32[8,128]{1,0:T(8,128)}, bf16[512,512]{1,0:T(8,128)(2,1)S(1)}) custom-call(s32[1]{0:T(128)} %bitcast.where_ref, bf16[512,4096]{1,0:T(8,128)(2,1)S(1)} %copy-done.1, bf16[34,8,512]{2,1,0:T(8,128)(2,1)S(1)} %collective-permute-done.5.refs_6_.refs_0_, ...), custom_call_target="tpu_custom_call" | custom-call | bytes 6291456 | tf_op jit(solution)/shard_map/pallas_call | solution.py:56
  44.3 2.0 %collective-permute-done.6.refs_7_.part_ref = bf16[34,8,512]{2,1,0:T(8,128)(2,1)S(1)} collective-permute-done((bf16[34,8,512]{2,1,0:T(8,128)(2,1)S(1)}, bf16[34,8,512]{2,1,0:T(8,128)(2,1)S(1)}, u32[]{:S(2)}, u32[]{:S(2)}) %collective-permute-start.6) | collective-permute-done | bytes 278560 | tf_op jit(solution)/shard_map/ppermute | solution.py:22
  46.3 0.8 shard_map.90.refs_0_
  47.1 0.1 collective-permute-start.7
  47.1 0.1 broadcast_add_fusion
  47.2 0.0 copy-done.7
  47.2 0.1 add.95
  47.3 0.1 stack_reshape.4
  47.4 0.4 collective-permute-start.9
  47.9 3.2 %collective-permute-start.11 = (bf16[32,4096]{1,0:T(8,128)(2,1)S(1)}, bf16[32,4096]{1,0:T(8,128)(2,1)S(1)}, u32[]{:S(2)}, u32[]{:S(2)}) collective-permute-start(bf16[32,4096]{1,0:T(8,128)(2,1)S(1)} %shard_map.90.refs_0_), channel_id=1, source_target_pairs={{0,16},{4,20},{8,24},{12,28},{16,0},{20,4},{24,8},{28,12},{1,17},{... | collective-permute-start | bytes 786440 | tf_op jit(solution)/shard_map/ppermute | solution.py:22
  51.1 2.5 %collective-permute-done.7.refs_1_ = bf16[32,4096]{1,0:T(8,128)(2,1)S(1)} collective-permute-done((bf16[32,4096]{1,0:T(8,128)(2,1)S(1)}, bf16[32,4096]{1,0:T(8,128)(2,1)S(1)}, u32[]{:S(2)}, u32[]{:S(2)}) %collective-permute-start.7) | collective-permute-done | bytes 262176 | tf_op jit(solution)/shard_map/ppermute | solution.py:22
  53.5 3.0 %collective-permute-start.8 = (bf16[32,4096]{1,0:T(8,128)(2,1)S(1)}, bf16[32,4096]{1,0:T(8,128)(2,1)S(1)}, u32[]{:S(2)}, u32[]{:S(2)}) collective-permute-start(bf16[32,4096]{1,0:T(8,128)(2,1)S(1)} %shard_map.90.refs_0_), channel_id=1, source_target_pairs={{0,24},{4,28},{8,16},{12,20},{16,8},{20,12},{24,0},{28,4},{1,25},{... | collective-permute-start | bytes 786440 | tf_op jit(solution)/shard_map/ppermute | solution.py:22
  56.5 3.6 %shard_map.87 = (s32[24,128]{1,0:T(8,128)S(1)}, f32[514,8,128]{2,1,0:T(8,128)S(1)}) custom-call(s32[1]{0:T(128)} %bitcast.where_ref, bf16[34,8,512]{2,1,0:T(8,128)(2,1)S(1)} %shard_map.86.refs_0_, bf16[34,8,512]{2,1,0:T(8,128)(2,1)S(1)} %collective-permute-done.refs_1_, bf16[34,8,512]{2,1,0:T(8,128)(2,1)S(1)} %collective-permute-done.1.refs_2_, ...), custom_call_target="tpu_custom_call" | custom-call | bytes 16777216 | tf_op jit(solution)/shard_map/pallas_call | solution.py:243
  60.1 7.6 %collective-permute-done.11.refs_0_ = bf16[32,4096]{1,0:T(8,128)(2,1)S(1)} collective-permute-done((bf16[32,4096]{1,0:T(8,128)(2,1)S(1)}, bf16[32,4096]{1,0:T(8,128)(2,1)S(1)}, u32[]{:S(2)}, u32[]{:S(2)}) %collective-permute-start.11) | collective-permute-done | bytes 262176 | tf_op jit(solution)/shard_map/ppermute | solution.py:22
  67.7 1.6 %collective-permute-start.12 = (bf16[32,4096]{1,0:T(8,128)(2,1)S(1)}, bf16[32,4096]{1,0:T(8,128)(2,1)S(1)}, u32[]{:S(2)}, u32[]{:S(2)}) collective-permute-start(bf16[32,4096]{1,0:T(8,128)(2,1)S(1)} %collective-permute-done.11.refs_0_), channel_id=1, source_target_pairs={{0,4},{4,0},{8,12},{12,8},{16,20},{20,16},{24,28},{28,24},{1,5},{5... | collective-permute-start | bytes 786440 | tf_op jit(solution)/shard_map/ppermute | solution.py:22
  69.4 0.0 collective-permute-done.9.refs_2_
  69.4 0.4 collective-permute-start.13
  69.8 10.1 %shard_map.91 = (bf16[512,32,256]{2,1,0:T(8,128)(2,1)}, f32[8,64]{1,0:T(8,128)S(1)}) custom-call(s32[24,128]{1,0:T(8,128)S(1)} %get-tuple-element.20.meta_ref, f32[514,8,128]{2,1,0:T(8,128)S(1)} %get-tuple-element.21.table_ref, bf16[32,4096]{1,0:T(8,128)(2,1)S(1)} %shard_map.90.refs_0_, bf16[32,4096]{1,0:T(8,128)(2,1)S(1)} %collective-permute-done.7.refs_1_, ...), custom_call_target="tpu_custom_call" | custom-call | bytes 18874368 | tf_op jit(solution)/shard_map/pallas_call | solution.py:350
  79.9 0.0 collective-permute-done.8.refs_1_
  79.9 2.4 %collective-permute-start.10 = (bf16[32,4096]{1,0:T(8,128)(2,1)S(1)}, bf16[32,4096]{1,0:T(8,128)(2,1)S(1)}, u32[]{:S(2)}, u32[]{:S(2)}) collective-permute-start(bf16[32,4096]{1,0:T(8,128)(2,1)S(1)} %collective-permute-done.8.refs_1_), channel_id=1, source_target_pairs={{0,4},{4,0},{8,12},{12,8},{16,20},{20,16},{24,28},{28,24},{1,5},{5... | collective-permute-start | bytes 786440 | tf_op jit(solution)/shard_map/ppermute | solution.py:22
  82.3 0.0 collective-permute-done.13.refs_2_
  82.3 11.0 %shard_map.92 = (bf16[512,32,256]{2,1,0:T(8,128)(2,1)}, f32[8,64]{1,0:T(8,128)S(1)}) custom-call(s32[24,128]{1,0:T(8,128)S(1)} %get-tuple-element.20.meta_ref, f32[514,8,128]{2,1,0:T(8,128)S(1)} %get-tuple-element.21.table_ref, bf16[32,4096]{1,0:T(8,128)(2,1)S(1)} %collective-permute-done.11.refs_0_, ...), custom_call_target="tpu_custom_call", output_to_operand_aliasing={{0}: (5, {})} | custom-call | bytes 18874368 | tf_op jit(solution)/shard_map/pallas_call | solution.py:350
  93.3 0.0 collective-permute-done.12.refs_0_
  93.3 4.6 %shard_map.93 = (bf16[512,32,256]{2,1,0:T(8,128)(2,1)}, f32[8,64]{1,0:T(8,128)S(1)}) custom-call(s32[24,128]{1,0:T(8,128)S(1)} %get-tuple-element.20.meta_ref, f32[514,8,128]{2,1,0:T(8,128)S(1)} %get-tuple-element.21.table_ref, bf16[32,4096]{1,0:T(8,128)(2,1)S(1)} %collective-permute-done.12.refs_0_, ...), custom_call_target="tpu_custom_call", output_to_operand_aliasing={{0}: (3, {})} | custom-call | bytes 6291456 | tf_op jit(solution)/shard_map/pallas_call | solution.py:350
  97.9 0.0 collective-permute-done.10.refs_0_
  97.9 4.6 %shard_map.94 = (bf16[512,32,256]{2,1,0:T(8,128)(2,1)}, f32[8,64]{1,0:T(8,128)S(1)}) custom-call(s32[24,128]{1,0:T(8,128)S(1)} %get-tuple-element.20.meta_ref, f32[514,8,128]{2,1,0:T(8,128)S(1)} %get-tuple-element.21.table_ref, bf16[32,4096]{1,0:T(8,128)(2,1)S(1)} %collective-permute-done.10.refs_0_, ...), custom_call_target="tpu_custom_call", output_to_operand_aliasing={{0}: (3, {})} | custom-call | bytes 6291456 | tf_op jit(solution)/shard_map/pallas_call | solution.py:350
  102.5 0.1 collective-permute-start.14
  102.6 1.6 %collective-permute-start.15 = (f32[8,64]{1,0:T(8,128)S(1)}, f32[8,64]{1,0:T(8,128)S(1)}, u32[]{:S(2)}, u32[]{:S(2)}) collective-permute-start(f32[8,64]{1,0:T(8,128)S(1)} %get-tuple-element.35), channel_id=1, source_target_pairs={{0,2},{1,3},{2,0},{3,1},{4,6},{5,7},{6,4},{7,5},{8,10},{9,11},{10,... | collective-permute-start | bytes 6152 | tf_op jit(solution)/shard_map/ppermute | solution.py:22
  104.1 0.3 collective-permute-start.16
  104.4 0.0 collective-permute-done.14
  104.4 1.8 %collective-permute-done.15 = f32[8,64]{1,0:T(8,128)S(1)} collective-permute-done((f32[8,64]{1,0:T(8,128)S(1)}, f32[8,64]{1,0:T(8,128)S(1)}, u32[]{:S(2)}, u32[]{:S(2)}) %collective-permute-start.15) | collective-permute-done | bytes 2080 | tf_op jit(solution)/shard_map/ppermute | solution.py:22
  106.2 0.9 collective-permute-done.16
  107.2 0.7 sqrt.7
  (11 shorter events, 0.1 us)
Async XLA Ops:
  0.6 1.0 copy-start.2
  1.6 0.7 copy-start.3
  2.3 0.7 copy-start.4
  3.0 0.7 copy-start.5
  3.6 0.7 copy-start.6
  4.4 9.7 %collective-permute-start = (bf16[34,8,512]{2,1,0:T(8,128)(2,1)S(1)}, bf16[34,8,512]{2,1,0:T(8,128)(2,1)S(1)}, u32[]{:S(2)}, u32[]{:S(2)}) collective-permute-start(bf16[34,8,512]{2,1,0:T(8,128)(2,1)S(1)} %shard_map.86.refs_0_), channel_id=1, source_target_pairs={{0,4},{4,0},{8,12},{12,8},{16,20},{20,16},{24,28},{28,24},{1,5},{5... | collective-permute-start | bytes 835592 | tf_op jit(solution)/shard_map/ppermute | solution.py:22
  7.5 23.5 %collective-permute-start.1 = (bf16[34,8,512]{2,1,0:T(8,128)(2,1)S(1)}, bf16[34,8,512]{2,1,0:T(8,128)(2,1)S(1)}, u32[]{:S(2)}, u32[]{:S(2)}) collective-permute-start(bf16[34,8,512]{2,1,0:T(8,128)(2,1)S(1)} %shard_map.86.refs_0_), channel_id=1, source_target_pairs={{0,8},{4,12},{8,0},{12,4},{16,24},{20,28},{24,16},{28,20},{1,9},{5... | collective-permute-start | bytes 835592 | tf_op jit(solution)/shard_map/ppermute | solution.py:22
  9.0 21.9 %collective-permute-start.3 = (bf16[34,8,512]{2,1,0:T(8,128)(2,1)S(1)}, bf16[34,8,512]{2,1,0:T(8,128)(2,1)S(1)}, u32[]{:S(2)}, u32[]{:S(2)}) collective-permute-start(bf16[34,8,512]{2,1,0:T(8,128)(2,1)S(1)} %shard_map.86.refs_0_), channel_id=1, source_target_pairs={{0,16},{4,20},{8,24},{12,28},{16,0},{20,4},{24,8},{28,12},{1,17},{... | collective-permute-start | bytes 835592 | tf_op jit(solution)/shard_map/ppermute | solution.py:22
  14.1 18.9 %collective-permute-start.5 = (bf16[34,8,512]{2,1,0:T(8,128)(2,1)S(1)}, bf16[34,8,512]{2,1,0:T(8,128)(2,1)S(1)}, u32[]{:S(2)}, u32[]{:S(2)}) collective-permute-start(bf16[34,8,512]{2,1,0:T(8,128)(2,1)S(1)} %shard_map.86.refs_0_), channel_id=1, source_target_pairs={{0,24},{4,28},{8,16},{12,20},{16,8},{20,12},{24,0},{28,4},{1,25},{... | collective-permute-start | bytes 835592 | tf_op jit(solution)/shard_map/ppermute | solution.py:22
  31.0 11.5 %collective-permute-start.4 = (bf16[34,8,512]{2,1,0:T(8,128)(2,1)S(1)}, bf16[34,8,512]{2,1,0:T(8,128)(2,1)S(1)}, u32[]{:S(2)}, u32[]{:S(2)}) collective-permute-start(bf16[34,8,512]{2,1,0:T(8,128)(2,1)S(1)} %collective-permute-done.3.refs_4_.refs_3_), channel_id=1, source_target_pairs={{0,4},{4,0},{8,12},{12,8},{16,20},{20,16},{24,28},{28,24},{1,5},{5... | collective-permute-start | bytes 835592 | tf_op jit(solution)/shard_map/ppermute | solution.py:22
  31.0 11.5 %collective-permute-start.2 = (bf16[34,8,512]{2,1,0:T(8,128)(2,1)S(1)}, bf16[34,8,512]{2,1,0:T(8,128)(2,1)S(1)}, u32[]{:S(2)}, u32[]{:S(2)}) collective-permute-start(bf16[34,8,512]{2,1,0:T(8,128)(2,1)S(1)} %collective-permute-done.1.refs_2_), channel_id=1, source_target_pairs={{0,4},{4,0},{8,12},{12,8},{16,20},{20,16},{24,28},{28,24},{1,5},{5... | collective-permute-start | bytes 835592 | tf_op jit(solution)/shard_map/ppermute | solution.py:22
  33.0 13.3 %collective-permute-start.6 = (bf16[34,8,512]{2,1,0:T(8,128)(2,1)S(1)}, bf16[34,8,512]{2,1,0:T(8,128)(2,1)S(1)}, u32[]{:S(2)}, u32[]{:S(2)}) collective-permute-start(bf16[34,8,512]{2,1,0:T(8,128)(2,1)S(1)} %collective-permute-done.5.refs_6_.refs_0_), channel_id=1, source_target_pairs={{0,4},{4,0},{8,12},{12,8},{16,20},{20,16},{24,28},{28,24},{1,5},{5... | collective-permute-start | bytes 835592 | tf_op jit(solution)/shard_map/ppermute | solution.py:22
  33.5 2.2 %copy-start = (bf16[512,4096]{1,0:T(8,128)(2,1)S(1)}, bf16[512,4096]{1,0:T(8,128)(2,1)}, u32[]{:S(2)}) copy-start(bf16[512,4096]{1,0:T(8,128)(2,1)} %vir_ref.3) | copy-start | bytes 12582916
  35.7 6.8 %copy-start.1 = (bf16[512,4096]{1,0:T(8,128)(2,1)S(1)}, bf16[512,4096]{1,0:T(8,128)(2,1)}, u32[]{:S(2)}) copy-start(bf16[512,4096]{1,0:T(8,128)(2,1)} %vir_ref.3) | copy-start | bytes 12582916
  42.5 4.7 %copy-start.7 = (s32[8,64]{1,0:T(8,128)S(1)}, s32[8,64]{1,0:T(8,128)}, u32[]{:S(2)}) copy-start(s32[8,64]{1,0:T(8,128)} %param.10) | copy-start | bytes 6148
  47.1 6.4 %collective-permute-start.7 = (bf16[32,4096]{1,0:T(8,128)(2,1)S(1)}, bf16[32,4096]{1,0:T(8,128)(2,1)S(1)}, u32[]{:S(2)}, u32[]{:S(2)}) collective-permute-start(bf16[32,4096]{1,0:T(8,128)(2,1)S(1)} %shard_map.90.refs_0_), channel_id=1, source_target_pairs={{0,4},{4,0},{8,12},{12,8},{16,20},{20,16},{24,28},{28,24},{1,5},{5... | collective-permute-start | bytes 786440 | tf_op jit(solution)/shard_map/ppermute | solution.py:22
  47.4 22.0 %collective-permute-start.9 = (bf16[32,4096]{1,0:T(8,128)(2,1)S(1)}, bf16[32,4096]{1,0:T(8,128)(2,1)S(1)}, u32[]{:S(2)}, u32[]{:S(2)}) collective-permute-start(bf16[32,4096]{1,0:T(8,128)(2,1)S(1)} %shard_map.90.refs_0_), channel_id=1, source_target_pairs={{0,8},{4,12},{8,0},{12,4},{16,24},{20,28},{24,16},{28,20},{1,9},{5... | collective-permute-start | bytes 786440 | tf_op jit(solution)/shard_map/ppermute | solution.py:22
  47.9 19.9 %collective-permute-start.11 = (bf16[32,4096]{1,0:T(8,128)(2,1)S(1)}, bf16[32,4096]{1,0:T(8,128)(2,1)S(1)}, u32[]{:S(2)}, u32[]{:S(2)}) collective-permute-start(bf16[32,4096]{1,0:T(8,128)(2,1)S(1)} %shard_map.90.refs_0_), channel_id=1, source_target_pairs={{0,16},{4,20},{8,24},{12,28},{16,0},{20,4},{24,8},{28,12},{1,17},{... | collective-permute-start | bytes 786440 | tf_op jit(solution)/shard_map/ppermute | solution.py:22
  53.5 26.4 %collective-permute-start.8 = (bf16[32,4096]{1,0:T(8,128)(2,1)S(1)}, bf16[32,4096]{1,0:T(8,128)(2,1)S(1)}, u32[]{:S(2)}, u32[]{:S(2)}) collective-permute-start(bf16[32,4096]{1,0:T(8,128)(2,1)S(1)} %shard_map.90.refs_0_), channel_id=1, source_target_pairs={{0,24},{4,28},{8,16},{12,20},{16,8},{20,12},{24,0},{28,4},{1,25},{... | collective-permute-start | bytes 786440 | tf_op jit(solution)/shard_map/ppermute | solution.py:22
  67.7 25.6 %collective-permute-start.12 = (bf16[32,4096]{1,0:T(8,128)(2,1)S(1)}, bf16[32,4096]{1,0:T(8,128)(2,1)S(1)}, u32[]{:S(2)}, u32[]{:S(2)}) collective-permute-start(bf16[32,4096]{1,0:T(8,128)(2,1)S(1)} %collective-permute-done.11.refs_0_), channel_id=1, source_target_pairs={{0,4},{4,0},{8,12},{12,8},{16,20},{20,16},{24,28},{28,24},{1,5},{5... | collective-permute-start | bytes 786440 | tf_op jit(solution)/shard_map/ppermute | solution.py:22
  69.4 12.9 %collective-permute-start.13 = (bf16[32,4096]{1,0:T(8,128)(2,1)S(1)}, bf16[32,4096]{1,0:T(8,128)(2,1)S(1)}, u32[]{:S(2)}, u32[]{:S(2)}) collective-permute-start(bf16[32,4096]{1,0:T(8,128)(2,1)S(1)} %collective-permute-done.9.refs_2_), channel_id=1, source_target_pairs={{0,4},{4,0},{8,12},{12,8},{16,20},{20,16},{24,28},{28,24},{1,5},{5... | collective-permute-start | bytes 786440 | tf_op jit(solution)/shard_map/ppermute | solution.py:22
  79.9 18.0 %collective-permute-start.10 = (bf16[32,4096]{1,0:T(8,128)(2,1)S(1)}, bf16[32,4096]{1,0:T(8,128)(2,1)S(1)}, u32[]{:S(2)}, u32[]{:S(2)}) collective-permute-start(bf16[32,4096]{1,0:T(8,128)(2,1)S(1)} %collective-permute-done.8.refs_1_), channel_id=1, source_target_pairs={{0,4},{4,0},{8,12},{12,8},{16,20},{20,16},{24,28},{28,24},{1,5},{5... | collective-permute-start | bytes 786440 | tf_op jit(solution)/shard_map/ppermute | solution.py:22
  102.5 1.9 %collective-permute-start.14 = (f32[8,64]{1,0:T(8,128)S(1)}, f32[8,64]{1,0:T(8,128)S(1)}, u32[]{:S(2)}, u32[]{:S(2)}) collective-permute-start(f32[8,64]{1,0:T(8,128)S(1)} %get-tuple-element.35), channel_id=1, source_target_pairs={{0,1},{1,0},{2,3},{3,2},{4,5},{5,4},{6,7},{7,6},{8,9},{9,8},{10,11... | collective-permute-start | bytes 6152 | tf_op jit(solution)/shard_map/ppermute | solution.py:22
  102.6 3.7 %collective-permute-start.15 = (f32[8,64]{1,0:T(8,128)S(1)}, f32[8,64]{1,0:T(8,128)S(1)}, u32[]{:S(2)}, u32[]{:S(2)}) collective-permute-start(f32[8,64]{1,0:T(8,128)S(1)} %get-tuple-element.35), channel_id=1, source_target_pairs={{0,2},{1,3},{2,0},{3,1},{4,6},{5,7},{6,4},{7,5},{8,10},{9,11},{10,... | collective-permute-start | bytes 6152 | tf_op jit(solution)/shard_map/ppermute | solution.py:22
  104.1 3.0 %collective-permute-start.16 = (f32[8,64]{1,0:T(8,128)S(1)}, f32[8,64]{1,0:T(8,128)S(1)}, u32[]{:S(2)}, u32[]{:S(2)}) collective-permute-start(f32[8,64]{1,0:T(8,128)S(1)} %get-tuple-element.35), channel_id=1, source_target_pairs={{0,3},{1,2},{2,1},{3,0},{4,7},{5,6},{6,5},{7,4},{8,11},{9,10},{10,... | collective-permute-start | bytes 6152 | tf_op jit(solution)/shard_map/ppermute | solution.py:22

commit v2 on v1

--- a/solution.py
+++ b/solution.py
@@ -11,8 +11,9 @@
 PAD = 16
 LANES = 128
 DIGIT = 128
-CODE = 32
-GROUP = 16
+CODE_BITS = 5
+CODE = 1 << CODE_BITS
+GROUP = 32
 MIB = 1 << 20
 VMEM = pl.BlockSpec(memory_space=pltpu.VMEM)
 HBM = pl.BlockSpec(memory_space=pltpu.HBM)
@@ -22,25 +23,29 @@
     return lax.ppermute(x, axis, [(i, i ^ k) for i in range(count)])
 
 
-def after(x, *earlier):
-    return lax.optimization_barrier((x, *earlier))[0]
-
-
-def gather(x, count, first, second):
+def tie(*arrays):
+    return lax.optimization_barrier(arrays)
+
+
+def gather(x, count, name, early):
     parts = {0: x}
+
+    def move(k, value, by):
+        with jax.named_scope(f"{name}_{k}"):
+            parts[k] = swap(value, by, count)
+
     for k in (4, 2):
         if k < count:
-            parts[k] = swap(x, k, count)
-    parts[1] = swap(x, 1, count)
-    late = after(x, parts[1])
+            move(k, x, k)
+    move(1, x, 1)
+    x, parts[1] = tie(x, parts[1])
     for k in range(6, count, 2):
-        parts[k] = swap(late, k, count)
-    parts[3] = swap(parts[2], 1, count)
-    parts[5] = swap(after(parts[4], first(parts)), 1, count)
-    wait = second(parts)
-    for k in range(6, count, 2):
-        parts[k + 1] = swap(after(parts[k], wait) if wait is not None else parts[k], 1, count)
-    return [parts[k] for k in range(count)]
+        move(k, x, k)
+    move(3, parts[2], 1)
+    parts[4], parts[3], result = tie(parts[4], parts[3], early(parts))
+    for k in range(4, count, 2):
+        move(k + 1, parts[k], 1)
+    return [parts[k] for k in range(count)], result
 
 
 def dot(a, b):
@@ -51,7 +56,7 @@
     return lax.dot_general(a, b, (((1,), (1,)), ((), ())), preferred_element_type=jnp.float32)
 
 
-def whole(body, out_shape, args, scratch=(), scalars=0, specs=None, cost=None):
+def whole(body, out_shape, args, scratch=(), scalars=0, specs=None, cost=None, limit=44):
     outs = out_shape if isinstance(out_shape, tuple) else (out_shape,)
     return pl.pallas_call(
         body,
@@ -63,7 +68,7 @@
             out_specs=tuple(VMEM for _ in outs) if isinstance(out_shape, tuple) else VMEM,
             scratch_shapes=list(scratch),
         ),
-        compiler_params=pltpu.CompilerParams(vmem_limit_bytes=44 * MIB),
+        compiler_params=pltpu.CompilerParams(vmem_limit_bytes=limit * MIB),
         cost_estimate=pl.CostEstimate(flops=0, transcendentals=0, bytes_accessed=cost) if cost else None,
     )(*args)
 
@@ -95,9 +100,8 @@
     refs = list(refs)
     blocks = [refs.pop(0) for _ in ks]
     before_ref = refs.pop(0) if resumed else None
-    total_ref, token_ref = refs.pop(0), refs.pop(0)
+    total_ref = refs.pop(0)
     ahead_ref = refs.pop(0) if ahead is not None else None
-    token_ref[...] = jnp.zeros(token_ref.shape, jnp.float32)
     columns_ref, sems = refs
     _, occupied, width = blocks[0].shape
 
@@ -123,7 +127,7 @@
 def add_part(position, vir, parts, ks, before, ahead, aux):
     slab = vir.shape[0]
     _, occupied, width = parts[0].shape
-    out = [jax.ShapeDtypeStruct(shape, jnp.float32) for shape in ((aux * occupied, slab), (8, LANES))]
+    out = [jax.ShapeDtypeStruct((aux * occupied, slab), jnp.float32)]
     if ahead is not None:
         out.append(jax.ShapeDtypeStruct((slab, width), vir.dtype))
     args = [position, vir] + [parts[k] for k in ks] + ([] if before is None else [before])
@@ -161,17 +165,12 @@
     count = lax.axis_size("rows")
     slab = vir.shape[0]
     occupied = packed.shape[1]
-    order = [0, 1, 2, 4] + list(range(6, count, 2)) + list(range(3, count, 2))
+    order = [0, 1, 2, 3] + list(range(4, count, 2)) + list(range(5, count, 2))
     early, middle, last = order[:4], order[4:-1], order[-1]
-    totals = []
-
-    def start(parts):
-        total, token = add_part(position, vir, parts, early, None, None, aux)
-        totals.append(total)
-        return token
-
-    parts = gather(packed, count, start, lambda parts: None)
-    total, _, column = add_part(position, vir, parts, middle, totals[0], last, aux)
+    parts, total = gather(
+        packed, count, "density", lambda parts: add_part(position, vir, parts, early, None, None, aux)[0]
+    )
+    total, column = add_part(position, vir, parts, middle, total, last, aux)
     half = whole(
         functools.partial(half_kernel, aux),
         jax.ShapeDtypeStruct((aux, slab * occupied), jnp.bfloat16),
@@ -228,7 +227,10 @@
             jnp.where((slot == rank + shift) & (rank >= 0), 1.0, 0.0).astype(bf16) for shift in (0, capacity)
         ]
         mixed = dot_t(found[0], placed[0]) + dot_t(found[1], placed[1])
-        code = ((mixed[0:1] * DIGIT + mixed[1:2]) * CODE + mixed[2:3]).astype(jnp.int32)
+        start = mixed[0:1] * DIGIT + mixed[1:2]
+        number_of = lax.broadcasted_iota(jnp.int32, (1, LANES), 1)
+        start = jnp.where(number_of < capacity, start, jnp.maximum(start - source * slab, 0.0))
+        code = (start * CODE + mixed[2:3]).astype(jnp.int32)
         meta_ref[pl.ds(k, 1), :] = code
         live = jnp.sum(mine, axis=1, keepdims=True).astype(jnp.int32)
         meta_ref[pl.ds(count + k, 1), :] = jnp.broadcast_to(live, (1, LANES))
@@ -261,7 +263,7 @@
 def window(ref, tile, shift, lane):
     top = ref.shape[1] // LANES - 1
     tiles = [ref[:, pl.ds(pl.multiple_of(t * LANES, LANES), LANES)] for t in (tile, jnp.minimum(tile + 1, top))]
-    turned = [pltpu.roll(t.astype(jnp.float32), (LANES - shift) % LANES, 1) for t in tiles]
+    turned = [pltpu.roll(t.astype(jnp.float32), (LANES - shift) & (LANES - 1), 1) for t in tiles]
     return jnp.where(lane < LANES - shift, turned[0], turned[1]).astype(jnp.bfloat16)
 
 
@@ -275,6 +277,7 @@
     aux = halves[0].shape[0]
     occupied = table_ref.shape[1]
     per = LANES // occupied
+    per_bits = per.bit_length() - 1
     lane = lax.broadcasted_iota(jnp.int32, (occupied, LANES), 1)
     column = lane % PAD
     wide_lane = lax.broadcasted_iota(jnp.int32, (aux, LANES), 1)
@@ -299,16 +302,16 @@
             def _():
                 for s in range(group):
                     mu, nu = meta_ref[k, at + s], meta_ref[k, capacity + at + s]
-                    mu_start, mu_length = mu // CODE, mu % CODE
-                    nu_length = nu % CODE
-                    nu_start = jnp.maximum(nu // CODE - base * slab, 0)
-                    left = window(halves[n], nu_start // per, nu_start % per * occupied, wide_lane)
-                    tile, shift = mu_start // (LANES // PAD), mu_start % (LANES // PAD) * PAD
-                    x = [pltpu.roll(table_ref[tile + q], (LANES - shift) % LANES, 1) for q in range(3)]
+                    mu_wide, nu_length = (mu & (CODE - 1)) * PAD, nu & (CODE - 1)
+                    nu_tile, nu_shift = nu >> (CODE_BITS + per_bits), (nu >> CODE_BITS) & (per - 1)
+                    left = window(halves[n], nu_tile, nu_shift * occupied, wide_lane)
+                    tile, shift = mu >> (CODE_BITS + 3), ((mu >> CODE_BITS) & 7) * PAD
+                    back = (LANES - shift) & (LANES - 1)
+                    x = [pltpu.roll(table_ref[tile + q], back, 1) for q in range(3)]
                     keep = lane < LANES - shift
                     coeff = []
                     for q in range(2):
-                        valid = (column < nu_length) & (lane + q * LANES < mu_length * PAD)
+                        valid = (column < nu_length) & (lane + q * LANES < mu_wide)
                         coeff.append(jnp.where(valid, jnp.where(keep, x[q], x[q + 1]), 0.0))
                     right = [
                         jnp.concatenate([jnp.where(column == m, c, 0.0) for m in range(PAD)], axis=0) for c in coeff
@@ -387,6 +390,7 @@
         [density, occ_coeffs, mu_shell.reshape(1, pairs), nu_shell.reshape(1, pairs), owner.reshape(1, pairs)],
         scratch=[pltpu.VMEM((3, 1, pairs), jnp.int32), pltpu.SemaphoreType.DMA((5,))],
         specs=[HBM] * 5,
+        limit=60,
     )
 
     span = occupied * LANES
@@ -405,20 +409,21 @@
     half, parts = make_half(position, packed, vir_coeffs, spread, aux)
     state = {}
 
-    def tables(halves):
-        state["meta"], state["table"] = make_tables(
-            position, parts, shell_table, repeat, pairs, capacity, shells, slab, aux
-        )
-        return state["meta"]
-
     def blocks_of(ks, halves):
         state["done"] = make_blocks(
             ks, count, capacity, slab, state["meta"], halves, state["table"], state.get("done")
         )
+
+    def first_blocks(halves):
+        state["meta"], state["table"] = make_tables(
+            position, parts, shell_table, repeat, pairs, capacity, shells, slab, aux
+        )
+        blocks_of([0, 1, 2], halves)
         return state["done"][1]
 
-    halves = gather(half, count, tables, lambda halves: blocks_of([0, 1, 2], halves))
-    blocks_of([4, *range(6, count, 2), 3], halves)
+    halves, sums = gather(half, count, "half", first_blocks)
+    state["done"] = (state["done"][0], sums)
+    blocks_of([3, *range(4, count, 2)], halves)
     for k in range(5, count, 2):
         blocks_of([k], halves)
     blocks, sums = state["done"]

time: 107 us -> 85.1 us (0.80); the launches traced: 108 us -> 84.6 us
  Pallas kernels: 38.1 us -> 25.1 us
  waiting for transfers between devices: 34.6 us -> 27.8 us
  local copies, waits for them, and re-layouts: 6.68 us -> 3.98 us
    pallas_call x4, Pallas kernels: 30.3 us -> 16.5 us  [make_blocks(): pl.pallas_call(functools.partial(block_kernel, ks, bool(carried), group,...]
    ppermute x17, waiting for transfers between devices: 34.6 us -> 27.8 us  [swap(): return lax.ppermute(x, axis, [(i, i ^ k) for i in range(count)])]
    unnamed x16 -> x10, local copies, waits for them, and re-layouts: 5.87 us -> 3.16 us
  transfers between devices with their start and end apart: 17 -> 17, of which waited for: 8 -> 10; matrix products, arithmetic and copies ran while one was open for 2% -> 2% of each run, Pallas kernels for 30% -> 23%
where the time goes in v2:
time: 85.1 us; the launch traced here: 84.6 us
  waiting for transfers between devices  27.8 us (33%)
  starting transfers between devices  25.4 us (30%)
  Pallas kernels  25.1 us (29%)
  local copies, waits for them, and re-layouts  3.98 us (5%)
  other arithmetic  1.49 us (2%)
    ppermute x17, waiting for transfers between devices, swap(): return lax.ppermute(x, axis, [(i, i ^ k) for i in range(count)])  27.8 us
    ppermute x17, starting transfers between devices, swap(): return lax.ppermute(x, axis, [(i, i ^ k) for i in range(count)])  25.4 us
    pallas_call x4, Pallas kernels, make_blocks(): pl.pallas_call(functools.partial(block_kernel, ks, bool(carried), group,...  16.5 us
    pallas_call x4, Pallas kernels, whole(): pl.pallas_call(body, out_shape=out_shape, grid_spec=pltpu.PrefetchScalarG...  4.93 us
    pallas_call x1, Pallas kernels, make_tables(): pl.pallas_call(functools.partial(table_kernel, count, pairs, capacity, sh...  3.67 us
    unnamed x10, local copies, waits for them, and re-layouts  3.16 us
  transfers between devices with their start and end apart: 17, of which 10 were waited for; matrix products, arithmetic and copies ran while one was open for 2% of the time, Pallas kernels for 23%

profile of v2, /device:TPU:0, one launch (start us, length us, event | category | flops | bytes accessed | tf_op | source)
XLA Modules:
  0.0 84.6 jit_solution(6220400865837419652)
XLA Ops:
  0.6 1.7 %shard_map.86.refs_0_ = bf16[34,8,512]{2,1,0:T(8,128)(2,1)} custom-call(bf16[32,8,512]{2,1,0:T(8,128)(2,1)} %density_ref.1, bf16[8,512]{1,0:T(8,128)(2,1)} %occ_ref.1, s32[1,256]{1,0:T(1,128)} %bitcast.4, s32[1,256]{1,0:T(1,128)} %bitcast.5, s32[1,256]{1,0:T(1,128)} %bitcast.6), custom_call_target="tpu_custom_call" | custom-call | tf_op jit(solution)/shard_map/pallas_call | solution.py:61
  2.3 3.0 %collective-permute-start = (bf16[34,8,512]{2,1,0:T(8,128)(2,1)}, bf16[34,8,512]{2,1,0:T(8,128)(2,1)S(1)}, u32[]{:S(2)}, u32[]{:S(2)}) collective-permute-start(bf16[34,8,512]{2,1,0:T(8,128)(2,1)} %shard_map.86.refs_0_), channel_id=1, source_target_pairs={{0,4},{4,0},{8,12},{12,8},{16,20},{20,16},{24,28},{28,24},{1,5},{5... | collective-permute-start | bytes 835592 | tf_op jit(solution)/shard_map/density_1/ppermute | solution.py:23
  5.4 1.6 %collective-permute-start.1 = (bf16[34,8,512]{2,1,0:T(8,128)(2,1)}, bf16[34,8,512]{2,1,0:T(8,128)(2,1)S(1)}, u32[]{:S(2)}, u32[]{:S(2)}) collective-permute-start(bf16[34,8,512]{2,1,0:T(8,128)(2,1)} %shard_map.86.refs_0_), channel_id=1, source_target_pairs={{0,8},{4,12},{8,0},{12,4},{16,24},{20,28},{24,16},{28,20},{1,9},{5... | collective-permute-start | bytes 835592 | tf_op jit(solution)/shard_map/density_2/ppermute | solution.py:23
  7.0 2.6 %collective-permute-start.2 = (bf16[34,8,512]{2,1,0:T(8,128)(2,1)}, bf16[34,8,512]{2,1,0:T(8,128)(2,1)S(1)}, u32[]{:S(2)}, u32[]{:S(2)}) collective-permute-start(bf16[34,8,512]{2,1,0:T(8,128)(2,1)} %shard_map.86.refs_0_), channel_id=1, source_target_pairs={{0,16},{4,20},{8,24},{12,28},{16,0},{20,4},{24,8},{28,12},{1,17},{... | collective-permute-start | bytes 835592 | tf_op jit(solution)/shard_map/density_4/ppermute | solution.py:23
  9.5 0.1 fusion.1.refs_9_
  9.7 2.6 %collective-permute-done.refs_1_ = bf16[34,8,512]{2,1,0:T(8,128)(2,1)S(1)} collective-permute-done((bf16[34,8,512]{2,1,0:T(8,128)(2,1)}, bf16[34,8,512]{2,1,0:T(8,128)(2,1)S(1)}, u32[]{:S(2)}, u32[]{:S(2)}) %collective-permute-start) | collective-permute-done | bytes 278560 | tf_op jit(solution)/shard_map/density_1/ppermute | solution.py:23
  12.2 3.8 %collective-permute-start.5 = (bf16[34,8,512]{2,1,0:T(8,128)(2,1)}, bf16[34,8,512]{2,1,0:T(8,128)(2,1)S(1)}, u32[]{:S(2)}, u32[]{:S(2)}) collective-permute-start(bf16[34,8,512]{2,1,0:T(8,128)(2,1)} %shard_map.86.refs_0_), channel_id=1, source_target_pairs={{0,24},{4,28},{8,16},{12,20},{16,8},{20,12},{24,0},{28,4},{1,25},{... | collective-permute-start | bytes 835592 | tf_op jit(solution)/shard_map/density_6/ppermute | solution.py:23
  16.1 3.0 %collective-permute-done.1.refs_2_ = bf16[34,8,512]{2,1,0:T(8,128)(2,1)S(1)} collective-permute-done((bf16[34,8,512]{2,1,0:T(8,128)(2,1)}, bf16[34,8,512]{2,1,0:T(8,128)(2,1)S(1)}, u32[]{:S(2)}, u32[]{:S(2)}) %collective-permute-start.1) | collective-permute-done | bytes 278560 | tf_op jit(solution)/shard_map/density_2/ppermute | solution.py:23
  19.0 0.6 collective-permute-start.3
  19.7 0.8 select_reduce_fusion
  20.5 5.7 %collective-permute-done.3.refs_3_ = bf16[34,8,512]{2,1,0:T(8,128)(2,1)S(1)} collective-permute-done((bf16[34,8,512]{2,1,0:T(8,128)(2,1)S(1)}, bf16[34,8,512]{2,1,0:T(8,128)(2,1)S(1)}, u32[]{:S(2)}, u32[]{:S(2)}) %collective-permute-start.3) | collective-permute-done | bytes 278560 | tf_op jit(solution)/shard_map/density_3/ppermute | solution.py:23
  26.2 0.0 copy-start
  26.2 2.2 %copy-done = bf16[512,4096]{1,0:T(8,128)(2,1)S(1)} copy-done((bf16[512,4096]{1,0:T(8,128)(2,1)S(1)}, bf16[512,4096]{1,0:T(8,128)(2,1)}, u32[]{:S(2)}) %copy-start) | copy-done | bytes 4194328
  28.4 0.0 copy-start.2
  28.4 1.0 %copy-done.2 = bf16[34,8,512]{2,1,0:T(8,128)(2,1)S(1)} copy-done((bf16[34,8,512]{2,1,0:T(8,128)(2,1)S(1)}, bf16[34,8,512]{2,1,0:T(8,128)(2,1)}, u32[]{:S(2)}) %copy-start.2) | copy-done | bytes 278552
  29.4 0.0 copy-start.1
  29.4 1.3 %shard_map.87.refs_3_ = f32[256,512]{1,0:T(8,128)S(1)} custom-call(s32[1]{0:T(128)} %bitcast.where_ref, bf16[512,4096]{1,0:T(8,128)(2,1)S(1)} %copy-done, bf16[34,8,512]{2,1,0:T(8,128)(2,1)S(1)} %copy-done.2, bf16[34,8,512]{2,1,0:T(8,128)(2,1)S(1)} %collective-permute-done.refs_1_, bf16[34,8,512]{2,1,0:T(8,128)(2,1)S(1)} %collective-permute-done.1.refs_2_, ...), custom_call_target="tpu_custom_call" | custom-call | bytes 8388608 | tf_op jit(solution)/shard_map/pallas_call | solution.py:61
  30.7 0.0 collective-permute-done.2.refs_4_.refs_0_
  30.7 1.0 %collective-permute-start.4 = (bf16[34,8,512]{2,1,0:T(8,128)(2,1)S(1)}, bf16[34,8,512]{2,1,0:T(8,128)(2,1)S(1)}, u32[]{:S(2)}, u32[]{:S(2)}) collective-permute-start(bf16[34,8,512]{2,1,0:T(8,128)(2,1)S(1)} %collective-permute-done.2.refs_4_.refs_0_), channel_id=1, source_target_pairs={{0,4},{4,0},{8,12},{12,8},{16,20},{20,16},{24,28},{28,24},{1,5},{5... | collective-permute-start | bytes 835592 | tf_op jit(solution)/shard_map/density_5/ppermute | solution.py:23
  31.7 0.0 collective-permute-done.5.refs_6_.refs_1_
  31.7 1.1 %collective-permute-start.6 = (bf16[34,8,512]{2,1,0:T(8,128)(2,1)S(1)}, bf16[34,8,512]{2,1,0:T(8,128)(2,1)S(1)}, u32[]{:S(2)}, u32[]{:S(2)}) collective-permute-start(bf16[34,8,512]{2,1,0:T(8,128)(2,1)S(1)} %collective-permute-done.5.refs_6_.refs_1_), channel_id=1, source_target_pairs={{0,4},{4,0},{8,12},{12,8},{16,20},{20,16},{24,28},{28,24},{1,5},{5... | collective-permute-start | bytes 835592 | tf_op jit(solution)/shard_map/density_7/ppermute | solution.py:23
  32.8 0.4 fusion.spread_ref
  33.2 0.0 copy-start.4
  33.2 0.0 copy-start.3
  33.3 6.8 %collective-permute-done.4.refs_5_.refs_2_ = bf16[34,8,512]{2,1,0:T(8,128)(2,1)S(1)} collective-permute-done((bf16[34,8,512]{2,1,0:T(8,128)(2,1)S(1)}, bf16[34,8,512]{2,1,0:T(8,128)(2,1)S(1)}, u32[]{:S(2)}, u32[]{:S(2)}) %collective-permute-start.4) | collective-permute-done | bytes 278560 | tf_op jit(solution)/shard_map/density_5/ppermute | solution.py:23
  40.1 0.0 copy-done.1
  40.1 1.2 %shard_map.89 = (f32[256,512]{1,0:T(8,128)S(1)}, bf16[512,512]{1,0:T(8,128)(2,1)S(1)}) custom-call(s32[1]{0:T(128)} %bitcast.where_ref, bf16[512,4096]{1,0:T(8,128)(2,1)S(1)} %copy-done.1, bf16[34,8,512]{2,1,0:T(8,128)(2,1)S(1)} %collective-permute-done.2.refs_4_.refs_0_, bf16[34,8,512]{2,1,0:T(8,128)(2,1)S(1)} %collective-permute-done.5.refs_6_.refs_1_, ...), custom_call_target="tpu_custom_call" | custom-call | bytes 6291456 | tf_op jit(solution)/shard_map/pallas_call | solution.py:61
  41.2 1.8 %collective-permute-done.6.refs_7_.part_ref = bf16[34,8,512]{2,1,0:T(8,128)(2,1)S(1)} collective-permute-done((bf16[34,8,512]{2,1,0:T(8,128)(2,1)S(1)}, bf16[34,8,512]{2,1,0:T(8,128)(2,1)S(1)}, u32[]{:S(2)}, u32[]{:S(2)}) %collective-permute-start.6) | collective-permute-done | bytes 278560 | tf_op jit(solution)/shard_map/density_7/ppermute | solution.py:23
  43.0 0.8 shard_map.90.refs_0_
  43.8 1.3 %collective-permute-start.7 = (bf16[32,4096]{1,0:T(8,128)(2,1)S(1)}, bf16[32,4096]{1,0:T(8,128)(2,1)S(1)}, u32[]{:S(2)}, u32[]{:S(2)}) collective-permute-start(bf16[32,4096]{1,0:T(8,128)(2,1)S(1)} %shard_map.90.refs_0_), channel_id=1, source_target_pairs={{0,4},{4,0},{8,12},{12,8},{16,20},{20,16},{24,28},{28,24},{1,5},{5... | collective-permute-start | bytes 786440 | tf_op jit(solution)/shard_map/half_1/ppermute | solution.py:23
  45.1 0.0 collective-permute-start.11
  45.1 0.1 broadcast_add_fusion
  45.2 0.0 copy-done.4
  45.2 0.1 add.95
  45.3 0.1 stack_reshape.4
  45.4 3.0 %collective-permute-start.10 = (bf16[32,4096]{1,0:T(8,128)(2,1)S(1)}, bf16[32,4096]{1,0:T(8,128)(2,1)S(1)}, u32[]{:S(2)}, u32[]{:S(2)}) collective-permute-start(bf16[32,4096]{1,0:T(8,128)(2,1)S(1)} %shard_map.90.refs_0_), channel_id=1, source_target_pairs={{0,16},{4,20},{8,24},{12,28},{16,0},{20,4},{24,8},{28,12},{1,17},{... | collective-permute-start | bytes 786440 | tf_op jit(solution)/shard_map/half_4/ppermute | solution.py:23
  48.4 1.8 %collective-permute-done.7.refs_1_ = bf16[32,4096]{1,0:T(8,128)(2,1)S(1)} collective-permute-done((bf16[32,4096]{1,0:T(8,128)(2,1)S(1)}, bf16[32,4096]{1,0:T(8,128)(2,1)S(1)}, u32[]{:S(2)}, u32[]{:S(2)}) %collective-permute-start.7) | collective-permute-done | bytes 262176 | tf_op jit(solution)/shard_map/half_1/ppermute | solution.py:23
  50.2 3.1 %collective-permute-start.8 = (bf16[32,4096]{1,0:T(8,128)(2,1)S(1)}, bf16[32,4096]{1,0:T(8,128)(2,1)S(1)}, u32[]{:S(2)}, u32[]{:S(2)}) collective-permute-start(bf16[32,4096]{1,0:T(8,128)(2,1)S(1)} %shard_map.90.refs_0_), channel_id=1, source_target_pairs={{0,24},{4,28},{8,16},{12,20},{16,8},{20,12},{24,0},{28,4},{1,25},{... | collective-permute-start | bytes 786440 | tf_op jit(solution)/shard_map/half_6/ppermute | solution.py:23
  53.4 0.6 collective-permute-done.11.refs_2_
  54.0 0.2 collective-permute-start.12
  54.2 0.0 copy-done.3
  54.2 3.7 %shard_map.88 = (s32[24,128]{1,0:T(8,128)S(1)}, f32[514,8,128]{2,1,0:T(8,128)S(1)}) custom-call(s32[1]{0:T(128)} %bitcast.where_ref, bf16[34,8,512]{2,1,0:T(8,128)(2,1)S(1)} %copy-done.3, bf16[34,8,512]{2,1,0:T(8,128)(2,1)S(1)} %collective-permute-done.refs_1_, bf16[34,8,512]{2,1,0:T(8,128)(2,1)S(1)} %collective-permute-done.1.refs_2_, ...), custom_call_target="tpu_custom_call" | custom-call | bytes 16777216 | tf_op jit(solution)/shard_map/pallas_call | solution.py:245
  57.9 5.6 %shard_map.91 = (bf16[512,32,256]{2,1,0:T(8,128)(2,1)}, f32[8,64]{1,0:T(8,128)S(1)}) custom-call(s32[24,128]{1,0:T(8,128)S(1)} %get-tuple-element.28.meta_ref, f32[514,8,128]{2,1,0:T(8,128)S(1)} %get-tuple-element.29.table_ref, bf16[32,4096]{1,0:T(8,128)(2,1)S(1)} %shard_map.90.refs_0_, bf16[32,4096]{1,0:T(8,128)(2,1)S(1)} %collective-permute-done.7.refs_1_, ...), custom_call_target="tpu_custom_call" | custom-call | bytes 18874368 | tf_op jit(solution)/shard_map/pallas_call | solution.py:353
  63.5 2.7 %collective-permute-done.10.refs_1_ = bf16[32,4096]{1,0:T(8,128)(2,1)S(1)} collective-permute-done((bf16[32,4096]{1,0:T(8,128)(2,1)S(1)}, bf16[32,4096]{1,0:T(8,128)(2,1)S(1)}, u32[]{:S(2)}, u32[]{:S(2)}) %collective-permute-start.10) | collective-permute-done | bytes 262176 | tf_op jit(solution)/shard_map/half_4/ppermute | solution.py:23
  66.3 0.0 collective-permute-done.12.refs_0_
  66.3 0.7 collective-permute-start.13
  67.0 0.0 collective-permute-done.8.refs_2_
  67.0 1.3 %collective-permute-start.9 = (bf16[32,4096]{1,0:T(8,128)(2,1)S(1)}, bf16[32,4096]{1,0:T(8,128)(2,1)S(1)}, u32[]{:S(2)}, u32[]{:S(2)}) collective-permute-start(bf16[32,4096]{1,0:T(8,128)(2,1)S(1)} %collective-permute-done.8.refs_2_), channel_id=1, source_target_pairs={{0,4},{4,0},{8,12},{12,8},{16,20},{20,16},{24,28},{28,24},{1,5},{5... | collective-permute-start | bytes 786440 | tf_op jit(solution)/shard_map/half_7/ppermute | solution.py:23
  68.3 5.1 %shard_map.92 = (bf16[512,32,256]{2,1,0:T(8,128)(2,1)}, f32[8,64]{1,0:T(8,128)S(1)}) custom-call(s32[24,128]{1,0:T(8,128)S(1)} %get-tuple-element.28.meta_ref, f32[514,8,128]{2,1,0:T(8,128)S(1)} %get-tuple-element.29.table_ref, bf16[32,4096]{1,0:T(8,128)(2,1)S(1)} %collective-permute-done.12.refs_0_, ...), custom_call_target="tpu_custom_call", output_to_operand_aliasing={{0}: (5, {})} | custom-call | bytes 18874368 | tf_op jit(solution)/shard_map/pallas_call | solution.py:353
  73.5 0.0 collective-permute-done.13.refs_0_
  73.5 2.9 %shard_map.93 = (bf16[512,32,256]{2,1,0:T(8,128)(2,1)}, f32[8,64]{1,0:T(8,128)S(1)}) custom-call(s32[24,128]{1,0:T(8,128)S(1)} %get-tuple-element.28.meta_ref, f32[514,8,128]{2,1,0:T(8,128)S(1)} %get-tuple-element.29.table_ref, bf16[32,4096]{1,0:T(8,128)(2,1)S(1)} %collective-permute-done.13.refs_0_, ...), custom_call_target="tpu_custom_call", output_to_operand_aliasing={{0}: (3, {})} | custom-call | bytes 6291456 | tf_op jit(solution)/shard_map/pallas_call | solution.py:353
  76.3 0.0 collective-permute-done.9.refs_0_
  76.3 2.9 %shard_map.94 = (bf16[512,32,256]{2,1,0:T(8,128)(2,1)}, f32[8,64]{1,0:T(8,128)S(1)}) custom-call(s32[24,128]{1,0:T(8,128)S(1)} %get-tuple-element.28.meta_ref, f32[514,8,128]{2,1,0:T(8,128)S(1)} %get-tuple-element.29.table_ref, bf16[32,4096]{1,0:T(8,128)(2,1)S(1)} %collective-permute-done.9.refs_0_, ...), custom_call_target="tpu_custom_call", output_to_operand_aliasing={{0}: (3, {})} | custom-call | bytes 6291456 | tf_op jit(solution)/shard_map/pallas_call | solution.py:353
  79.2 0.1 collective-permute-start.14
  79.3 1.6 %collective-permute-start.15 = (f32[8,64]{1,0:T(8,128)S(1)}, f32[8,64]{1,0:T(8,128)S(1)}, u32[]{:S(2)}, u32[]{:S(2)}) collective-permute-start(f32[8,64]{1,0:T(8,128)S(1)} %get-tuple-element.45), channel_id=1, source_target_pairs={{0,2},{1,3},{2,0},{3,1},{4,6},{5,7},{6,4},{7,5},{8,10},{9,11},{10,... | collective-permute-start | bytes 6152 | tf_op jit(solution)/shard_map/ppermute | solution.py:23
  80.8 0.3 collective-permute-start.16
  81.2 0.0 collective-permute-done.14
  81.2 1.8 %collective-permute-done.15 = f32[8,64]{1,0:T(8,128)S(1)} collective-permute-done((f32[8,64]{1,0:T(8,128)S(1)}, f32[8,64]{1,0:T(8,128)S(1)}, u32[]{:S(2)}, u32[]{:S(2)}) %collective-permute-start.15) | collective-permute-done | bytes 2080 | tf_op jit(solution)/shard_map/ppermute | solution.py:23
  83.0 0.9 %collective-permute-done.16 = f32[8,64]{1,0:T(8,128)S(1)} collective-permute-done((f32[8,64]{1,0:T(8,128)S(1)}, f32[8,64]{1,0:T(8,128)S(1)}, u32[]{:S(2)}, u32[]{:S(2)}) %collective-permute-start.16) | collective-permute-done | bytes 2080 | tf_op jit(solution)/shard_map/ppermute | solution.py:23
  83.9 0.7 sqrt.7
  (9 shorter events, 0.1 us)
Async XLA Ops:
  2.3 9.9 %collective-permute-start = (bf16[34,8,512]{2,1,0:T(8,128)(2,1)}, bf16[34,8,512]{2,1,0:T(8,128)(2,1)S(1)}, u32[]{:S(2)}, u32[]{:S(2)}) collective-permute-start(bf16[34,8,512]{2,1,0:T(8,128)(2,1)} %shard_map.86.refs_0_), channel_id=1, source_target_pairs={{0,4},{4,0},{8,12},{12,8},{16,20},{20,16},{24,28},{28,24},{1,5},{5... | collective-permute-start | bytes 835592 | tf_op jit(solution)/shard_map/density_1/ppermute | solution.py:23
  5.4 13.7 %collective-permute-start.1 = (bf16[34,8,512]{2,1,0:T(8,128)(2,1)}, bf16[34,8,512]{2,1,0:T(8,128)(2,1)S(1)}, u32[]{:S(2)}, u32[]{:S(2)}) collective-permute-start(bf16[34,8,512]{2,1,0:T(8,128)(2,1)} %shard_map.86.refs_0_), channel_id=1, source_target_pairs={{0,8},{4,12},{8,0},{12,4},{16,24},{20,28},{24,16},{28,20},{1,9},{5... | collective-permute-start | bytes 835592 | tf_op jit(solution)/shard_map/density_2/ppermute | solution.py:23
  7.0 23.8 %collective-permute-start.2 = (bf16[34,8,512]{2,1,0:T(8,128)(2,1)}, bf16[34,8,512]{2,1,0:T(8,128)(2,1)S(1)}, u32[]{:S(2)}, u32[]{:S(2)}) collective-permute-start(bf16[34,8,512]{2,1,0:T(8,128)(2,1)} %shard_map.86.refs_0_), channel_id=1, source_target_pairs={{0,16},{4,20},{8,24},{12,28},{16,0},{20,4},{24,8},{28,12},{1,17},{... | collective-permute-start | bytes 835592 | tf_op jit(solution)/shard_map/density_4/ppermute | solution.py:23
  12.2 19.5 %collective-permute-start.5 = (bf16[34,8,512]{2,1,0:T(8,128)(2,1)}, bf16[34,8,512]{2,1,0:T(8,128)(2,1)S(1)}, u32[]{:S(2)}, u32[]{:S(2)}) collective-permute-start(bf16[34,8,512]{2,1,0:T(8,128)(2,1)} %shard_map.86.refs_0_), channel_id=1, source_target_pairs={{0,24},{4,28},{8,16},{12,20},{16,8},{20,12},{24,0},{28,4},{1,25},{... | collective-permute-start | bytes 835592 | tf_op jit(solution)/shard_map/density_6/ppermute | solution.py:23
  19.0 7.2 %collective-permute-start.3 = (bf16[34,8,512]{2,1,0:T(8,128)(2,1)S(1)}, bf16[34,8,512]{2,1,0:T(8,128)(2,1)S(1)}, u32[]{:S(2)}, u32[]{:S(2)}) collective-permute-start(bf16[34,8,512]{2,1,0:T(8,128)(2,1)S(1)} %collective-permute-done.1.refs_2_), channel_id=1, source_target_pairs={{0,4},{4,0},{8,12},{12,8},{16,20},{20,16},{24,28},{28,24},{1,5},{5... | collective-permute-start | bytes 835592 | tf_op jit(solution)/shard_map/density_3/ppermute | solution.py:23
  26.2 2.2 %copy-start = (bf16[512,4096]{1,0:T(8,128)(2,1)S(1)}, bf16[512,4096]{1,0:T(8,128)(2,1)}, u32[]{:S(2)}) copy-start(bf16[512,4096]{1,0:T(8,128)(2,1)} %vir_ref.3) | copy-start | bytes 12582916
  28.4 1.0 %copy-start.2 = (bf16[34,8,512]{2,1,0:T(8,128)(2,1)S(1)}, bf16[34,8,512]{2,1,0:T(8,128)(2,1)}, u32[]{:S(2)}) copy-start(bf16[34,8,512]{2,1,0:T(8,128)(2,1)} %shard_map.86.refs_0_) | copy-start | bytes 835588
  29.4 10.7 %copy-start.1 = (bf16[512,4096]{1,0:T(8,128)(2,1)S(1)}, bf16[512,4096]{1,0:T(8,128)(2,1)}, u32[]{:S(2)}) copy-start(bf16[512,4096]{1,0:T(8,128)(2,1)} %vir_ref.3) | copy-start | bytes 12582916
  30.7 9.3 %collective-permute-start.4 = (bf16[34,8,512]{2,1,0:T(8,128)(2,1)S(1)}, bf16[34,8,512]{2,1,0:T(8,128)(2,1)S(1)}, u32[]{:S(2)}, u32[]{:S(2)}) collective-permute-start(bf16[34,8,512]{2,1,0:T(8,128)(2,1)S(1)} %collective-permute-done.2.refs_4_.refs_0_), channel_id=1, source_target_pairs={{0,4},{4,0},{8,12},{12,8},{16,20},{20,16},{24,28},{28,24},{1,5},{5... | collective-permute-start | bytes 835592 | tf_op jit(solution)/shard_map/density_5/ppermute | solution.py:23
  31.7 11.3 %collective-permute-start.6 = (bf16[34,8,512]{2,1,0:T(8,128)(2,1)S(1)}, bf16[34,8,512]{2,1,0:T(8,128)(2,1)S(1)}, u32[]{:S(2)}, u32[]{:S(2)}) collective-permute-start(bf16[34,8,512]{2,1,0:T(8,128)(2,1)S(1)} %collective-permute-done.5.refs_6_.refs_1_), channel_id=1, source_target_pairs={{0,4},{4,0},{8,12},{12,8},{16,20},{20,16},{24,28},{28,24},{1,5},{5... | collective-permute-start | bytes 835592 | tf_op jit(solution)/shard_map/density_7/ppermute | solution.py:23
  33.2 12.0 %copy-start.4 = (s32[8,64]{1,0:T(8,128)S(1)}, s32[8,64]{1,0:T(8,128)}, u32[]{:S(2)}) copy-start(s32[8,64]{1,0:T(8,128)} %param.10) | copy-start | bytes 6148
  33.2 21.0 %copy-start.3 = (bf16[34,8,512]{2,1,0:T(8,128)(2,1)S(1)}, bf16[34,8,512]{2,1,0:T(8,128)(2,1)}, u32[]{:S(2)}) copy-start(bf16[34,8,512]{2,1,0:T(8,128)(2,1)} %shard_map.86.refs_0_) | copy-start | bytes 835588
  43.8 6.4 %collective-permute-start.7 = (bf16[32,4096]{1,0:T(8,128)(2,1)S(1)}, bf16[32,4096]{1,0:T(8,128)(2,1)S(1)}, u32[]{:S(2)}, u32[]{:S(2)}) collective-permute-start(bf16[32,4096]{1,0:T(8,128)(2,1)S(1)} %shard_map.90.refs_0_), channel_id=1, source_target_pairs={{0,4},{4,0},{8,12},{12,8},{16,20},{20,16},{24,28},{28,24},{1,5},{5... | collective-permute-start | bytes 786440 | tf_op jit(solution)/shard_map/half_1/ppermute | solution.py:23
  45.1 8.8 %collective-permute-start.11 = (bf16[32,4096]{1,0:T(8,128)(2,1)S(1)}, bf16[32,4096]{1,0:T(8,128)(2,1)S(1)}, u32[]{:S(2)}, u32[]{:S(2)}) collective-permute-start(bf16[32,4096]{1,0:T(8,128)(2,1)S(1)} %shard_map.90.refs_0_), channel_id=1, source_target_pairs={{0,8},{4,12},{8,0},{12,4},{16,24},{20,28},{24,16},{28,20},{1,9},{5... | collective-permute-start | bytes 786440 | tf_op jit(solution)/shard_map/half_2/ppermute | solution.py:23
  45.4 20.9 %collective-permute-start.10 = (bf16[32,4096]{1,0:T(8,128)(2,1)S(1)}, bf16[32,4096]{1,0:T(8,128)(2,1)S(1)}, u32[]{:S(2)}, u32[]{:S(2)}) collective-permute-start(bf16[32,4096]{1,0:T(8,128)(2,1)S(1)} %shard_map.90.refs_0_), channel_id=1, source_target_pairs={{0,16},{4,20},{8,24},{12,28},{16,0},{20,4},{24,8},{28,12},{1,17},{... | collective-permute-start | bytes 786440 | tf_op jit(solution)/shard_map/half_4/ppermute | solution.py:23
  50.2 16.8 %collective-permute-start.8 = (bf16[32,4096]{1,0:T(8,128)(2,1)S(1)}, bf16[32,4096]{1,0:T(8,128)(2,1)S(1)}, u32[]{:S(2)}, u32[]{:S(2)}) collective-permute-start(bf16[32,4096]{1,0:T(8,128)(2,1)S(1)} %shard_map.90.refs_0_), channel_id=1, source_target_pairs={{0,24},{4,28},{8,16},{12,20},{16,8},{20,12},{24,0},{28,4},{1,25},{... | collective-permute-start | bytes 786440 | tf_op jit(solution)/shard_map/half_6/ppermute | solution.py:23
  54.0 12.3 %collective-permute-start.12 = (bf16[32,4096]{1,0:T(8,128)(2,1)S(1)}, bf16[32,4096]{1,0:T(8,128)(2,1)S(1)}, u32[]{:S(2)}, u32[]{:S(2)}) collective-permute-start(bf16[32,4096]{1,0:T(8,128)(2,1)S(1)} %collective-permute-done.11.refs_2_), channel_id=1, source_target_pairs={{0,4},{4,0},{8,12},{12,8},{16,20},{20,16},{24,28},{28,24},{1,5},{5... | collective-permute-start | bytes 786440 | tf_op jit(solution)/shard_map/half_3/ppermute | solution.py:23
  66.3 7.2 %collective-permute-start.13 = (bf16[32,4096]{1,0:T(8,128)(2,1)S(1)}, bf16[32,4096]{1,0:T(8,128)(2,1)S(1)}, u32[]{:S(2)}, u32[]{:S(2)}) collective-permute-start(bf16[32,4096]{1,0:T(8,128)(2,1)S(1)} %collective-permute-done.10.refs_1_), channel_id=1, source_target_pairs={{0,4},{4,0},{8,12},{12,8},{16,20},{20,16},{24,28},{28,24},{1,5},{5... | collective-permute-start | bytes 786440 | tf_op jit(solution)/shard_map/half_5/ppermute | solution.py:23
  67.0 9.3 %collective-permute-start.9 = (bf16[32,4096]{1,0:T(8,128)(2,1)S(1)}, bf16[32,4096]{1,0:T(8,128)(2,1)S(1)}, u32[]{:S(2)}, u32[]{:S(2)}) collective-permute-start(bf16[32,4096]{1,0:T(8,128)(2,1)S(1)} %collective-permute-done.8.refs_2_), channel_id=1, source_target_pairs={{0,4},{4,0},{8,12},{12,8},{16,20},{20,16},{24,28},{28,24},{1,5},{5... | collective-permute-start | bytes 786440 | tf_op jit(solution)/shard_map/half_7/ppermute | solution.py:23
  79.2 1.9 %collective-permute-start.14 = (f32[8,64]{1,0:T(8,128)S(1)}, f32[8,64]{1,0:T(8,128)S(1)}, u32[]{:S(2)}, u32[]{:S(2)}) collective-permute-start(f32[8,64]{1,0:T(8,128)S(1)} %get-tuple-element.45), channel_id=1, source_target_pairs={{0,1},{1,0},{2,3},{3,2},{4,5},{5,4},{6,7},{7,6},{8,9},{9,8},{10,11... | collective-permute-start | bytes 6152 | tf_op jit(solution)/shard_map/ppermute | solution.py:23
  79.3 3.7 %collective-permute-start.15 = (f32[8,64]{1,0:T(8,128)S(1)}, f32[8,64]{1,0:T(8,128)S(1)}, u32[]{:S(2)}, u32[]{:S(2)}) collective-permute-start(f32[8,64]{1,0:T(8,128)S(1)} %get-tuple-element.45), channel_id=1, source_target_pairs={{0,2},{1,3},{2,0},{3,1},{4,6},{5,7},{6,4},{7,5},{8,10},{9,11},{10,... | collective-permute-start | bytes 6152 | tf_op jit(solution)/shard_map/ppermute | solution.py:23
  80.8 3.0 %collective-permute-start.16 = (f32[8,64]{1,0:T(8,128)S(1)}, f32[8,64]{1,0:T(8,128)S(1)}, u32[]{:S(2)}, u32[]{:S(2)}) collective-permute-start(f32[8,64]{1,0:T(8,128)S(1)} %get-tuple-element.45), channel_id=1, source_target_pairs={{0,3},{1,2},{2,1},{3,0},{4,7},{5,6},{6,5},{7,4},{8,11},{9,10},{10,... | collective-permute-start | bytes 6152 | tf_op jit(solution)/shard_map/ppermute | solution.py:23

commit v3 on v2

--- a/solution.py
+++ b/solution.py
@@ -42,7 +42,10 @@
     for k in range(6, count, 2):
         move(k, x, k)
     move(3, parts[2], 1)
-    parts[4], parts[3], result = tie(parts[4], parts[3], early(parts))
+    if early is None:
+        (parts[4], parts[3]), result = tie(parts[4], parts[3]), None
+    else:
+        parts[4], parts[3], result = tie(parts[4], parts[3], early(parts))
     for k in range(4, count, 2):
         move(k + 1, parts[k], 1)
     return [parts[k] for k in range(count)], result
@@ -76,24 +79,37 @@
 def pack_kernel(density_ref, occ_ref, mu_ref, nu_ref, owner_ref, out_ref, small_ref, sems):
     aux, occupied, width = density_ref.shape
     pairs = mu_ref.shape[1]
-    copies = [
-        pltpu.make_async_copy(density_ref, out_ref.at[pl.ds(0, aux)], sems.at[0]),
-        pltpu.make_async_copy(occ_ref, out_ref.at[aux], sems.at[1]),
-    ]
+    tiles = width // LANES
+    copies = []
     for n, ref in enumerate((mu_ref, nu_ref, owner_ref)):
-        copies.append(pltpu.make_async_copy(ref, small_ref.at[n], sems.at[2 + n]))
+        copies.append(pltpu.make_async_copy(ref, small_ref.at[n], sems.at[n]))
+    for t in range(tiles):
+        lanes = pl.ds(t * LANES, LANES)
+        copies.append(
+            pltpu.make_async_copy(density_ref.at[:, :, lanes], out_ref.at[pl.ds(t * aux, aux)], sems.at[3 + 2 * t])
+        )
+        copies.append(
+            pltpu.make_async_copy(occ_ref.at[:, lanes], out_ref.at[tiles * aux + t], sems.at[4 + 2 * t])
+        )
     for copy in copies:
         copy.start()
-    for copy in copies[2:]:
+    for copy in copies[:3]:
         copy.wait()
     mu = small_ref[0]
     digits = [mu // DIGIT, mu % DIGIT, small_ref[1], small_ref[2]]
-    per = width // pairs
-    rows = [jnp.concatenate(digits[n : n + per], axis=1) for n in range(0, 4, per)]
-    rows.append(jnp.zeros((occupied - len(rows), width), jnp.int32))
-    out_ref[aux + 1] = jnp.concatenate(rows, axis=0).astype(jnp.float32).astype(jnp.bfloat16)
-    for copy in copies[:2]:
+    per = pairs // LANES
+    rows = [d[:, q * LANES : (q + 1) * LANES] for d in digits for q in range(per)]
+    rows = jnp.concatenate(rows, axis=0).astype(jnp.float32).astype(jnp.bfloat16)
+    for t in range(rows.shape[0] // occupied):
+        out_ref[tiles * (aux + 1) + t] = rows[t * occupied : (t + 1) * occupied]
+    for copy in copies[3:]:
         copy.wait()
+
+
+def side_by_side(part_ref, aux, tiles):
+    occupied = part_ref.shape[1]
+    rows = [part_ref[t * aux : (t + 1) * aux].reshape(aux * occupied, LANES) for t in range(tiles)]
+    return jnp.concatenate(rows, axis=1)
 
 
 def part_kernel(ks, resumed, ahead, aux, where_ref, vir_ref, *refs):
@@ -103,7 +119,7 @@
     total_ref = refs.pop(0)
     ahead_ref = refs.pop(0) if ahead is not None else None
     columns_ref, sems = refs
-    _, occupied, width = blocks[0].shape
+    width = columns_ref.shape[2]
 
     def fetch(k, target, n):
         start = pl.multiple_of((where_ref[0] ^ k) * width, width)
@@ -117,7 +133,7 @@
     total = None if before_ref is None else before_ref[...]
     for n in range(len(ks)):
         copies[n].wait()
-        term = dot_t(blocks[n][:aux].reshape(aux * occupied, width), columns_ref[n])
+        term = dot_t(side_by_side(blocks[n], aux, width // LANES), columns_ref[n])
         total = term if total is None else total + term
     total_ref[...] = total
     if ahead is not None:
@@ -126,7 +142,7 @@
 
 def add_part(position, vir, parts, ks, before, ahead, aux):
     slab = vir.shape[0]
-    _, occupied, width = parts[0].shape
+    occupied, width = parts[0].shape[1], vir.shape[1] // len(parts)
     out = [jax.ShapeDtypeStruct((aux * occupied, slab), jnp.float32)]
     if ahead is not None:
         out.append(jax.ShapeDtypeStruct((slab, width), vir.dtype))
@@ -146,9 +162,9 @@
 
 
 def half_kernel(aux, before_ref, part_ref, column_ref, spread_ref, out_ref, total_ref):
-    _, occupied, width = part_ref.shape
+    occupied, width = part_ref.shape[1], column_ref.shape[1]
     tiles = total_ref.shape[0]
-    total = before_ref[...] + dot_t(part_ref[:aux].reshape(aux * occupied, width), column_ref[...])
+    total = before_ref[...] + dot_t(side_by_side(part_ref, aux, width // LANES), column_ref[...])
     for t in range(tiles):
         total_ref[t] = total[:, t * LANES : (t + 1) * LANES]
     columns = []
@@ -167,9 +183,8 @@
     occupied = packed.shape[1]
     order = [0, 1, 2, 3] + list(range(4, count, 2)) + list(range(5, count, 2))
     early, middle, last = order[:4], order[4:-1], order[-1]
-    parts, total = gather(
-        packed, count, "density", lambda parts: add_part(position, vir, parts, early, None, None, aux)[0]
-    )
+    parts, _ = gather(packed, count, "density", None)
+    [total] = add_part(position, vir, parts, early, None, None, aux)
     total, column = add_part(position, vir, parts, middle, total, last, aux)
     half = whole(
         functools.partial(half_kernel, aux),
@@ -181,26 +196,35 @@
     return half, parts
 
 
-def table_kernel(count, pairs, capacity, shells, slab, where_ref, *refs):
-    parts, (shell_ref, repeat_ref, meta_ref, table_ref, digit_ref) = refs[:count], refs[count:]
-    occupied, width = parts[0].shape[1:]
+def table_kernel(count, pairs, capacity, shells, slab, width, where_ref, *refs):
+    parts, (shell_ref, repeat_ref, meta_ref, table_ref, digit_ref, small_ref, sems) = refs[:count], refs[count:]
+    occupied = parts[0].shape[1]
     tiles = width // LANES
+    extra = small_ref.shape[1]
+    first_extra = parts[0].shape[0] - extra
+    copies = [
+        pltpu.make_async_copy(parts[k].at[pl.ds(first_extra, extra)], small_ref.at[k], sems.at[k]) for k in range(count)
+    ]
+    for copy in copies:
+        copy.start()
     for k in range(count):
+        copies[k].wait()
         first = (where_ref[0] ^ k) * (tiles * PAD)
-        occ = jnp.concatenate([parts[k][0, :, t * LANES : (t + 1) * LANES] for t in range(tiles)], axis=0)
-        wide = dot(occ, repeat_ref[...])
+        occ = jnp.concatenate([small_ref[k, t] for t in range(tiles)], axis=0)
+        spread = dot(occ, repeat_ref[...])
         for t in range(tiles):
             for q in range(PAD):
-                table_ref[first + t * PAD + q] = wide[
+                table_ref[first + t * PAD + q] = spread[
                     t * occupied : (t + 1) * occupied, q * LANES : (q + 1) * LANES
                 ]
-        digit_ref[k] = parts[k][1].astype(jnp.float32)
+        for t in range(extra - tiles):
+            digit_ref[k, t * occupied : (t + 1) * occupied] = small_ref[k, tiles + t].astype(jnp.float32)
     last = count * tiles * PAD
     table_ref[last] = jnp.zeros((occupied, LANES), jnp.float32)
     table_ref[last + 1] = jnp.zeros((occupied, LANES), jnp.float32)
     meta_ref[2 * count :, :] = jnp.full((meta_ref.shape[0] - 2 * count, LANES), where_ref[0], jnp.int32)
 
-    per = width // pairs
+    per = pairs // LANES
     total = shell_ref.shape[1]
     f32, bf16 = jnp.float32, jnp.bfloat16
     before = (
@@ -213,7 +237,7 @@
     def body(k, carry):
         source = (where_ref[0] ^ k).astype(f32)
         rows = digit_ref[k]
-        d = [rows[n // per : n // per + 1, n % per * pairs : (n % per + 1) * pairs] for n in range(4)]
+        d = [jnp.concatenate([rows[n * per + q : n * per + q + 1] for q in range(per)], axis=1) for n in range(4)]
         mu = d[0] * DIGIT + d[1]
         nu = d[2] + source * shells
         mine = jnp.where(d[3] == place, 1.0, 0.0)
@@ -239,25 +263,28 @@
     lax.fori_loop(0, count, body, 0)
 
 
-def make_tables(position, parts, shell_table, repeat, pairs, capacity, shells, slab, aux):
+def make_tables(position, parts, shell_table, repeat, pairs, capacity, shells, slab, width):
     count = len(parts)
-    _, occupied, width = parts[0].shape
-    return pl.pallas_call(
-        functools.partial(table_kernel, count, pairs, capacity, shells, slab),
-        out_shape=(
+    occupied = parts[0].shape[1]
+    tiles = width // LANES
+    digits = 4 * pairs // LANES
+    extra = tiles + digits // occupied
+    return whole(
+        functools.partial(table_kernel, count, pairs, capacity, shells, slab, width),
+        (
             jax.ShapeDtypeStruct((2 * count + 8, LANES), jnp.int32),
             jax.ShapeDtypeStruct((count * width // 8 + 2, occupied, LANES), jnp.float32),
         ),
-        grid_spec=pltpu.PrefetchScalarGridSpec(
-            num_scalar_prefetch=1,
-            grid=(1,),
-            in_specs=[pl.BlockSpec((2, occupied, width), lambda g, w: (aux // 2, 0, 0))] * count + [VMEM] * 2,
-            out_specs=(VMEM, VMEM),
-            scratch_shapes=[pltpu.VMEM((count, occupied, width), jnp.float32)],
-        ),
-        compiler_params=pltpu.CompilerParams(vmem_limit_bytes=44 * MIB),
-        cost_estimate=pl.CostEstimate(flops=0, transcendentals=0, bytes_accessed=16 * MIB),
-    )(position, *parts, shell_table, repeat)
+        [position, *parts, shell_table, repeat],
+        scratch=[
+            pltpu.VMEM((count, digits, LANES), jnp.float32),
+            pltpu.VMEM((count, extra, occupied, LANES), jnp.bfloat16),
+            pltpu.SemaphoreType.DMA((count,)),
+        ],
+        scalars=1,
+        specs=[HBM] * count + [VMEM] * 2,
+        cost=16 * MIB,
+    )
 
 
 def window(ref, tile, shift, lane):
@@ -267,13 +294,31 @@
     return jnp.where(lane < LANES - shift, turned[0], turned[1]).astype(jnp.bfloat16)
 
 
-def block_kernel(ks, resumed, group, count, capacity, slab, meta_ref, table_ref, *refs):
+def ship(ks, held_ref, out_ref, sems, place, capacity):
+    copies = []
+    for n, k in enumerate(ks):
+        target = out_ref.at[pl.ds((place ^ k) * capacity, capacity)]
+        copies.append(pltpu.make_async_copy(held_ref.at[n], target, sems.at[n]))
+    return copies
+
+
+def ship_kernel(ks, count, capacity, meta_ref, held_ref, _, out_ref, sems):
+    copies = ship(ks, held_ref, out_ref, sems, meta_ref[2 * count, 0], capacity)
+    for copy in copies:
+        copy.start()
+    for copy in copies:
+        copy.wait()
+
+
+def block_kernel(ks, old_ks, resumed, group, count, capacity, meta_ref, table_ref, *refs):
     refs = list(refs)
     halves = [refs.pop(0) for _ in ks]
-    old_sum_ref = refs.pop(1) if resumed else None
+    old_sum_ref, old_held_ref = (refs.pop(0), refs.pop(0)) if old_ks else (None, None)
     if resumed:
         refs.pop(0)
-    out_ref, sum_ref, buffer_ref, zero_ref, square_ref, sems = refs
+    held_ref, sum_ref = refs.pop(0), refs.pop(0)
+    out_ref = refs.pop(0) if old_ks else None
+    square_ref, sems = refs
     aux = halves[0].shape[0]
     occupied = table_ref.shape[1]
     per = LANES // occupied
@@ -282,20 +327,17 @@
     column = lane % PAD
     wide_lane = lax.broadcasted_iota(jnp.int32, (aux, LANES), 1)
     ones = jnp.ones((8, LANES), jnp.float32)
-    zero_ref[...] = jnp.zeros(zero_ref.shape, zero_ref.dtype)
-    sum_ref[...] = old_sum_ref[...] if resumed else jnp.zeros(sum_ref.shape, jnp.float32)
-    groups = capacity // group
+    place = meta_ref[2 * count, 0]
+    copies = ship(old_ks, old_held_ref, out_ref, sems, place, capacity) if old_ks else []
+    for copy in copies:
+        copy.start()
+    sum_ref[...] = old_sum_ref[...] if old_ks else jnp.zeros(sum_ref.shape, jnp.float32)
 
     for n, k in enumerate(ks):
-        base = meta_ref[2 * count, 0] ^ k
         live = meta_ref[count + k, 0]
 
-        def send(source, at, n=n, base=base):
-            target = out_ref.at[pl.ds(base * capacity + at, group)]
-            return pltpu.make_async_copy(source, target, sems.at[n * groups + at // group])
-
-        @pl.loop(0, groups)
-        def _(turn, n=n, k=k, base=base, live=live, send=send):
+        @pl.loop(0, capacity // group)
+        def _(turn, n=n, k=k, live=live):
             at = turn * group
 
             @pl.when(at < live)
@@ -318,16 +360,15 @@
                     ]
                     right = jnp.concatenate(right, axis=1).astype(jnp.bfloat16)
                     block = dot(left, right).astype(jnp.bfloat16)
-                    buffer_ref[n, at + s] = block
-                    wide = block.astype(jnp.float32)
-                    total = jnp.sum(wide * wide, axis=0, keepdims=True)
+                    held_ref[n, at + s] = block
+                    flat = block.astype(jnp.float32)
+                    total = jnp.sum(flat * flat, axis=0, keepdims=True)
                     square_ref[pl.ds(at + s, 1), :] = total[:, :LANES] + total[:, LANES:]
-                send(buffer_ref.at[n, pl.ds(at, group)], at).start()
 
             @pl.when(at >= live)
             def _():
                 square_ref[pl.ds(at, group), :] = jnp.zeros((group, LANES), jnp.float32)
-                send(zero_ref, at).start()
+                held_ref[n, pl.ds(at, group)] = jnp.zeros((group, aux, PAD * PAD), jnp.bfloat16)
 
         sums = lax.dot_general(
             ones,
@@ -336,42 +377,58 @@
             precision=lax.Precision.HIGHEST,
             preferred_element_type=jnp.float32,
         )
-        sum_ref[pl.ds(base, 1), :] = sums[:1]
-
-    for n, k in enumerate(ks):
-        base = meta_ref[2 * count, 0] ^ k
-        for turn in range(groups):
-            target = out_ref.at[pl.ds(base * capacity + turn * group, group)]
-            pltpu.make_async_copy(zero_ref, target, sems.at[n * groups + turn]).wait()
-
-
-def make_blocks(ks, count, capacity, slab, meta, halves, table, done):
+        sum_ref[pl.ds(place ^ k, 1), :] = sums[:1]
+
+    for copy in copies:
+        copy.wait()
+
+
+def make_blocks(ks, count, capacity, meta, halves, table, done):
     aux = halves[ks[0]].shape[0]
-    slots = count * capacity
-    group = min(GROUP, capacity)
-    carried = [] if done is None else list(done)
-    return pl.pallas_call(
-        functools.partial(block_kernel, ks, bool(carried), group, count, capacity, slab),
-        out_shape=(
-            jax.ShapeDtypeStruct((slots, aux, PAD * PAD), jnp.bfloat16),
-            jax.ShapeDtypeStruct((count, capacity), jnp.float32),
-        ),
+    old_ks, sums, held, out = done or ([], None, None, None)
+    carried = [] if not old_ks else [sums, held] + ([] if out is None else [out])
+    shapes = [
+        jax.ShapeDtypeStruct((len(ks), capacity, aux, PAD * PAD), jnp.bfloat16),
+        jax.ShapeDtypeStruct((count, capacity), jnp.float32),
+    ]
+    if old_ks:
+        shapes.append(jax.ShapeDtypeStruct((count * capacity, aux, PAD * PAD), jnp.bfloat16))
+    result = pl.pallas_call(
+        functools.partial(block_kernel, ks, old_ks, out is not None, min(GROUP, capacity), count, capacity),
+        out_shape=tuple(shapes),
         grid_spec=pltpu.PrefetchScalarGridSpec(
             num_scalar_prefetch=1,
             grid=(),
-            in_specs=[VMEM] * (1 + len(ks)) + ([HBM, VMEM] if carried else []),
-            out_specs=(HBM, VMEM),
+            in_specs=[VMEM] * (1 + len(ks) + min(len(carried), 2)) + [HBM] * (out is not None),
+            out_specs=(VMEM, VMEM, HBM)[: len(shapes)],
             scratch_shapes=[
-                pltpu.VMEM((len(ks), capacity, aux, PAD * PAD), jnp.bfloat16),
-                pltpu.VMEM((group, aux, PAD * PAD), jnp.bfloat16),
                 pltpu.VMEM((capacity, LANES), jnp.float32),
-                pltpu.SemaphoreType.DMA((len(ks) * capacity // group,)),
+                pltpu.SemaphoreType.DMA((max(len(old_ks), 1),)),
             ],
         ),
-        input_output_aliases={2 + len(ks): 0} if carried else {},
+        input_output_aliases={} if out is None else {4 + len(ks): 2},
         compiler_params=pltpu.CompilerParams(vmem_limit_bytes=24 * MIB),
         cost_estimate=pl.CostEstimate(flops=0, transcendentals=0, bytes_accessed=len(ks) * 6 * MIB),
     )(meta, table, *[halves[k] for k in ks], *carried)
+    return ks, result[1], result[0], result[2] if old_ks else None
+
+
+def make_output(count, capacity, meta, done):
+    ks, _, held, out = done
+    return pl.pallas_call(
+        functools.partial(ship_kernel, ks, count, capacity),
+        out_shape=jax.ShapeDtypeStruct(out.shape, out.dtype),
+        grid_spec=pltpu.PrefetchScalarGridSpec(
+            num_scalar_prefetch=1,
+            grid=(),
+            in_specs=[VMEM, HBM],
+            out_specs=HBM,
+            scratch_shapes=[pltpu.SemaphoreType.DMA((len(ks),))],
+        ),
+        input_output_aliases={2: 0},
+        compiler_params=pltpu.CompilerParams(vmem_limit_bytes=24 * MIB),
+        cost_estimate=pl.CostEstimate(flops=0, transcendentals=0, bytes_accessed=4 * MIB),
+    )(meta, held, out)
 
 
 def per_device(density, vir_coeffs, occ_coeffs, shell_len, mu_shell, nu_shell, owner):
@@ -384,11 +441,13 @@
     pairs = mu_shell.shape[0]
     capacity = 2 * pairs // count
 
+    tiles = width // LANES
+    rows = tiles * (aux + 1) + 4 * pairs // (LANES * occupied)
     packed = whole(
         pack_kernel,
-        jax.ShapeDtypeStruct((aux + 2, occupied, width), jnp.bfloat16),
+        jax.ShapeDtypeStruct((rows, occupied, LANES), jnp.bfloat16),
         [density, occ_coeffs, mu_shell.reshape(1, pairs), nu_shell.reshape(1, pairs), owner.reshape(1, pairs)],
-        scratch=[pltpu.VMEM((3, 1, pairs), jnp.int32), pltpu.SemaphoreType.DMA((5,))],
+        scratch=[pltpu.VMEM((3, 1, pairs), jnp.int32), pltpu.SemaphoreType.DMA((3 + 2 * tiles,))],
         specs=[HBM] * 5,
         limit=60,
     )
@@ -410,23 +469,23 @@
     state = {}
 
     def blocks_of(ks, halves):
-        state["done"] = make_blocks(
-            ks, count, capacity, slab, state["meta"], halves, state["table"], state.get("done")
-        )
+        state["done"] = make_blocks(ks, count, capacity, state["meta"], halves, state["table"], state.get("done"))
 
     def first_blocks(halves):
         state["meta"], state["table"] = make_tables(
-            position, parts, shell_table, repeat, pairs, capacity, shells, slab, aux
+            position, parts, shell_table, repeat, pairs, capacity, shells, slab, width
         )
         blocks_of([0, 1, 2], halves)
         return state["done"][1]
 
     halves, sums = gather(half, count, "half", first_blocks)
-    state["done"] = (state["done"][0], sums)
+    ks, _, held, out = state["done"]
+    state["done"] = (ks, sums, held, out)
     blocks_of([3, *range(4, count, 2)], halves)
     for k in range(5, count, 2):
         blocks_of([k], halves)
-    blocks, sums = state["done"]
+    sums = state["done"][1]
+    blocks = make_output(count, capacity, state["meta"], state["done"])
     sums = [sums] + [swap(sums, k, columns, "aux") for k in range(1, columns)]
     while len(sums) > 1:
         sums = [sums[n] + sums[n + 1] for n in range(0, len(sums), 2)]

time: 85.1 us -> 81.6 us (0.959)
  the two profiles are of different devices: /device:TPU:0 before, /device:TPU:17 now
where the time goes in v3:
time: 81.6 us; the launch traced here: 81.1 us
  waiting for transfers between devices  31.7 us (39%)
  Pallas kernels  25.2 us (31%)
  starting transfers between devices  17 us (21%)
  local copies, waits for them, and re-layouts  4.79 us (6%)
  other arithmetic  1.49 us (2%)
  between operations  0.88 us (1%)
    ppermute x17, waiting for transfers between devices, swap(): return lax.ppermute(x, axis, [(i, i ^ k) for i in range(count)])  31.7 us
    ppermute x17, starting transfers between devices, swap(): return lax.ppermute(x, axis, [(i, i ^ k) for i in range(count)])  17 us
    pallas_call x4, Pallas kernels, make_blocks(): pl.pallas_call(functools.partial(block_kernel, ks, old_ks, out is not Non...  13.6 us
    pallas_call x5, Pallas kernels, whole(): pl.pallas_call(body, out_shape=out_shape, grid_spec=pltpu.PrefetchScalarG...  9.93 us
    unnamed x10, local copies, waits for them, and re-layouts  3.97 us
    pallas_call x1, Pallas kernels, make_output(): pl.pallas_call(functools.partial(ship_kernel, ks, count, capacity), out_s...  1.71 us
  transfers between devices with their start and end apart: 17, of which 7 were waited for; matrix products, arithmetic and copies ran while one was open for 2% of the time, Pallas kernels for 26%

profile of v3, /device:TPU:17, one launch (start us, length us, event | category | flops | bytes accessed | tf_op | source)
XLA Modules:
  0.0 81.1 jit_solution(2287384086567315844)
XLA Ops:
  0.6 1.8 %shard_map.86.refs_0_ = bf16[133,8,128]{2,1,0:T(8,128)(2,1)} custom-call(bf16[32,8,512]{2,1,0:T(8,128)(2,1)} %density_ref.1, bf16[8,512]{1,0:T(8,128)(2,1)} %occ_ref.1, s32[1,256]{1,0:T(1,128)} %bitcast.4, s32[1,256]{1,0:T(1,128)} %bitcast.5, s32[1,256]{1,0:T(1,128)} %bitcast.6), custom_call_target="tpu_custom_call" | custom-call | tf_op jit(solution)/shard_map/pallas_call | solution.py:64
  2.5 0.1 collective-permute-start.2
  2.5 1.4 %collective-permute-start.1 = (bf16[133,8,128]{2,1,0:T(8,128)(2,1)}, bf16[133,8,128]{2,1,0:T(8,128)(2,1)S(1)}, u32[]{:S(2)}, u32[]{:S(2)}) collective-permute-start(bf16[133,8,128]{2,1,0:T(8,128)(2,1)} %shard_map.86.refs_0_), channel_id=1, source_target_pairs={{0,8},{4,12},{8,0},{12,4},{16,24},{20,28},{24,16},{28,20},{1,9},{5... | collective-permute-start | bytes 817160 | tf_op jit(solution)/shard_map/density_2/ppermute | solution.py:23
  3.9 1.2 %collective-permute-start = (bf16[133,8,128]{2,1,0:T(8,128)(2,1)}, bf16[133,8,128]{2,1,0:T(8,128)(2,1)S(1)}, u32[]{:S(2)}, u32[]{:S(2)}) collective-permute-start(bf16[133,8,128]{2,1,0:T(8,128)(2,1)} %shard_map.86.refs_0_), channel_id=1, source_target_pairs={{0,4},{4,0},{8,12},{12,8},{16,20},{20,16},{24,28},{28,24},{1,5},{5... | collective-permute-start | bytes 817160 | tf_op jit(solution)/shard_map/density_1/ppermute | solution.py:23
  5.1 0.1 fusion.1.refs_9_
  5.3 5.6 %collective-permute-done.refs_1_ = bf16[133,8,128]{2,1,0:T(8,128)(2,1)S(1)} collective-permute-done((bf16[133,8,128]{2,1,0:T(8,128)(2,1)}, bf16[133,8,128]{2,1,0:T(8,128)(2,1)S(1)}, u32[]{:S(2)}, u32[]{:S(2)}) %collective-permute-start) | collective-permute-done | bytes 272416 | tf_op jit(solution)/shard_map/density_1/ppermute | solution.py:23
  10.9 1.2 %collective-permute-start.5 = (bf16[133,8,128]{2,1,0:T(8,128)(2,1)}, bf16[133,8,128]{2,1,0:T(8,128)(2,1)S(1)}, u32[]{:S(2)}, u32[]{:S(2)}) collective-permute-start(bf16[133,8,128]{2,1,0:T(8,128)(2,1)} %shard_map.86.refs_0_), channel_id=1, source_target_pairs={{0,24},{4,28},{8,16},{12,20},{16,8},{20,12},{24,0},{28,4},{1,25},{... | collective-permute-start | bytes 817160 | tf_op jit(solution)/shard_map/density_6/ppermute | solution.py:23
  12.2 3.8 %collective-permute-done.1.refs_2_ = bf16[133,8,128]{2,1,0:T(8,128)(2,1)S(1)} collective-permute-done((bf16[133,8,128]{2,1,0:T(8,128)(2,1)}, bf16[133,8,128]{2,1,0:T(8,128)(2,1)S(1)}, u32[]{:S(2)}, u32[]{:S(2)}) %collective-permute-start.1) | collective-permute-done | bytes 272416 | tf_op jit(solution)/shard_map/density_2/ppermute | solution.py:23
  15.9 1.2 %collective-permute-start.3 = (bf16[133,8,128]{2,1,0:T(8,128)(2,1)S(1)}, bf16[133,8,128]{2,1,0:T(8,128)(2,1)S(1)}, u32[]{:S(2)}, u32[]{:S(2)}) collective-permute-start(bf16[133,8,128]{2,1,0:T(8,128)(2,1)S(1)} %collective-permute-done.1.refs_2_), channel_id=1, source_target_pairs={{0,4},{4,0},{8,12},{12,8},{16,20},{20,16},{24,28},{28,24},{1,5},{5... | collective-permute-start | bytes 817160 | tf_op jit(solution)/shard_map/density_3/ppermute | solution.py:23
  17.2 0.8 %select_reduce_fusion = s32[8,64]{1,0:T(8,128)S(1)} fusion(s32[8,64]{1,0:T(8,128)} %param.10, pred[64,64]{1,0:T(8,128)(4,1)S(1)} %iota_compare_fusion.2), kind=kLoop, calls=%fused_computation.4 | loop fusion | flops 65024 | bytes 8192 | tf_op jit(solution)/shard_map/reduce_sum | solution.py:463
  18.0 0.0 collective-permute-done.2.refs_4_.refs_0_
  18.0 3.5 %collective-permute-done.3.refs_3_ = bf16[133,8,128]{2,1,0:T(8,128)(2,1)S(1)} collective-permute-done((bf16[133,8,128]{2,1,0:T(8,128)(2,1)S(1)}, bf16[133,8,128]{2,1,0:T(8,128)(2,1)S(1)}, u32[]{:S(2)}, u32[]{:S(2)}) %collective-permute-start.3) | collective-permute-done | bytes 272416 | tf_op jit(solution)/shard_map/density_3/ppermute | solution.py:23
  21.6 1.2 %collective-permute-start.4 = (bf16[133,8,128]{2,1,0:T(8,128)(2,1)S(1)}, bf16[133,8,128]{2,1,0:T(8,128)(2,1)S(1)}, u32[]{:S(2)}, u32[]{:S(2)}) collective-permute-start(bf16[133,8,128]{2,1,0:T(8,128)(2,1)S(1)} %collective-permute-done.2.refs_4_.refs_0_), channel_id=1, source_target_pairs={{0,4},{4,0},{8,12},{12,8},{16,20},{20,16},{24,28},{28,24},{1,5},{5... | collective-permute-start | bytes 817160 | tf_op jit(solution)/shard_map/density_5/ppermute | solution.py:23
  22.8 6.8 %collective-permute-done.5.refs_6_.refs_1_ = bf16[133,8,128]{2,1,0:T(8,128)(2,1)S(1)} collective-permute-done((bf16[133,8,128]{2,1,0:T(8,128)(2,1)}, bf16[133,8,128]{2,1,0:T(8,128)(2,1)S(1)}, u32[]{:S(2)}, u32[]{:S(2)}) %collective-permute-start.5) | collective-permute-done | bytes 272416 | tf_op jit(solution)/shard_map/density_6/ppermute | solution.py:23
  29.6 1.2 %collective-permute-start.6 = (bf16[133,8,128]{2,1,0:T(8,128)(2,1)S(1)}, bf16[133,8,128]{2,1,0:T(8,128)(2,1)S(1)}, u32[]{:S(2)}, u32[]{:S(2)}) collective-permute-start(bf16[133,8,128]{2,1,0:T(8,128)(2,1)S(1)} %collective-permute-done.5.refs_6_.refs_1_), channel_id=1, source_target_pairs={{0,4},{4,0},{8,12},{12,8},{16,20},{20,16},{24,28},{28,24},{1,5},{5... | collective-permute-start | bytes 817160 | tf_op jit(solution)/shard_map/density_7/ppermute | solution.py:23
  30.8 0.4 fusion.spread_ref
  31.2 0.0 copy-start
  31.3 2.2 %copy-done = bf16[512,4096]{1,0:T(8,128)(2,1)S(1)} copy-done((bf16[512,4096]{1,0:T(8,128)(2,1)S(1)}, bf16[512,4096]{1,0:T(8,128)(2,1)}, u32[]{:S(2)}) %copy-start) | copy-done | bytes 4194328
  33.4 0.0 copy-start.2
  33.4 1.0 %copy-done.2 = bf16[133,8,128]{2,1,0:T(8,128)(2,1)S(1)} copy-done((bf16[133,8,128]{2,1,0:T(8,128)(2,1)S(1)}, bf16[133,8,128]{2,1,0:T(8,128)(2,1)}, u32[]{:S(2)}) %copy-start.2) | copy-done | bytes 272408
  34.4 0.0 copy-start.1
  34.4 1.3 %shard_map.88.refs_3_ = f32[256,512]{1,0:T(8,128)S(1)} custom-call(s32[1]{0:T(128)} %bitcast.where_ref, bf16[512,4096]{1,0:T(8,128)(2,1)S(1)} %copy-done, bf16[133,8,128]{2,1,0:T(8,128)(2,1)S(1)} %copy-done.2, bf16[133,8,128]{2,1,0:T(8,128)(2,1)S(1)} %collective-permute-done.refs_1_, bf16[133,8,128]{2,1,0:T(8,128)(2,1)S(1)} %collective-permute-done.1.refs_2_, ...), custom_call_target="tpu_custom_call" | custom-call | bytes 8388608 | tf_op jit(solution)/shard_map/pallas_call | solution.py:64
  35.7 0.0 copy-start.4
  35.7 0.0 copy-start.3
  35.8 0.0 collective-permute-done.4.refs_5_.refs_2_
  35.8 0.8 %copy-done.1 = bf16[512,4096]{1,0:T(8,128)(2,1)S(1)} copy-done((bf16[512,4096]{1,0:T(8,128)(2,1)S(1)}, bf16[512,4096]{1,0:T(8,128)(2,1)}, u32[]{:S(2)}) %copy-start.1) | copy-done | bytes 4194328
  36.6 1.2 %shard_map.89 = (f32[256,512]{1,0:T(8,128)S(1)}, bf16[512,512]{1,0:T(8,128)(2,1)S(1)}) custom-call(s32[1]{0:T(128)} %bitcast.where_ref, bf16[512,4096]{1,0:T(8,128)(2,1)S(1)} %copy-done.1, bf16[133,8,128]{2,1,0:T(8,128)(2,1)S(1)} %collective-permute-done.2.refs_4_.refs_0_, bf16[133,8,128]{2,1,0:T(8,128)(2,1)S(1)} %collective-permute-done.5.refs_6_.refs_1_, ...), custom_call_target="tpu_custom_call" | custom-call | bytes 6291456 | tf_op jit(solution)/shard_map/pallas_call | solution.py:64
  37.8 0.0 collective-permute-done.6.refs_7_.part_ref
  37.8 0.8 shard_map.90.refs_0_
  38.5 0.1 collective-permute-start.11
  38.6 0.7 collective-permute-start.7
  39.4 0.1 broadcast_add_fusion
  39.4 0.0 copy-done.4
  39.4 0.1 stack_reshape.4
  39.5 0.1 add.95
  39.6 1.5 %collective-permute-start.10 = (bf16[32,4096]{1,0:T(8,128)(2,1)S(1)}, bf16[32,4096]{1,0:T(8,128)(2,1)S(1)}, u32[]{:S(2)}, u32[]{:S(2)}) collective-permute-start(bf16[32,4096]{1,0:T(8,128)(2,1)S(1)} %shard_map.90.refs_0_), channel_id=1, source_target_pairs={{0,16},{4,20},{8,24},{12,28},{16,0},{20,4},{24,8},{28,12},{1,17},{... | collective-permute-start | bytes 786440 | tf_op jit(solution)/shard_map/half_4/ppermute | solution.py:23
  41.2 4.6 %collective-permute-done.7.refs_1_ = bf16[32,4096]{1,0:T(8,128)(2,1)S(1)} collective-permute-done((bf16[32,4096]{1,0:T(8,128)(2,1)S(1)}, bf16[32,4096]{1,0:T(8,128)(2,1)S(1)}, u32[]{:S(2)}, u32[]{:S(2)}) %collective-permute-start.7) | collective-permute-done | bytes 262176 | tf_op jit(solution)/shard_map/half_1/ppermute | solution.py:23
  45.8 0.0 collective-permute-start.8
  45.8 0.0 collective-permute-done.11.refs_2_
  45.8 0.1 collective-permute-start.12
  45.9 0.0 copy-done.3
  45.9 4.8 %shard_map.87 = (s32[24,128]{1,0:T(8,128)S(1)}, f32[514,8,128]{2,1,0:T(8,128)S(1)}) custom-call(s32[1]{0:T(128)} %bitcast.where_ref, bf16[133,8,128]{2,1,0:T(8,128)(2,1)S(1)} %copy-done.3, bf16[133,8,128]{2,1,0:T(8,128)(2,1)S(1)} %collective-permute-done.refs_1_, bf16[133,8,128]{2,1,0:T(8,128)(2,1)S(1)} %collective-permute-done.1.refs_2_, ...), custom_call_target="tpu_custom_call" | custom-call | bytes 16777216 | tf_op jit(solution)/shard_map/pallas_call | solution.py:64
  50.7 4.4 %shard_map.91 = (bf16[3,64,32,256]{3,2,1,0:T(8,128)(2,1)S(1)}, f32[8,64]{1,0:T(8,128)S(1)}) custom-call(s32[24,128]{1,0:T(8,128)S(1)} %get-tuple-element.30.meta_ref, f32[514,8,128]{2,1,0:T(8,128)S(1)} %get-tuple-element.31.table_ref, bf16[32,4096]{1,0:T(8,128)(2,1)S(1)} %shard_map.90.refs_0_, bf16[32,4096]{1,0:T(8,128)(2,1)S(1)} %collective-permute-done.7.refs_1_, ...), custom_call_target="tpu_custom_call" | custom-call | bytes 18874368 | tf_op jit(solution)/shard_map/pallas_call | solution.py:396
  55.1 0.0 collective-permute-done.10.refs_1_
  55.1 0.0 collective-permute-done.12.refs_0_
  55.1 2.1 %collective-permute-start.13 = (bf16[32,4096]{1,0:T(8,128)(2,1)S(1)}, bf16[32,4096]{1,0:T(8,128)(2,1)S(1)}, u32[]{:S(2)}, u32[]{:S(2)}) collective-permute-start(bf16[32,4096]{1,0:T(8,128)(2,1)S(1)} %collective-permute-done.10.refs_1_), channel_id=1, source_target_pairs={{0,4},{4,0},{8,12},{12,8},{16,20},{20,16},{24,28},{28,24},{1,5},{5... | collective-permute-start | bytes 786440 | tf_op jit(solution)/shard_map/half_5/ppermute | solution.py:23
  57.2 7.1 %collective-permute-done.8.refs_2_ = bf16[32,4096]{1,0:T(8,128)(2,1)S(1)} collective-permute-done((bf16[32,4096]{1,0:T(8,128)(2,1)S(1)}, bf16[32,4096]{1,0:T(8,128)(2,1)S(1)}, u32[]{:S(2)}, u32[]{:S(2)}) %collective-permute-start.8) | collective-permute-done | bytes 262176 | tf_op jit(solution)/shard_map/half_6/ppermute | solution.py:23
  64.3 1.1 %collective-permute-start.9 = (bf16[32,4096]{1,0:T(8,128)(2,1)S(1)}, bf16[32,4096]{1,0:T(8,128)(2,1)S(1)}, u32[]{:S(2)}, u32[]{:S(2)}) collective-permute-start(bf16[32,4096]{1,0:T(8,128)(2,1)S(1)} %collective-permute-done.8.refs_2_), channel_id=1, source_target_pairs={{0,4},{4,0},{8,12},{12,8},{16,20},{20,16},{24,28},{28,24},{1,5},{5... | collective-permute-start | bytes 786440 | tf_op jit(solution)/shard_map/half_7/ppermute | solution.py:23
  65.3 5.1 %shard_map.92 = (bf16[3,64,32,256]{3,2,1,0:T(8,128)(2,1)S(1)}, f32[8,64]{1,0:T(8,128)S(1)}, bf16[512,32,256]{2,1,0:T(8,128)(2,1)}) custom-call(s32[24,128]{1,0:T(8,128)S(1)} %get-tuple-element.30.meta_ref, f32[514,8,128]{2,1,0:T(8,128)S(1)} %get-tuple-element.31.table_ref, bf16[32,4096]{1,0:T(8,128)(2,1)S(1)} %collective-permute-done.12.refs_0_, ...), custom_call_target="tpu_custom_call" | custom-call | bytes 18874368 | tf_op jit(solution)/shard_map/pallas_call | solution.py:396
  70.5 0.0 collective-permute-done.13.refs_0_
  70.5 2.4 %shard_map.93 = (bf16[1,64,32,256]{3,2,1,0:T(8,128)(2,1)S(1)}, f32[8,64]{1,0:T(8,128)S(1)}, bf16[512,32,256]{2,1,0:T(8,128)(2,1)}) custom-call(s32[24,128]{1,0:T(8,128)S(1)} %get-tuple-element.30.meta_ref, f32[514,8,128]{2,1,0:T(8,128)S(1)} %get-tuple-element.31.table_ref, ...), custom_call_target="tpu_custom_call", output_to_operand_aliasing={{2}: (5, {})} | custom-call | bytes 6291456 | tf_op jit(solution)/shard_map/pallas_call | solution.py:396
  72.9 0.0 collective-permute-done.9.refs_0_
  72.9 1.7 %shard_map.94 = (bf16[1,64,32,256]{3,2,1,0:T(8,128)(2,1)S(1)}, f32[8,64]{1,0:T(8,128)S(1)}, bf16[512,32,256]{2,1,0:T(8,128)(2,1)}) custom-call(s32[24,128]{1,0:T(8,128)S(1)} %get-tuple-element.30.meta_ref, f32[514,8,128]{2,1,0:T(8,128)S(1)} %get-tuple-element.31.table_ref, ...), custom_call_target="tpu_custom_call", output_to_operand_aliasing={{2}: (5, {})} | custom-call | bytes 6291456 | tf_op jit(solution)/shard_map/pallas_call | solution.py:396
  74.6 3.3 %collective-permute-start.16 = (f32[8,64]{1,0:T(8,128)S(1)}, f32[8,64]{1,0:T(8,128)S(1)}, u32[]{:S(2)}, u32[]{:S(2)}) collective-permute-start(f32[8,64]{1,0:T(8,128)S(1)} %get-tuple-element.49), channel_id=1, source_target_pairs={{0,3},{1,2},{2,1},{3,0},{4,7},{5,6},{6,5},{7,4},{8,11},{9,10},{10,... | collective-permute-start | bytes 6152 | tf_op jit(solution)/shard_map/ppermute | solution.py:23
  77.9 0.3 collective-permute-start.15
  78.2 0.2 collective-permute-start.14
  78.4 1.7 %shard_map.95 = bf16[512,32,256]{2,1,0:T(8,128)(2,1)} custom-call(s32[24,128]{1,0:T(8,128)S(1)} %get-tuple-element.30.meta_ref, bf16[1,64,32,256]{3,2,1,0:T(8,128)(2,1)S(1)} %get-tuple-element.47.held_ref, bf16[512,32,256]{2,1,0:T(8,128)(2,1)} %get-tuple-element.48._), custom_call_target="tpu_custom_call", output_to_operand_aliasing={{}: (2, {})} | custom-call | bytes 4194304 | tf_op jit(solution)/shard_map/pallas_call | solution.py:418
  80.1 0.0 collective-permute-done.16
  80.1 0.3 collective-permute-done.15
  80.4 0.0 collective-permute-done.14
  80.4 0.7 sqrt.7
  (9 shorter events, 0.1 us)
Async XLA Ops:
  2.5 15.6 %collective-permute-start.2 = (bf16[133,8,128]{2,1,0:T(8,128)(2,1)}, bf16[133,8,128]{2,1,0:T(8,128)(2,1)S(1)}, u32[]{:S(2)}, u32[]{:S(2)}) collective-permute-start(bf16[133,8,128]{2,1,0:T(8,128)(2,1)} %shard_map.86.refs_0_), channel_id=1, source_target_pairs={{0,16},{4,20},{8,24},{12,28},{16,0},{20,4},{24,8},{28,12},{1,17},{... | collective-permute-start | bytes 817160 | tf_op jit(solution)/shard_map/density_4/ppermute | solution.py:23
  2.5 13.4 %collective-permute-start.1 = (bf16[133,8,128]{2,1,0:T(8,128)(2,1)}, bf16[133,8,128]{2,1,0:T(8,128)(2,1)S(1)}, u32[]{:S(2)}, u32[]{:S(2)}) collective-permute-start(bf16[133,8,128]{2,1,0:T(8,128)(2,1)} %shard_map.86.refs_0_), channel_id=1, source_target_pairs={{0,8},{4,12},{8,0},{12,4},{16,24},{20,28},{24,16},{28,20},{1,9},{5... | collective-permute-start | bytes 817160 | tf_op jit(solution)/shard_map/density_2/ppermute | solution.py:23
  3.9 7.0 %collective-permute-start = (bf16[133,8,128]{2,1,0:T(8,128)(2,1)}, bf16[133,8,128]{2,1,0:T(8,128)(2,1)S(1)}, u32[]{:S(2)}, u32[]{:S(2)}) collective-permute-start(bf16[133,8,128]{2,1,0:T(8,128)(2,1)} %shard_map.86.refs_0_), channel_id=1, source_target_pairs={{0,4},{4,0},{8,12},{12,8},{16,20},{20,16},{24,28},{28,24},{1,5},{5... | collective-permute-start | bytes 817160 | tf_op jit(solution)/shard_map/density_1/ppermute | solution.py:23
  10.9 18.7 %collective-permute-start.5 = (bf16[133,8,128]{2,1,0:T(8,128)(2,1)}, bf16[133,8,128]{2,1,0:T(8,128)(2,1)S(1)}, u32[]{:S(2)}, u32[]{:S(2)}) collective-permute-start(bf16[133,8,128]{2,1,0:T(8,128)(2,1)} %shard_map.86.refs_0_), channel_id=1, source_target_pairs={{0,24},{4,28},{8,16},{12,20},{16,8},{20,12},{24,0},{28,4},{1,25},{... | collective-permute-start | bytes 817160 | tf_op jit(solution)/shard_map/density_6/ppermute | solution.py:23
  15.9 5.6 %collective-permute-start.3 = (bf16[133,8,128]{2,1,0:T(8,128)(2,1)S(1)}, bf16[133,8,128]{2,1,0:T(8,128)(2,1)S(1)}, u32[]{:S(2)}, u32[]{:S(2)}) collective-permute-start(bf16[133,8,128]{2,1,0:T(8,128)(2,1)S(1)} %collective-permute-done.1.refs_2_), channel_id=1, source_target_pairs={{0,4},{4,0},{8,12},{12,8},{16,20},{20,16},{24,28},{28,24},{1,5},{5... | collective-permute-start | bytes 817160 | tf_op jit(solution)/shard_map/density_3/ppermute | solution.py:23
  21.6 14.2 %collective-permute-start.4 = (bf16[133,8,128]{2,1,0:T(8,128)(2,1)S(1)}, bf16[133,8,128]{2,1,0:T(8,128)(2,1)S(1)}, u32[]{:S(2)}, u32[]{:S(2)}) collective-permute-start(bf16[133,8,128]{2,1,0:T(8,128)(2,1)S(1)} %collective-permute-done.2.refs_4_.refs_0_), channel_id=1, source_target_pairs={{0,4},{4,0},{8,12},{12,8},{16,20},{20,16},{24,28},{28,24},{1,5},{5... | collective-permute-start | bytes 817160 | tf_op jit(solution)/shard_map/density_5/ppermute | solution.py:23
  29.6 8.2 %collective-permute-start.6 = (bf16[133,8,128]{2,1,0:T(8,128)(2,1)S(1)}, bf16[133,8,128]{2,1,0:T(8,128)(2,1)S(1)}, u32[]{:S(2)}, u32[]{:S(2)}) collective-permute-start(bf16[133,8,128]{2,1,0:T(8,128)(2,1)S(1)} %collective-permute-done.5.refs_6_.refs_1_), channel_id=1, source_target_pairs={{0,4},{4,0},{8,12},{12,8},{16,20},{20,16},{24,28},{28,24},{1,5},{5... | collective-permute-start | bytes 817160 | tf_op jit(solution)/shard_map/density_7/ppermute | solution.py:23
  31.2 2.2 %copy-start = (bf16[512,4096]{1,0:T(8,128)(2,1)S(1)}, bf16[512,4096]{1,0:T(8,128)(2,1)}, u32[]{:S(2)}) copy-start(bf16[512,4096]{1,0:T(8,128)(2,1)} %vir_ref.3) | copy-start | bytes 12582916
  33.4 1.0 %copy-start.2 = (bf16[133,8,128]{2,1,0:T(8,128)(2,1)S(1)}, bf16[133,8,128]{2,1,0:T(8,128)(2,1)}, u32[]{:S(2)}) copy-start(bf16[133,8,128]{2,1,0:T(8,128)(2,1)} %shard_map.86.refs_0_) | copy-start | bytes 817156
  34.4 2.2 %copy-start.1 = (bf16[512,4096]{1,0:T(8,128)(2,1)S(1)}, bf16[512,4096]{1,0:T(8,128)(2,1)}, u32[]{:S(2)}) copy-start(bf16[512,4096]{1,0:T(8,128)(2,1)} %vir_ref.3) | copy-start | bytes 12582916
  35.7 3.7 %copy-start.4 = (s32[8,64]{1,0:T(8,128)S(1)}, s32[8,64]{1,0:T(8,128)}, u32[]{:S(2)}) copy-start(s32[8,64]{1,0:T(8,128)} %param.10) | copy-start | bytes 6148
  35.7 10.1 %copy-start.3 = (bf16[133,8,128]{2,1,0:T(8,128)(2,1)S(1)}, bf16[133,8,128]{2,1,0:T(8,128)(2,1)}, u32[]{:S(2)}) copy-start(bf16[133,8,128]{2,1,0:T(8,128)(2,1)} %shard_map.86.refs_0_) | copy-start | bytes 817156
  38.5 7.2 %collective-permute-start.11 = (bf16[32,4096]{1,0:T(8,128)(2,1)S(1)}, bf16[32,4096]{1,0:T(8,128)(2,1)S(1)}, u32[]{:S(2)}, u32[]{:S(2)}) collective-permute-start(bf16[32,4096]{1,0:T(8,128)(2,1)S(1)} %shard_map.90.refs_0_), channel_id=1, source_target_pairs={{0,8},{4,12},{8,0},{12,4},{16,24},{20,28},{24,16},{28,20},{1,9},{5... | collective-permute-start | bytes 786440 | tf_op jit(solution)/shard_map/half_2/ppermute | solution.py:23
  38.6 7.1 %collective-permute-start.7 = (bf16[32,4096]{1,0:T(8,128)(2,1)S(1)}, bf16[32,4096]{1,0:T(8,128)(2,1)S(1)}, u32[]{:S(2)}, u32[]{:S(2)}) collective-permute-start(bf16[32,4096]{1,0:T(8,128)(2,1)S(1)} %shard_map.90.refs_0_), channel_id=1, source_target_pairs={{0,4},{4,0},{8,12},{12,8},{16,20},{20,16},{24,28},{28,24},{1,5},{5... | collective-permute-start | bytes 786440 | tf_op jit(solution)/shard_map/half_1/ppermute | solution.py:23
  39.6 15.5 %collective-permute-start.10 = (bf16[32,4096]{1,0:T(8,128)(2,1)S(1)}, bf16[32,4096]{1,0:T(8,128)(2,1)S(1)}, u32[]{:S(2)}, u32[]{:S(2)}) collective-permute-start(bf16[32,4096]{1,0:T(8,128)(2,1)S(1)} %shard_map.90.refs_0_), channel_id=1, source_target_pairs={{0,16},{4,20},{8,24},{12,28},{16,0},{20,4},{24,8},{28,12},{1,17},{... | collective-permute-start | bytes 786440 | tf_op jit(solution)/shard_map/half_4/ppermute | solution.py:23
  45.8 18.5 %collective-permute-start.8 = (bf16[32,4096]{1,0:T(8,128)(2,1)S(1)}, bf16[32,4096]{1,0:T(8,128)(2,1)S(1)}, u32[]{:S(2)}, u32[]{:S(2)}) collective-permute-start(bf16[32,4096]{1,0:T(8,128)(2,1)S(1)} %shard_map.90.refs_0_), channel_id=1, source_target_pairs={{0,24},{4,28},{8,16},{12,20},{16,8},{20,12},{24,0},{28,4},{1,25},{... | collective-permute-start | bytes 786440 | tf_op jit(solution)/shard_map/half_6/ppermute | solution.py:23
  45.8 9.3 %collective-permute-start.12 = (bf16[32,4096]{1,0:T(8,128)(2,1)S(1)}, bf16[32,4096]{1,0:T(8,128)(2,1)S(1)}, u32[]{:S(2)}, u32[]{:S(2)}) collective-permute-start(bf16[32,4096]{1,0:T(8,128)(2,1)S(1)} %collective-permute-done.11.refs_2_), channel_id=1, source_target_pairs={{0,4},{4,0},{8,12},{12,8},{16,20},{20,16},{24,28},{28,24},{1,5},{5... | collective-permute-start | bytes 786440 | tf_op jit(solution)/shard_map/half_3/ppermute | solution.py:23
  55.1 15.4 %collective-permute-start.13 = (bf16[32,4096]{1,0:T(8,128)(2,1)S(1)}, bf16[32,4096]{1,0:T(8,128)(2,1)S(1)}, u32[]{:S(2)}, u32[]{:S(2)}) collective-permute-start(bf16[32,4096]{1,0:T(8,128)(2,1)S(1)} %collective-permute-done.10.refs_1_), channel_id=1, source_target_pairs={{0,4},{4,0},{8,12},{12,8},{16,20},{20,16},{24,28},{28,24},{1,5},{5... | collective-permute-start | bytes 786440 | tf_op jit(solution)/shard_map/half_5/ppermute | solution.py:23
  64.3 8.6 %collective-permute-start.9 = (bf16[32,4096]{1,0:T(8,128)(2,1)S(1)}, bf16[32,4096]{1,0:T(8,128)(2,1)S(1)}, u32[]{:S(2)}, u32[]{:S(2)}) collective-permute-start(bf16[32,4096]{1,0:T(8,128)(2,1)S(1)} %collective-permute-done.8.refs_2_), channel_id=1, source_target_pairs={{0,4},{4,0},{8,12},{12,8},{16,20},{20,16},{24,28},{28,24},{1,5},{5... | collective-permute-start | bytes 786440 | tf_op jit(solution)/shard_map/half_7/ppermute | solution.py:23
  74.6 5.5 %collective-permute-start.16 = (f32[8,64]{1,0:T(8,128)S(1)}, f32[8,64]{1,0:T(8,128)S(1)}, u32[]{:S(2)}, u32[]{:S(2)}) collective-permute-start(f32[8,64]{1,0:T(8,128)S(1)} %get-tuple-element.49), channel_id=1, source_target_pairs={{0,3},{1,2},{2,1},{3,0},{4,7},{5,6},{6,5},{7,4},{8,11},{9,10},{10,... | collective-permute-start | bytes 6152 | tf_op jit(solution)/shard_map/ppermute | solution.py:23
  77.9 2.5 %collective-permute-start.15 = (f32[8,64]{1,0:T(8,128)S(1)}, f32[8,64]{1,0:T(8,128)S(1)}, u32[]{:S(2)}, u32[]{:S(2)}) collective-permute-start(f32[8,64]{1,0:T(8,128)S(1)} %get-tuple-element.49), channel_id=1, source_target_pairs={{0,2},{1,3},{2,0},{3,1},{4,6},{5,7},{6,4},{7,5},{8,10},{9,11},{10,... | collective-permute-start | bytes 6152 | tf_op jit(solution)/shard_map/ppermute | solution.py:23
  78.2 2.2 %collective-permute-start.14 = (f32[8,64]{1,0:T(8,128)S(1)}, f32[8,64]{1,0:T(8,128)S(1)}, u32[]{:S(2)}, u32[]{:S(2)}) collective-permute-start(f32[8,64]{1,0:T(8,128)S(1)} %get-tuple-element.49), channel_id=1, source_target_pairs={{0,1},{1,0},{2,3},{3,2},{4,5},{5,4},{6,7},{7,6},{8,9},{9,8},{10,11... | collective-permute-start | bytes 6152 | tf_op jit(solution)/shard_map/ppermute | solution.py:23

commit v4 on v3

--- a/solution.py
+++ b/solution.py
@@ -13,7 +13,7 @@
 DIGIT = 128
 CODE_BITS = 5
 CODE = 1 << CODE_BITS
-GROUP = 32
+GROUP = 64
 MIB = 1 << 20
 VMEM = pl.BlockSpec(memory_space=pltpu.VMEM)
 HBM = pl.BlockSpec(memory_space=pltpu.HBM)

time: 81.6 us -> 80.6 us (0.988)
  the two profiles are of different devices: /device:TPU:17 before, /device:TPU:0 now
where the time goes in v4:
time: 80.6 us; the launch traced here: 80.1 us
  starting transfers between devices  25 us (31%)
  waiting for transfers between devices  24.6 us (31%)
  Pallas kernels  24.3 us (30%)
  local copies, waits for them, and re-layouts  3.97 us (5%)
  other arithmetic  1.49 us (2%)
  between operations  0.83 us (1%)
    ppermute x17, starting transfers between devices, swap(): return lax.ppermute(x, axis, [(i, i ^ k) for i in range(count)])  25 us
    ppermute x17, waiting for transfers between devices, swap(): return lax.ppermute(x, axis, [(i, i ^ k) for i in range(count)])  24.6 us
    pallas_call x4, Pallas kernels, make_blocks(): pl.pallas_call(functools.partial(block_kernel, ks, old_ks, out is not Non...  12.6 us
    pallas_call x5, Pallas kernels, whole(): pl.pallas_call(body, out_shape=out_shape, grid_spec=pltpu.PrefetchScalarG...  9.92 us
    unnamed x10, local copies, waits for them, and re-layouts  3.15 us
    pallas_call x1, Pallas kernels, make_output(): pl.pallas_call(functools.partial(ship_kernel, ks, count, capacity), out_s...  1.71 us
  transfers between devices with their start and end apart: 17, of which 10 were waited for; matrix products, arithmetic and copies ran while one was open for 2% of the time, Pallas kernels for 25%

profile of v4, /device:TPU:0, one launch (start us, length us, event | category | flops | bytes accessed | tf_op | source)
XLA Modules:
  0.0 80.1 jit_solution(8911886227459924183)
XLA Ops:
  0.6 1.8 %shard_map.86.refs_0_ = bf16[133,8,128]{2,1,0:T(8,128)(2,1)} custom-call(bf16[32,8,512]{2,1,0:T(8,128)(2,1)} %density_ref.1, bf16[8,512]{1,0:T(8,128)(2,1)} %occ_ref.1, s32[1,256]{1,0:T(1,128)} %bitcast.4, s32[1,256]{1,0:T(1,128)} %bitcast.5, s32[1,256]{1,0:T(1,128)} %bitcast.6), custom_call_target="tpu_custom_call" | custom-call | tf_op jit(solution)/shard_map/pallas_call | solution.py:64
  2.5 4.1 %collective-permute-start.2 = (bf16[133,8,128]{2,1,0:T(8,128)(2,1)}, bf16[133,8,128]{2,1,0:T(8,128)(2,1)S(1)}, u32[]{:S(2)}, u32[]{:S(2)}) collective-permute-start(bf16[133,8,128]{2,1,0:T(8,128)(2,1)} %shard_map.86.refs_0_), channel_id=1, source_target_pairs={{0,16},{4,20},{8,24},{12,28},{16,0},{20,4},{24,8},{28,12},{1,17},{... | collective-permute-start | bytes 817160 | tf_op jit(solution)/shard_map/density_4/ppermute | solution.py:23
  6.6 1.6 %collective-permute-start.1 = (bf16[133,8,128]{2,1,0:T(8,128)(2,1)}, bf16[133,8,128]{2,1,0:T(8,128)(2,1)S(1)}, u32[]{:S(2)}, u32[]{:S(2)}) collective-permute-start(bf16[133,8,128]{2,1,0:T(8,128)(2,1)} %shard_map.86.refs_0_), channel_id=1, source_target_pairs={{0,8},{4,12},{8,0},{12,4},{16,24},{20,28},{24,16},{28,20},{1,9},{5... | collective-permute-start | bytes 817160 | tf_op jit(solution)/shard_map/density_2/ppermute | solution.py:23
  8.1 1.5 %collective-permute-start = (bf16[133,8,128]{2,1,0:T(8,128)(2,1)}, bf16[133,8,128]{2,1,0:T(8,128)(2,1)S(1)}, u32[]{:S(2)}, u32[]{:S(2)}) collective-permute-start(bf16[133,8,128]{2,1,0:T(8,128)(2,1)} %shard_map.86.refs_0_), channel_id=1, source_target_pairs={{0,4},{4,0},{8,12},{12,8},{16,20},{20,16},{24,28},{28,24},{1,5},{5... | collective-permute-start | bytes 817160 | tf_op jit(solution)/shard_map/density_1/ppermute | solution.py:23
  9.7 0.1 fusion.1.refs_9_
  9.8 6.3 %collective-permute-done.refs_1_ = bf16[133,8,128]{2,1,0:T(8,128)(2,1)S(1)} collective-permute-done((bf16[133,8,128]{2,1,0:T(8,128)(2,1)}, bf16[133,8,128]{2,1,0:T(8,128)(2,1)S(1)}, u32[]{:S(2)}, u32[]{:S(2)}) %collective-permute-start) | collective-permute-done | bytes 272416 | tf_op jit(solution)/shard_map/density_1/ppermute | solution.py:23
  16.1 0.2 collective-permute-start.5
  16.3 3.4 %collective-permute-done.1.refs_2_ = bf16[133,8,128]{2,1,0:T(8,128)(2,1)S(1)} collective-permute-done((bf16[133,8,128]{2,1,0:T(8,128)(2,1)}, bf16[133,8,128]{2,1,0:T(8,128)(2,1)S(1)}, u32[]{:S(2)}, u32[]{:S(2)}) %collective-permute-start.1) | collective-permute-done | bytes 272416 | tf_op jit(solution)/shard_map/density_2/ppermute | solution.py:23
  19.7 1.5 %collective-permute-start.3 = (bf16[133,8,128]{2,1,0:T(8,128)(2,1)S(1)}, bf16[133,8,128]{2,1,0:T(8,128)(2,1)S(1)}, u32[]{:S(2)}, u32[]{:S(2)}) collective-permute-start(bf16[133,8,128]{2,1,0:T(8,128)(2,1)S(1)} %collective-permute-done.1.refs_2_), channel_id=1, source_target_pairs={{0,4},{4,0},{8,12},{12,8},{16,20},{20,16},{24,28},{28,24},{1,5},{5... | collective-permute-start | bytes 817160 | tf_op jit(solution)/shard_map/density_3/ppermute | solution.py:23
  21.2 0.8 %select_reduce_fusion = s32[8,64]{1,0:T(8,128)S(1)} fusion(s32[8,64]{1,0:T(8,128)} %param.10, pred[64,64]{1,0:T(8,128)(4,1)S(1)} %iota_compare_fusion.2), kind=kLoop, calls=%fused_computation.4 | loop fusion | flops 65024 | bytes 8192 | tf_op jit(solution)/shard_map/reduce_sum | solution.py:463
  22.1 0.0 collective-permute-done.2.refs_4_.refs_0_
  22.1 4.5 %collective-permute-done.3.refs_3_ = bf16[133,8,128]{2,1,0:T(8,128)(2,1)S(1)} collective-permute-done((bf16[133,8,128]{2,1,0:T(8,128)(2,1)S(1)}, bf16[133,8,128]{2,1,0:T(8,128)(2,1)S(1)}, u32[]{:S(2)}, u32[]{:S(2)}) %collective-permute-start.3) | collective-permute-done | bytes 272416 | tf_op jit(solution)/shard_map/density_3/ppermute | solution.py:23
  26.5 1.5 %collective-permute-start.4 = (bf16[133,8,128]{2,1,0:T(8,128)(2,1)S(1)}, bf16[133,8,128]{2,1,0:T(8,128)(2,1)S(1)}, u32[]{:S(2)}, u32[]{:S(2)}) collective-permute-start(bf16[133,8,128]{2,1,0:T(8,128)(2,1)S(1)} %collective-permute-done.2.refs_4_.refs_0_), channel_id=1, source_target_pairs={{0,4},{4,0},{8,12},{12,8},{16,20},{20,16},{24,28},{28,24},{1,5},{5... | collective-permute-start | bytes 817160 | tf_op jit(solution)/shard_map/density_5/ppermute | solution.py:23
  28.1 0.0 collective-permute-done.5.refs_6_.refs_1_
  28.1 0.5 collective-permute-start.6
  28.6 0.4 fusion.spread_ref
  29.0 0.0 copy-start
  29.0 2.2 %copy-done = bf16[512,4096]{1,0:T(8,128)(2,1)S(1)} copy-done((bf16[512,4096]{1,0:T(8,128)(2,1)S(1)}, bf16[512,4096]{1,0:T(8,128)(2,1)}, u32[]{:S(2)}) %copy-start) | copy-done | bytes 4194328
  31.2 0.0 copy-start.2
  31.2 1.0 %copy-done.2 = bf16[133,8,128]{2,1,0:T(8,128)(2,1)S(1)} copy-done((bf16[133,8,128]{2,1,0:T(8,128)(2,1)S(1)}, bf16[133,8,128]{2,1,0:T(8,128)(2,1)}, u32[]{:S(2)}) %copy-start.2) | copy-done | bytes 272408
  32.1 0.0 copy-start.1
  32.1 1.3 %shard_map.88.refs_3_ = f32[256,512]{1,0:T(8,128)S(1)} custom-call(s32[1]{0:T(128)} %bitcast.where_ref, bf16[512,4096]{1,0:T(8,128)(2,1)S(1)} %copy-done, bf16[133,8,128]{2,1,0:T(8,128)(2,1)S(1)} %copy-done.2, bf16[133,8,128]{2,1,0:T(8,128)(2,1)S(1)} %collective-permute-done.refs_1_, bf16[133,8,128]{2,1,0:T(8,128)(2,1)S(1)} %collective-permute-done.1.refs_2_, ...), custom_call_target="tpu_custom_call" | custom-call | bytes 8388608 | tf_op jit(solution)/shard_map/pallas_call | solution.py:64
  33.5 0.0 copy-start.4
  33.5 0.0 copy-start.3
  33.5 1.4 %collective-permute-done.4.refs_5_.refs_2_ = bf16[133,8,128]{2,1,0:T(8,128)(2,1)S(1)} collective-permute-done((bf16[133,8,128]{2,1,0:T(8,128)(2,1)S(1)}, bf16[133,8,128]{2,1,0:T(8,128)(2,1)S(1)}, u32[]{:S(2)}, u32[]{:S(2)}) %collective-permute-start.4) | collective-permute-done | bytes 272416 | tf_op jit(solution)/shard_map/density_5/ppermute | solution.py:23
  34.9 0.0 copy-done.1
  34.9 1.2 %shard_map.89 = (f32[256,512]{1,0:T(8,128)S(1)}, bf16[512,512]{1,0:T(8,128)(2,1)S(1)}) custom-call(s32[1]{0:T(128)} %bitcast.where_ref, bf16[512,4096]{1,0:T(8,128)(2,1)S(1)} %copy-done.1, bf16[133,8,128]{2,1,0:T(8,128)(2,1)S(1)} %collective-permute-done.2.refs_4_.refs_0_, bf16[133,8,128]{2,1,0:T(8,128)(2,1)S(1)} %collective-permute-done.5.refs_6_.refs_1_, ...), custom_call_target="tpu_custom_call" | custom-call | bytes 6291456 | tf_op jit(solution)/shard_map/pallas_call | solution.py:64
  36.1 1.7 %collective-permute-done.6.refs_7_.part_ref = bf16[133,8,128]{2,1,0:T(8,128)(2,1)S(1)} collective-permute-done((bf16[133,8,128]{2,1,0:T(8,128)(2,1)S(1)}, bf16[133,8,128]{2,1,0:T(8,128)(2,1)S(1)}, u32[]{:S(2)}, u32[]{:S(2)}) %collective-permute-start.6) | collective-permute-done | bytes 272416 | tf_op jit(solution)/shard_map/density_7/ppermute | solution.py:23
  37.9 0.8 shard_map.90.refs_0_
  38.6 3.5 %collective-permute-start.11 = (bf16[32,4096]{1,0:T(8,128)(2,1)S(1)}, bf16[32,4096]{1,0:T(8,128)(2,1)S(1)}, u32[]{:S(2)}, u32[]{:S(2)}) collective-permute-start(bf16[32,4096]{1,0:T(8,128)(2,1)S(1)} %shard_map.90.refs_0_), channel_id=1, source_target_pairs={{0,8},{4,12},{8,0},{12,4},{16,24},{20,28},{24,16},{28,20},{1,9},{5... | collective-permute-start | bytes 786440 | tf_op jit(solution)/shard_map/half_2/ppermute | solution.py:23
  42.1 1.8 %collective-permute-start.7 = (bf16[32,4096]{1,0:T(8,128)(2,1)S(1)}, bf16[32,4096]{1,0:T(8,128)(2,1)S(1)}, u32[]{:S(2)}, u32[]{:S(2)}) collective-permute-start(bf16[32,4096]{1,0:T(8,128)(2,1)S(1)} %shard_map.90.refs_0_), channel_id=1, source_target_pairs={{0,4},{4,0},{8,12},{12,8},{16,20},{20,16},{24,28},{28,24},{1,5},{5... | collective-permute-start | bytes 786440 | tf_op jit(solution)/shard_map/half_1/ppermute | solution.py:23
  43.9 0.1 broadcast_add_fusion
  44.0 0.0 copy-done.4
  44.0 0.1 stack_reshape.4
  44.1 0.1 add.95
  44.2 0.5 collective-permute-start.10
  44.7 4.4 %collective-permute-done.7.refs_1_ = bf16[32,4096]{1,0:T(8,128)(2,1)S(1)} collective-permute-done((bf16[32,4096]{1,0:T(8,128)(2,1)S(1)}, bf16[32,4096]{1,0:T(8,128)(2,1)S(1)}, u32[]{:S(2)}, u32[]{:S(2)}) %collective-permute-start.7) | collective-permute-done | bytes 262176 | tf_op jit(solution)/shard_map/half_1/ppermute | solution.py:23
  49.0 2.8 %collective-permute-start.8 = (bf16[32,4096]{1,0:T(8,128)(2,1)S(1)}, bf16[32,4096]{1,0:T(8,128)(2,1)S(1)}, u32[]{:S(2)}, u32[]{:S(2)}) collective-permute-start(bf16[32,4096]{1,0:T(8,128)(2,1)S(1)} %shard_map.90.refs_0_), channel_id=1, source_target_pairs={{0,24},{4,28},{8,16},{12,20},{16,8},{20,12},{24,0},{28,4},{1,25},{... | collective-permute-start | bytes 786440 | tf_op jit(solution)/shard_map/half_6/ppermute | solution.py:23
  51.9 0.0 collective-permute-done.11.refs_2_
  51.9 1.4 %collective-permute-start.12 = (bf16[32,4096]{1,0:T(8,128)(2,1)S(1)}, bf16[32,4096]{1,0:T(8,128)(2,1)S(1)}, u32[]{:S(2)}, u32[]{:S(2)}) collective-permute-start(bf16[32,4096]{1,0:T(8,128)(2,1)S(1)} %collective-permute-done.11.refs_2_), channel_id=1, source_target_pairs={{0,4},{4,0},{8,12},{12,8},{16,20},{20,16},{24,28},{28,24},{1,5},{5... | collective-permute-start | bytes 786440 | tf_op jit(solution)/shard_map/half_3/ppermute | solution.py:23
  53.3 0.0 copy-done.3
  53.3 4.8 %shard_map.87 = (s32[24,128]{1,0:T(8,128)S(1)}, f32[514,8,128]{2,1,0:T(8,128)S(1)}) custom-call(s32[1]{0:T(128)} %bitcast.where_ref, bf16[133,8,128]{2,1,0:T(8,128)(2,1)S(1)} %copy-done.3, bf16[133,8,128]{2,1,0:T(8,128)(2,1)S(1)} %collective-permute-done.refs_1_, bf16[133,8,128]{2,1,0:T(8,128)(2,1)S(1)} %collective-permute-done.1.refs_2_, ...), custom_call_target="tpu_custom_call" | custom-call | bytes 16777216 | tf_op jit(solution)/shard_map/pallas_call | solution.py:64
  58.2 4.1 %shard_map.91 = (bf16[3,64,32,256]{3,2,1,0:T(8,128)(2,1)S(1)}, f32[8,64]{1,0:T(8,128)S(1)}) custom-call(s32[24,128]{1,0:T(8,128)S(1)} %get-tuple-element.30.meta_ref, f32[514,8,128]{2,1,0:T(8,128)S(1)} %get-tuple-element.31.table_ref, bf16[32,4096]{1,0:T(8,128)(2,1)S(1)} %shard_map.90.refs_0_, bf16[32,4096]{1,0:T(8,128)(2,1)S(1)} %collective-permute-done.7.refs_1_, ...), custom_call_target="tpu_custom_call" | custom-call | bytes 18874368 | tf_op jit(solution)/shard_map/pallas_call | solution.py:396
  62.3 2.2 %collective-permute-done.10.refs_1_ = bf16[32,4096]{1,0:T(8,128)(2,1)S(1)} collective-permute-done((bf16[32,4096]{1,0:T(8,128)(2,1)S(1)}, bf16[32,4096]{1,0:T(8,128)(2,1)S(1)}, u32[]{:S(2)}, u32[]{:S(2)}) %collective-permute-start.10) | collective-permute-done | bytes 262176 | tf_op jit(solution)/shard_map/half_4/ppermute | solution.py:23
  64.6 0.0 collective-permute-done.12.refs_0_
  64.6 0.7 collective-permute-start.13
  65.3 0.0 collective-permute-done.8.refs_2_
  65.3 1.3 %collective-permute-start.9 = (bf16[32,4096]{1,0:T(8,128)(2,1)S(1)}, bf16[32,4096]{1,0:T(8,128)(2,1)S(1)}, u32[]{:S(2)}, u32[]{:S(2)}) collective-permute-start(bf16[32,4096]{1,0:T(8,128)(2,1)S(1)} %collective-permute-done.8.refs_2_), channel_id=1, source_target_pairs={{0,4},{4,0},{8,12},{12,8},{16,20},{20,16},{24,28},{28,24},{1,5},{5... | collective-permute-start | bytes 786440 | tf_op jit(solution)/shard_map/half_7/ppermute | solution.py:23
  66.6 4.2 %shard_map.92 = (bf16[3,64,32,256]{3,2,1,0:T(8,128)(2,1)S(1)}, f32[8,64]{1,0:T(8,128)S(1)}, bf16[512,32,256]{2,1,0:T(8,128)(2,1)}) custom-call(s32[24,128]{1,0:T(8,128)S(1)} %get-tuple-element.30.meta_ref, f32[514,8,128]{2,1,0:T(8,128)S(1)} %get-tuple-element.31.table_ref, bf16[32,4096]{1,0:T(8,128)(2,1)S(1)} %collective-permute-done.12.refs_0_, ...), custom_call_target="tpu_custom_call" | custom-call | bytes 18874368 | tf_op jit(solution)/shard_map/pallas_call | solution.py:396
  70.8 0.2 collective-permute-done.13.refs_0_
  70.9 2.4 %shard_map.93 = (bf16[1,64,32,256]{3,2,1,0:T(8,128)(2,1)S(1)}, f32[8,64]{1,0:T(8,128)S(1)}, bf16[512,32,256]{2,1,0:T(8,128)(2,1)}) custom-call(s32[24,128]{1,0:T(8,128)S(1)} %get-tuple-element.30.meta_ref, f32[514,8,128]{2,1,0:T(8,128)S(1)} %get-tuple-element.31.table_ref, ...), custom_call_target="tpu_custom_call", output_to_operand_aliasing={{2}: (5, {})} | custom-call | bytes 6291456 | tf_op jit(solution)/shard_map/pallas_call | solution.py:396
  73.4 0.4 collective-permute-done.9.refs_0_
  73.8 1.9 %shard_map.94 = (bf16[1,64,32,256]{3,2,1,0:T(8,128)(2,1)S(1)}, f32[8,64]{1,0:T(8,128)S(1)}, bf16[512,32,256]{2,1,0:T(8,128)(2,1)}) custom-call(s32[24,128]{1,0:T(8,128)S(1)} %get-tuple-element.30.meta_ref, f32[514,8,128]{2,1,0:T(8,128)S(1)} %get-tuple-element.31.table_ref, ...), custom_call_target="tpu_custom_call", output_to_operand_aliasing={{2}: (5, {})} | custom-call | bytes 6291456 | tf_op jit(solution)/shard_map/pallas_call | solution.py:396
  75.7 0.1 collective-permute-start.16
  75.7 1.6 %collective-permute-start.15 = (f32[8,64]{1,0:T(8,128)S(1)}, f32[8,64]{1,0:T(8,128)S(1)}, u32[]{:S(2)}, u32[]{:S(2)}) collective-permute-start(f32[8,64]{1,0:T(8,128)S(1)} %get-tuple-element.49), channel_id=1, source_target_pairs={{0,2},{1,3},{2,0},{3,1},{4,6},{5,7},{6,4},{7,5},{8,10},{9,11},{10,... | collective-permute-start | bytes 6152 | tf_op jit(solution)/shard_map/ppermute | solution.py:23
  77.3 0.3 collective-permute-start.14
  77.6 1.7 %shard_map.95 = bf16[512,32,256]{2,1,0:T(8,128)(2,1)} custom-call(s32[24,128]{1,0:T(8,128)S(1)} %get-tuple-element.30.meta_ref, bf16[1,64,32,256]{3,2,1,0:T(8,128)(2,1)S(1)} %get-tuple-element.47.held_ref, bf16[512,32,256]{2,1,0:T(8,128)(2,1)} %get-tuple-element.48._), custom_call_target="tpu_custom_call", output_to_operand_aliasing={{}: (2, {})} | custom-call | bytes 4194304 | tf_op jit(solution)/shard_map/pallas_call | solution.py:418
  79.3 0.0 collective-permute-done.16
  79.3 0.1 collective-permute-done.15
  79.4 0.0 collective-permute-done.14
  79.4 0.7 sqrt.7
  (9 shorter events, 0.1 us)
Async XLA Ops:
  2.5 19.6 %collective-permute-start.2 = (bf16[133,8,128]{2,1,0:T(8,128)(2,1)}, bf16[133,8,128]{2,1,0:T(8,128)(2,1)S(1)}, u32[]{:S(2)}, u32[]{:S(2)}) collective-permute-start(bf16[133,8,128]{2,1,0:T(8,128)(2,1)} %shard_map.86.refs_0_), channel_id=1, source_target_pairs={{0,16},{4,20},{8,24},{12,28},{16,0},{20,4},{24,8},{28,12},{1,17},{... | collective-permute-start | bytes 817160 | tf_op jit(solution)/shard_map/density_4/ppermute | solution.py:23
  6.6 13.1 %collective-permute-start.1 = (bf16[133,8,128]{2,1,0:T(8,128)(2,1)}, bf16[133,8,128]{2,1,0:T(8,128)(2,1)S(1)}, u32[]{:S(2)}, u32[]{:S(2)}) collective-permute-start(bf16[133,8,128]{2,1,0:T(8,128)(2,1)} %shard_map.86.refs_0_), channel_id=1, source_target_pairs={{0,8},{4,12},{8,0},{12,4},{16,24},{20,28},{24,16},{28,20},{1,9},{5... | collective-permute-start | bytes 817160 | tf_op jit(solution)/shard_map/density_2/ppermute | solution.py:23
  8.1 7.9 %collective-permute-start = (bf16[133,8,128]{2,1,0:T(8,128)(2,1)}, bf16[133,8,128]{2,1,0:T(8,128)(2,1)S(1)}, u32[]{:S(2)}, u32[]{:S(2)}) collective-permute-start(bf16[133,8,128]{2,1,0:T(8,128)(2,1)} %shard_map.86.refs_0_), channel_id=1, source_target_pairs={{0,4},{4,0},{8,12},{12,8},{16,20},{20,16},{24,28},{28,24},{1,5},{5... | collective-permute-start | bytes 817160 | tf_op jit(solution)/shard_map/density_1/ppermute | solution.py:23
  16.1 12.0 %collective-permute-start.5 = (bf16[133,8,128]{2,1,0:T(8,128)(2,1)}, bf16[133,8,128]{2,1,0:T(8,128)(2,1)S(1)}, u32[]{:S(2)}, u32[]{:S(2)}) collective-permute-start(bf16[133,8,128]{2,1,0:T(8,128)(2,1)} %shard_map.86.refs_0_), channel_id=1, source_target_pairs={{0,24},{4,28},{8,16},{12,20},{16,8},{20,12},{24,0},{28,4},{1,25},{... | collective-permute-start | bytes 817160 | tf_op jit(solution)/shard_map/density_6/ppermute | solution.py:23
  19.7 6.9 %collective-permute-start.3 = (bf16[133,8,128]{2,1,0:T(8,128)(2,1)S(1)}, bf16[133,8,128]{2,1,0:T(8,128)(2,1)S(1)}, u32[]{:S(2)}, u32[]{:S(2)}) collective-permute-start(bf16[133,8,128]{2,1,0:T(8,128)(2,1)S(1)} %collective-permute-done.1.refs_2_), channel_id=1, source_target_pairs={{0,4},{4,0},{8,12},{12,8},{16,20},{20,16},{24,28},{28,24},{1,5},{5... | collective-permute-start | bytes 817160 | tf_op jit(solution)/shard_map/density_3/ppermute | solution.py:23
  26.5 8.4 %collective-permute-start.4 = (bf16[133,8,128]{2,1,0:T(8,128)(2,1)S(1)}, bf16[133,8,128]{2,1,0:T(8,128)(2,1)S(1)}, u32[]{:S(2)}, u32[]{:S(2)}) collective-permute-start(bf16[133,8,128]{2,1,0:T(8,128)(2,1)S(1)} %collective-permute-done.2.refs_4_.refs_0_), channel_id=1, source_target_pairs={{0,4},{4,0},{8,12},{12,8},{16,20},{20,16},{24,28},{28,24},{1,5},{5... | collective-permute-start | bytes 817160 | tf_op jit(solution)/shard_map/density_5/ppermute | solution.py:23
  28.1 9.8 %collective-permute-start.6 = (bf16[133,8,128]{2,1,0:T(8,128)(2,1)S(1)}, bf16[133,8,128]{2,1,0:T(8,128)(2,1)S(1)}, u32[]{:S(2)}, u32[]{:S(2)}) collective-permute-start(bf16[133,8,128]{2,1,0:T(8,128)(2,1)S(1)} %collective-permute-done.5.refs_6_.refs_1_), channel_id=1, source_target_pairs={{0,4},{4,0},{8,12},{12,8},{16,20},{20,16},{24,28},{28,24},{1,5},{5... | collective-permute-start | bytes 817160 | tf_op jit(solution)/shard_map/density_7/ppermute | solution.py:23
  29.0 2.2 %copy-start = (bf16[512,4096]{1,0:T(8,128)(2,1)S(1)}, bf16[512,4096]{1,0:T(8,128)(2,1)}, u32[]{:S(2)}) copy-start(bf16[512,4096]{1,0:T(8,128)(2,1)} %vir_ref.3) | copy-start | bytes 12582916
  31.2 1.0 %copy-start.2 = (bf16[133,8,128]{2,1,0:T(8,128)(2,1)S(1)}, bf16[133,8,128]{2,1,0:T(8,128)(2,1)}, u32[]{:S(2)}) copy-start(bf16[133,8,128]{2,1,0:T(8,128)(2,1)} %shard_map.86.refs_0_) | copy-start | bytes 817156
  32.1 2.8 %copy-start.1 = (bf16[512,4096]{1,0:T(8,128)(2,1)S(1)}, bf16[512,4096]{1,0:T(8,128)(2,1)}, u32[]{:S(2)}) copy-start(bf16[512,4096]{1,0:T(8,128)(2,1)} %vir_ref.3) | copy-start | bytes 12582916
  33.5 10.5 %copy-start.4 = (s32[8,64]{1,0:T(8,128)S(1)}, s32[8,64]{1,0:T(8,128)}, u32[]{:S(2)}) copy-start(s32[8,64]{1,0:T(8,128)} %param.10) | copy-start | bytes 6148
  33.5 19.8 %copy-start.3 = (bf16[133,8,128]{2,1,0:T(8,128)(2,1)S(1)}, bf16[133,8,128]{2,1,0:T(8,128)(2,1)}, u32[]{:S(2)}) copy-start(bf16[133,8,128]{2,1,0:T(8,128)(2,1)} %shard_map.86.refs_0_) | copy-start | bytes 817156
  38.6 13.3 %collective-permute-start.11 = (bf16[32,4096]{1,0:T(8,128)(2,1)S(1)}, bf16[32,4096]{1,0:T(8,128)(2,1)S(1)}, u32[]{:S(2)}, u32[]{:S(2)}) collective-permute-start(bf16[32,4096]{1,0:T(8,128)(2,1)S(1)} %shard_map.90.refs_0_), channel_id=1, source_target_pairs={{0,8},{4,12},{8,0},{12,4},{16,24},{20,28},{24,16},{28,20},{1,9},{5... | collective-permute-start | bytes 786440 | tf_op jit(solution)/shard_map/half_2/ppermute | solution.py:23
  42.1 6.9 %collective-permute-start.7 = (bf16[32,4096]{1,0:T(8,128)(2,1)S(1)}, bf16[32,4096]{1,0:T(8,128)(2,1)S(1)}, u32[]{:S(2)}, u32[]{:S(2)}) collective-permute-start(bf16[32,4096]{1,0:T(8,128)(2,1)S(1)} %shard_map.90.refs_0_), channel_id=1, source_target_pairs={{0,4},{4,0},{8,12},{12,8},{16,20},{20,16},{24,28},{28,24},{1,5},{5... | collective-permute-start | bytes 786440 | tf_op jit(solution)/shard_map/half_1/ppermute | solution.py:23
  44.2 20.4 %collective-permute-start.10 = (bf16[32,4096]{1,0:T(8,128)(2,1)S(1)}, bf16[32,4096]{1,0:T(8,128)(2,1)S(1)}, u32[]{:S(2)}, u32[]{:S(2)}) collective-permute-start(bf16[32,4096]{1,0:T(8,128)(2,1)S(1)} %shard_map.90.refs_0_), channel_id=1, source_target_pairs={{0,16},{4,20},{8,24},{12,28},{16,0},{20,4},{24,8},{28,12},{1,17},{... | collective-permute-start | bytes 786440 | tf_op jit(solution)/shard_map/half_4/ppermute | solution.py:23
  49.0 16.2 %collective-permute-start.8 = (bf16[32,4096]{1,0:T(8,128)(2,1)S(1)}, bf16[32,4096]{1,0:T(8,128)(2,1)S(1)}, u32[]{:S(2)}, u32[]{:S(2)}) collective-permute-start(bf16[32,4096]{1,0:T(8,128)(2,1)S(1)} %shard_map.90.refs_0_), channel_id=1, source_target_pairs={{0,24},{4,28},{8,16},{12,20},{16,8},{20,12},{24,0},{28,4},{1,25},{... | collective-permute-start | bytes 786440 | tf_op jit(solution)/shard_map/half_6/ppermute | solution.py:23
  51.9 12.7 %collective-permute-start.12 = (bf16[32,4096]{1,0:T(8,128)(2,1)S(1)}, bf16[32,4096]{1,0:T(8,128)(2,1)S(1)}, u32[]{:S(2)}, u32[]{:S(2)}) collective-permute-start(bf16[32,4096]{1,0:T(8,128)(2,1)S(1)} %collective-permute-done.11.refs_2_), channel_id=1, source_target_pairs={{0,4},{4,0},{8,12},{12,8},{16,20},{20,16},{24,28},{28,24},{1,5},{5... | collective-permute-start | bytes 786440 | tf_op jit(solution)/shard_map/half_3/ppermute | solution.py:23
  64.6 6.4 %collective-permute-start.13 = (bf16[32,4096]{1,0:T(8,128)(2,1)S(1)}, bf16[32,4096]{1,0:T(8,128)(2,1)S(1)}, u32[]{:S(2)}, u32[]{:S(2)}) collective-permute-start(bf16[32,4096]{1,0:T(8,128)(2,1)S(1)} %collective-permute-done.10.refs_1_), channel_id=1, source_target_pairs={{0,4},{4,0},{8,12},{12,8},{16,20},{20,16},{24,28},{28,24},{1,5},{5... | collective-permute-start | bytes 786440 | tf_op jit(solution)/shard_map/half_5/ppermute | solution.py:23
  65.3 8.5 %collective-permute-start.9 = (bf16[32,4096]{1,0:T(8,128)(2,1)S(1)}, bf16[32,4096]{1,0:T(8,128)(2,1)S(1)}, u32[]{:S(2)}, u32[]{:S(2)}) collective-permute-start(bf16[32,4096]{1,0:T(8,128)(2,1)S(1)} %collective-permute-done.8.refs_2_), channel_id=1, source_target_pairs={{0,4},{4,0},{8,12},{12,8},{16,20},{20,16},{24,28},{28,24},{1,5},{5... | collective-permute-start | bytes 786440 | tf_op jit(solution)/shard_map/half_7/ppermute | solution.py:23
  75.7 3.7 %collective-permute-start.16 = (f32[8,64]{1,0:T(8,128)S(1)}, f32[8,64]{1,0:T(8,128)S(1)}, u32[]{:S(2)}, u32[]{:S(2)}) collective-permute-start(f32[8,64]{1,0:T(8,128)S(1)} %get-tuple-element.49), channel_id=1, source_target_pairs={{0,3},{1,2},{2,1},{3,0},{4,7},{5,6},{6,5},{7,4},{8,11},{9,10},{10,... | collective-permute-start | bytes 6152 | tf_op jit(solution)/shard_map/ppermute | solution.py:23
  75.7 3.7 %collective-permute-start.15 = (f32[8,64]{1,0:T(8,128)S(1)}, f32[8,64]{1,0:T(8,128)S(1)}, u32[]{:S(2)}, u32[]{:S(2)}) collective-permute-start(f32[8,64]{1,0:T(8,128)S(1)} %get-tuple-element.49), channel_id=1, source_target_pairs={{0,2},{1,3},{2,0},{3,1},{4,6},{5,7},{6,4},{7,5},{8,10},{9,11},{10,... | collective-permute-start | bytes 6152 | tf_op jit(solution)/shard_map/ppermute | solution.py:23
  77.3 2.1 %collective-permute-start.14 = (f32[8,64]{1,0:T(8,128)S(1)}, f32[8,64]{1,0:T(8,128)S(1)}, u32[]{:S(2)}, u32[]{:S(2)}) collective-permute-start(f32[8,64]{1,0:T(8,128)S(1)} %get-tuple-element.49), channel_id=1, source_target_pairs={{0,1},{1,0},{2,3},{3,2},{4,5},{5,4},{6,7},{7,6},{8,9},{9,8},{10,11... | collective-permute-start | bytes 6152 | tf_op jit(solution)/shard_map/ppermute | solution.py:23
